TPU v7x, 128 devices: a whole 4x4x4 slice. The times are simulated.
128 devices in a mesh: dp: 8 (over z, core), ctx: 16 (over y, x).
Axes of the slice: x: 4, y: 4, z: 4, core: 2. Of those that a mesh axis runs over, the one named last changes fastest.
Arguments:
- hidden_in: bfloat16 [2, 8, 1024, 896], P(None, 'dp', 'ctx'), may hold values from -6 to 6
- positions: int32 [2, 8, 1024], P(None, 'dp', 'ctx'), may hold values from 0 to 1023, as said below
- norm_attn: bfloat16 [896], P(('dp', 'ctx')), may hold values from 0.099609375 to 1.8984375
- w_query: bfloat16 [896, 896], P(('dp', 'ctx')), may hold values from -0.1875 to 0.1875
- b_query: bfloat16 [896], P(('dp', 'ctx')), may hold values from -3 to 3
- w_key: bfloat16 [896, 128], P(('dp', 'ctx')), may hold values from -0.1875 to 0.1875
- b_key: bfloat16 [128], P(('dp', 'ctx')), may hold values from -3 to 3
- value_weight: bfloat16 [896, 128], P(('dp', 'ctx')), may hold values from -0.1875 to 0.1875
- value_bias: bfloat16 [128], P(('dp', 'ctx')), may hold values from -3 to 3
- w_output: bfloat16 [896, 896], P(('dp', 'ctx')), may hold values from -0.375 to 0.375
- norm_mlp: bfloat16 [896], P(('dp', 'ctx')), may hold values from 0.099609375 to 1.8984375
- w_gate: bfloat16 [896, 4864], P(('dp', 'ctx')), may hold values from -0.1875 to 0.1875
- w_up: bfloat16 [896, 4864], P(('dp', 'ctx')), may hold values from -0.1875 to 0.1875
- w_down: bfloat16 [4864, 896], P(('dp', 'ctx')), may hold values from -0.078125 to 0.078125
- cotangent: bfloat16 [2, 8, 1024, 896], P(None, 'dp', 'ctx'), may hold values from -6 to 6
Outputs:
- layer_out: bfloat16 [2, 8, 1024, 896], P(None, 'dp', 'ctx')
- grad_in: float32 [2, 8, 1024, 896], P(None, 'dp', 'ctx')
- grad_norm_attn: float32 [896], P(('dp', 'ctx'))
- grad_w_query: float32 [896, 896], P(('dp', 'ctx'))
- grad_b_query: float32 [896], P(('dp', 'ctx'))
- grad_w_key: float32 [896, 128], P(('dp', 'ctx'))
- grad_b_key: float32 [128], replicated
- grad_w_value: float32 [896, 128], P(('dp', 'ctx'))
- grad_b_value: float32 [128], P(('dp', 'ctx'))
- grad_w_output: float32 [896, 896], P(('dp', 'ctx'))
- grad_norm_mlp: float32 [896], P(('dp', 'ctx'))
- grad_w_gate: float32 [896, 4864], P(('dp', 'ctx'))
- grad_w_up: float32 [896, 4864], P(('dp', 'ctx'))
- grad_w_down: float32 [4864, 896], P(('dp', 'ctx'))
Inputs may be any that keep to these rules, and one draw needn't show every extreme that they name: Each sequence's stored rows hold every position 0 to 1023 once. The 64 rows of a sequence on one index of ctx are two runs of 32 consecutive positions: first one starting at p * 32, then one starting at (31 - p) * 32, with p differing between the indices of ctx.
All inputs are finite; a program needn't handle non-finite values.
Results may differ from a plain program's by a relative error of at most 0.024.
Values may be sent and summed in bfloat16 or wider, within the bound.
A program may use at most 192 MiB of HBM per device.

v0:
```python
import jax
import jax.numpy as jnp
from jax import lax
from jax.sharding import PartitionSpec as P

QUERY_HEADS = 14
KEY_VALUE_HEADS = 2
HEAD_SIZE = 64
MB = 2


EPSILON = 1e-06
THETA_BASE = 1000000.0


def matrix_product(left, right):
    return jnp.dot(left, right, preferred_element_type=jnp.float32)


def matmul_tn(left, right):
    return lax.dot_general(
        left, right, (((0,), (0,)), ((), ())), preferred_element_type=jnp.float32
    )


def matmul_nt(left, right):
    return lax.dot_general(
        left, right, (((1,), (1,)), ((), ())), preferred_element_type=jnp.float32
    )


def rms_scale(values):
    return lax.rsqrt(jnp.mean(values * values, axis=-1, keepdims=True) + EPSILON)


def rope_tables(places, head_dim):
    freqs = THETA_BASE ** (-jnp.arange(0, head_dim, 2).astype(jnp.float32) / head_dim)
    angles = places.astype(jnp.float32)[:, None] * freqs[None, :]
    angles = jnp.concatenate([angles, angles], axis=-1)
    return (jnp.cos(angles), jnp.sin(angles))


def apply_rotary(values, cosine_table, sine_table):
    half_dim = values.shape[-1] // 2
    turned = jnp.concatenate([-values[..., half_dim:], values[..., :half_dim]], axis=-1)
    return values * cosine_table[:, None, :] + turned * sine_table[:, None, :]


def inverse_rotary(grads, cosine_table, sine_table):
    half_dim = grads.shape[-1] // 2
    direct = grads * cosine_table[:, None, :]
    turned = grads * sine_table[:, None, :]
    return direct + jnp.concatenate([turned[..., half_dim:], -turned[..., :half_dim]], axis=-1)


def masked_scores(rotated_queries, key_all, query_places, key_places, factor):
    scores = (
        jnp.einsum("qghd,kgd->ghqk", rotated_queries, key_all, preferred_element_type=jnp.float32)
        * factor
    )
    allowed = key_places[None, :] <= query_places[:, None]
    return jnp.where(allowed[None, None], scores, -1e30)


def attend(rotated_queries, key_all, value_all, query_places, key_places, factor):
    scores = masked_scores(rotated_queries, key_all, query_places, key_places, factor)
    top_score = jnp.max(scores, axis=-1, keepdims=True)
    expo = jnp.exp(scores - top_score)
    total = jnp.sum(expo, axis=-1, keepdims=True)
    probs_low = (expo / total).astype(jnp.bfloat16)
    attended = jnp.einsum(
        "ghqk,kgd->qghd", probs_low, value_all, preferred_element_type=jnp.float32
    )
    return (attended, top_score + jnp.log(total))


def attend_back(
    rotated_queries, key_all, value_all, query_places, key_places, factor, logsum, attended_gradient
):
    scores = masked_scores(rotated_queries, key_all, query_places, key_places, factor)
    probs = jnp.exp(scores - logsum)
    grad_probs = jnp.einsum(
        "qghd,kgd->ghqk", attended_gradient, value_all, preferred_element_type=jnp.float32
    )
    inner = jnp.sum(probs * grad_probs, axis=-1, keepdims=True)
    grad_scores = (probs * (grad_probs - inner)).astype(jnp.bfloat16)
    probs_low = probs.astype(jnp.bfloat16)
    grad_query = (
        jnp.einsum("ghqk,kgd->qghd", grad_scores, key_all, preferred_element_type=jnp.float32)
        * factor
    )
    grad_key = (
        jnp.einsum(
            "ghqk,qghd->kgd", grad_scores, rotated_queries, preferred_element_type=jnp.float32
        )
        * factor
    )
    grad_value = jnp.einsum(
        "ghqk,qghd->kgd", probs_low, attended_gradient, preferred_element_type=jnp.float32
    )
    return (grad_query, grad_key, grad_value)


def accumulate(totals, fresh):
    if totals is None:
        return fresh
    return tuple((earlier + later for earlier, later in zip(totals, fresh)))


def spread_key_bias(totals, copies):
    return totals[:4] + (jnp.tile(totals[4], copies),) + totals[5:]


def body(
    hidden_in,
    positions,
    norm_attn,
    w_query,
    b_query,
    w_key,
    b_key,
    value_weight,
    value_bias,
    w_output,
    norm_mlp,
    w_gate,
    w_up,
    w_down,
    cotangent,
):
    factor = HEAD_SIZE ** (-0.5)
    query_group_count = QUERY_HEADS // KEY_VALUE_HEADS
    device_count = lax.axis_size(("dp", "ctx"))
    attn_totals = None
    ffn_totals = None
    outputs = []
    input_grads = []
    for micro_batch in range(MB):
        residual = hidden_in[micro_batch, 0].astype(jnp.float32)
        query_places = positions[micro_batch, 0]
        count_of_rows = residual.shape[0]
        attn_weights = (
            lax.all_gather(norm_attn, ("dp", "ctx"), axis=0, tiled=True),
            lax.all_gather(w_query, ("dp", "ctx"), axis=0, tiled=True),
            lax.all_gather(b_query, ("dp", "ctx"), axis=0, tiled=True),
            lax.all_gather(w_key, ("dp", "ctx"), axis=0, tiled=True),
            lax.all_gather(b_key, ("dp", "ctx"), axis=0, tiled=True),
            lax.all_gather(value_weight, ("dp", "ctx"), axis=0, tiled=True),
            lax.all_gather(value_bias, ("dp", "ctx"), axis=0, tiled=True),
            lax.all_gather(w_output, ("dp", "ctx"), axis=0, tiled=True),
        )
        (
            gain_attn,
            query_full,
            bias_query,
            key_full,
            bias_key,
            value_full,
            bias_value,
            output_full,
        ) = attn_weights
        inv_rms = rms_scale(residual)
        unit_in = residual * inv_rms
        normalized_input = (unit_in * gain_attn.astype(jnp.float32)).astype(jnp.bfloat16)
        cosine_table, sine_table = rope_tables(query_places, HEAD_SIZE)
        query_lin = matrix_product(normalized_input, query_full) + bias_query.astype(jnp.float32)
        key_linear = matrix_product(normalized_input, key_full) + bias_key.astype(jnp.float32)
        value_linear = matrix_product(normalized_input, value_full) + bias_value.astype(jnp.float32)
        rotated_queries = apply_rotary(
            query_lin.reshape(count_of_rows, QUERY_HEADS, HEAD_SIZE), cosine_table, sine_table
        ).astype(jnp.bfloat16)
        rotated_queries = rotated_queries.reshape(
            count_of_rows, KEY_VALUE_HEADS, query_group_count, HEAD_SIZE
        )
        rotated_keys = apply_rotary(
            key_linear.reshape(count_of_rows, KEY_VALUE_HEADS, HEAD_SIZE), cosine_table, sine_table
        ).astype(jnp.bfloat16)
        narrow_values = value_linear.astype(jnp.bfloat16).reshape(
            count_of_rows, KEY_VALUE_HEADS, HEAD_SIZE
        )
        key_all, value_all, key_places = (
            lax.all_gather(rotated_keys, "ctx", axis=0, tiled=True),
            lax.all_gather(narrow_values, "ctx", axis=0, tiled=True),
            lax.all_gather(query_places, "ctx", axis=0, tiled=True),
        )
        attended, logsum = attend(
            rotated_queries, key_all, value_all, query_places, key_places, factor
        )
        attended_low = attended.reshape(count_of_rows, QUERY_HEADS * HEAD_SIZE).astype(jnp.bfloat16)
        mixed = residual + matrix_product(attended_low, output_full)
        ffn_weights = (
            lax.all_gather(norm_mlp, ("dp", "ctx"), axis=0, tiled=True),
            lax.all_gather(w_gate, ("dp", "ctx"), axis=0, tiled=True),
            lax.all_gather(w_up, ("dp", "ctx"), axis=0, tiled=True),
            lax.all_gather(w_down, ("dp", "ctx"), axis=0, tiled=True),
        )
        gain_mlp, gate_full, up_full, down_full = ffn_weights
        inv_mid = rms_scale(mixed)
        unit_mid = mixed * inv_mid
        normed_mid = (unit_mid * gain_mlp.astype(jnp.float32)).astype(jnp.bfloat16)
        gate_lin = matrix_product(normed_mid, gate_full)
        up_lin = matrix_product(normed_mid, up_full)
        sigmoid_gate = jax.nn.sigmoid(gate_lin)
        hidden_low = (gate_lin * sigmoid_gate * up_lin).astype(jnp.bfloat16)
        outputs.append((mixed + matrix_product(hidden_low, down_full)).astype(jnp.bfloat16))
        ffn_back = (
            lax.all_gather(norm_mlp, ("dp", "ctx"), axis=0, tiled=True),
            lax.all_gather(w_gate, ("dp", "ctx"), axis=0, tiled=True),
            lax.all_gather(w_up, ("dp", "ctx"), axis=0, tiled=True),
            lax.all_gather(w_down, ("dp", "ctx"), axis=0, tiled=True),
        )
        gain_mlp_back, gate_back, up_back, down_back = ffn_back
        gain_mid = gain_mlp_back.astype(jnp.float32)
        grad_top = cotangent[micro_batch, 0].astype(jnp.float32)
        grad_branch = grad_top.astype(jnp.bfloat16)
        grad_down_w = matmul_tn(hidden_low, grad_branch)
        hidden_back = matmul_nt(grad_branch, down_back).astype(jnp.bfloat16).astype(jnp.float32)
        grad_gate = (
            hidden_back * up_lin * sigmoid_gate * (1.0 + gate_lin * (1.0 - sigmoid_gate))
        ).astype(jnp.bfloat16)
        grad_upward = (hidden_back * gate_lin * sigmoid_gate).astype(jnp.bfloat16)
        grad_gate_w = matmul_tn(normed_mid, grad_gate)
        grad_up_w = matmul_tn(normed_mid, grad_upward)
        grad_normed_mid = matmul_nt(grad_gate, gate_back) + matmul_nt(grad_upward, up_back)
        grad_gain_mid = jnp.sum(grad_normed_mid * unit_mid, axis=0)
        scaled_mid = grad_normed_mid * gain_mid
        grad_mixed = grad_top + inv_mid * (
            scaled_mid - unit_mid * jnp.mean(scaled_mid * unit_mid, axis=-1, keepdims=True)
        )
        ffn_totals = accumulate(ffn_totals, (grad_gain_mid, grad_gate_w, grad_up_w, grad_down_w))
        gain_attn_back, query_back, key_back, value_back, output_back = (
            lax.all_gather(norm_attn, ("dp", "ctx"), axis=0, tiled=True),
            lax.all_gather(w_query, ("dp", "ctx"), axis=0, tiled=True),
            lax.all_gather(w_key, ("dp", "ctx"), axis=0, tiled=True),
            lax.all_gather(value_weight, ("dp", "ctx"), axis=0, tiled=True),
            lax.all_gather(w_output, ("dp", "ctx"), axis=0, tiled=True),
        )
        gain_in = gain_attn_back.astype(jnp.float32)
        grad_attn_branch = grad_mixed.astype(jnp.bfloat16)
        grad_output_w = matmul_tn(attended_low, grad_attn_branch)
        attended_gradient = matmul_nt(grad_attn_branch, output_back).astype(jnp.bfloat16)
        attended_gradient = attended_gradient.reshape(
            count_of_rows, KEY_VALUE_HEADS, query_group_count, HEAD_SIZE
        )
        grad_query_rot, full_key_gradient, full_value_gradient = attend_back(
            rotated_queries,
            key_all,
            value_all,
            query_places,
            key_places,
            factor,
            logsum,
            attended_gradient,
        )
        rotated_key_gradient, grad_value_sum = (
            lax.psum_scatter(
                full_key_gradient.reshape(-1, KEY_VALUE_HEADS * HEAD_SIZE),
                "ctx",
                scatter_dimension=0,
                tiled=True,
            ),
            lax.psum_scatter(
                full_value_gradient.reshape(-1, KEY_VALUE_HEADS * HEAD_SIZE),
                "ctx",
                scatter_dimension=0,
                tiled=True,
            ),
        )
        grad_query_low = inverse_rotary(
            grad_query_rot.reshape(count_of_rows, QUERY_HEADS, HEAD_SIZE), cosine_table, sine_table
        )
        grad_query_low = grad_query_low.reshape(count_of_rows, QUERY_HEADS * HEAD_SIZE).astype(
            jnp.bfloat16
        )
        narrow_key_gradient = inverse_rotary(
            rotated_key_gradient.reshape(count_of_rows, KEY_VALUE_HEADS, HEAD_SIZE),
            cosine_table,
            sine_table,
        )
        narrow_key_gradient = narrow_key_gradient.reshape(
            count_of_rows, KEY_VALUE_HEADS * HEAD_SIZE
        ).astype(jnp.bfloat16)
        grad_value_low = grad_value_sum.astype(jnp.bfloat16)
        grad_query_w = matmul_tn(normalized_input, grad_query_low)
        grad_key_w = matmul_tn(normalized_input, narrow_key_gradient)
        grad_value_w = matmul_tn(normalized_input, grad_value_low)
        grad_query_b = jnp.sum(grad_query_low.astype(jnp.float32), axis=0)
        grad_key_b = jnp.sum(narrow_key_gradient.astype(jnp.float32), axis=0)
        grad_value_b = jnp.sum(grad_value_low.astype(jnp.float32), axis=0)
        grad_normed_in = (
            matmul_nt(grad_query_low, query_back)
            + matmul_nt(narrow_key_gradient, key_back)
            + matmul_nt(grad_value_low, value_back)
        )
        grad_gain_in = jnp.sum(grad_normed_in * unit_in, axis=0)
        scaled_in = grad_normed_in * gain_in
        input_grads.append(
            grad_mixed
            + inv_rms
            * (scaled_in - unit_in * jnp.mean(scaled_in * unit_in, axis=-1, keepdims=True))
        )
        attn_totals = accumulate(
            attn_totals,
            (
                grad_gain_in,
                grad_query_w,
                grad_query_b,
                grad_key_w,
                grad_key_b,
                grad_value_w,
                grad_value_b,
                grad_output_w,
            ),
        )
    attn_totals = spread_key_bias(attn_totals, device_count)
    shards = tuple(
        lax.psum_scatter(attn_totals + ffn_totals, ("dp", "ctx"), scatter_dimension=0, tiled=True)
    )
    layer_out = jnp.stack(outputs)[:, None]
    grad_in = jnp.stack(input_grads)[:, None]
    return (layer_out, grad_in) + shards


def solution(mesh):
    in_specs = (
        P(None, "dp", "ctx", None),
        P(None, "dp", "ctx"),
        P(("dp", "ctx")),
        P(("dp", "ctx"), None),
        P(("dp", "ctx")),
        P(("dp", "ctx"), None),
        P(("dp", "ctx")),
        P(("dp", "ctx"), None),
        P(("dp", "ctx")),
        P(("dp", "ctx"), None),
        P(("dp", "ctx")),
        P(("dp", "ctx"), None),
        P(("dp", "ctx"), None),
        P(("dp", "ctx"), None),
        P(None, "dp", "ctx", None),
    )
    out_specs = (
        P(None, "dp", "ctx", None),
        P(None, "dp", "ctx", None),
        P(("dp", "ctx")),
        P(("dp", "ctx"), None),
        P(("dp", "ctx")),
        P(("dp", "ctx"), None),
        P(),
        P(("dp", "ctx"), None),
        P(("dp", "ctx")),
        P(("dp", "ctx"), None),
        P(("dp", "ctx")),
        P(("dp", "ctx"), None),
        P(("dp", "ctx"), None),
        P(("dp", "ctx"), None),
    )
    return jax.shard_map(body, mesh=mesh, in_specs=in_specs, out_specs=out_specs, check_vma=False)
```

profile of v0, /device:TPU:1, one launch (start us, length us, event | category | flops | bytes accessed | tf_op | source)
XLA Modules:
  0.0 1923.0 jit_solution(14354433653152831716)
XLA Ops:
  15.9 69.1 %all-reduce.25 = (bf16[896]{0:T(1024)(128)(2,1)S(1)}, bf16[896]{0:T(1024)(128)(2,1)S(1)}, bf16[128]{0:T(256)(128)(2,1)S(1)}, bf16[128]{0:T(256)(128)(2,1)S(1)}, bf16[896]{0:T(1024)(128)(2,1)S(1)}) all-reduce(bf16[896]{0:T(1024)(128)(2,1)S(1)} %dynamic-update-slice.4, ...), channel_id=1, replica_groups=mesh['dp'=8,'ctx'=16] {'dp','ctx'}, use_global_device_ids=true, to_apply=%add.4 | all-reduce | flops 2944 | bytes 11776
  91.9 58.0 %all-gather.3 = bf16[128,7,128]{2,1,0:T(8,128)(2,1)S(1)} all-gather(bf16[1,7,128]{2,1,0:T(8,128)(2,1)} %bitcast.385), channel_id=1, replica_groups=mesh['dp'=8,'ctx'=16] {'dp','ctx'}, dimensions={0}, use_global_device_ids=true | all-gather | bytes 231168 | tf_op jit(solution)/shard_map/all_gather | solution.py:146
  153.7 60.5 %all-gather.2 = bf16[128,7,128]{2,1,0:T(8,128)(2,1)S(1)} all-gather(bf16[1,7,128]{2,1,0:T(8,128)(2,1)S(1)} %bitcast.386), channel_id=1, replica_groups=mesh['dp'=8,'ctx'=16] {'dp','ctx'}, dimensions={0}, use_global_device_ids=true | all-gather | bytes 231168 | tf_op jit(solution)/shard_map/all_gather | solution.py:148
  215.8 11.0 all-reduce.22
  227.1 17.9 all_gather.101
  245.1 19.6 %all_gather.43 = bf16[1024,2,64]{2,0,1:T(8,128)(2,1)S(1)} all-gather(bf16[64,2,64]{2,0,1:T(8,128)(2,1)S(1)} %fusion.106), channel_id=1, replica_groups=mesh['dp'=8,'ctx'=16] {'ctx'}, dimensions={0}, use_global_device_ids=true | all-gather | bytes 278528 | tf_op jit(solution)/shard_map/all_gather | solution.py:182
  264.7 21.1 %all_gather.99 = bf16[1024,2,64]{2,1,0:T(2,128)(2,1)} all-gather(bf16[64,2,64]{2,1,0:T(2,128)(2,1)S(1)} %reshape.449), channel_id=1, replica_groups=mesh['dp'=8,'ctx'=16] {'ctx'}, dimensions={0}, use_global_device_ids=true | all-gather | bytes 278528 | tf_op jit(solution)/shard_map/all_gather | solution.py:183
  285.8 20.2 %all_gather.39 = bf16[1024,2,64]{2,1,0:T(2,128)(2,1)} all-gather(bf16[64,2,64]{2,1,0:T(2,128)(2,1)S(1)} %reshape.445), channel_id=1, replica_groups=mesh['dp'=8,'ctx'=16] {'ctx'}, dimensions={0}, use_global_device_ids=true | all-gather | bytes 278528 | tf_op jit(solution)/shard_map/all_gather | solution.py:183
  342.1 13.9 reshape.494
  356.0 13.6 reshape.496
  369.6 6.0 fusion.150
  378.0 13.4 reshape.498
  391.4 7.0 multiply_convert_fusion.2
  398.5 6.7 fusion.153
  405.2 6.9 multiply_reduce_fusion.1
  412.1 4.9 fusion.152
  426.2 6.8 multiply_reduce_fusion
  453.7 8.5 fusion.158
  464.7 14.7 convolution_add_fusion.1
  479.4 8.5 convolution_add_fusion.2
  488.0 465.0 %fusion.140 = (f32[8,4864]{1,0:T(8,128)}, f32[8,4864]{1,0:T(8,128)}) fusion(f32[896,4864]{1,0:T(8,128)} %convolution_add_fusion.2, f32[896,4864]{1,0:T(8,128)} %convolution_add_fusion.1), kind=kCustom, calls=%all-reduce-scatter.3 | all-reduce-scatter fusion | flops 9961473 | bytes 35176448
  969.6 5.8 fusion.30
  994.0 7.4 fusion.94
  1001.5 11.1 convolution_add_fusion
  1012.6 374.3 %fusion.2 = f32[48,896]{1,0:T(8,128)S(1)} fusion(f32[4864,896]{1,0:T(8,128)} %convolution_add_fusion), kind=kCustom, calls=%all-reduce-scatter.2 | all-reduce-scatter fusion | flops 5505025 | bytes 17604608
  1394.1 5.8 fusion.29
  1406.8 16.9 collective-permute-start.12
  1426.8 6.8 collective-permute-start.10
  1446.0 14.6 collective-permute-start.4
  1463.7 16.6 collective-permute-start.2
  1484.8 5.5 collective-permute-start.30
  1491.8 24.4 %reduce-scatter.21.cloned.1.call-done = f32[64,128]{1,0:T(8,128)} async-done(((f32[1024,128]{1,0:T(8,128)}), f32[64,128]{1,0:T(8,128)}) %reduce-scatter.21.cloned.1.call-update) | async-done | bytes 32784
  1517.1 4.9 collective-permute-start.29
  1522.0 5.7 collective-permute-start.28
  1529.6 7.3 collective-permute-start.26
  1545.8 5.0 collective-permute-start.22
  1550.8 6.1 collective-permute-start.21
  1564.0 4.9 collective-permute-start.18
  1573.4 5.7 collective-permute-start.57
  1583.5 6.5 collective-permute-start.55
  1611.6 4.7 collective-permute-start.48
  1622.4 5.9 collective-permute-start.46
  1643.9 52.3 %concatenate.102 = f32[135,4864]{1,0:T(8,128)} concatenate(f32[7,4864]{1,0:T(8,128)} %collective-permute-done.15, f32[8,4864]{1,0:T(8,128)} %collective-permute-done.14, f32[8,4864]{1,0:T(8,128)} %collective-permute-done.13, f32[8,4864]{1,0:T(8,128)} %copy-done.98, f32[8,4864]{1,0:T(8,128)} %copy-done.99, f32[8,4864]{1,0:T(8,128)} %copy-done.100, f32[8,4864]{1,0:T(8,128)} %copy-done.101, ...), dimensions={0} | concatenate | bytes 5253120
  1713.9 52.2 %concatenate.103 = f32[135,4864]{1,0:T(8,128)} concatenate(f32[7,4864]{1,0:T(8,128)} %collective-permute-done.31, f32[8,4864]{1,0:T(8,128)} %collective-permute-done.30, f32[8,4864]{1,0:T(8,128)} %copy-done.107, f32[8,4864]{1,0:T(8,128)} %copy-done.108, f32[8,4864]{1,0:T(8,128)} %copy-done.109, f32[8,4864]{1,0:T(8,128)} %copy-done.110, f32[8,4864]{1,0:T(8,128)} %copy-done.111, ...), dimensions={0} | concatenate | bytes 5253120
  1771.3 5.6 collective-permute-start.34
  1783.3 6.0 collective-permute-done.35
  1794.6 44.4 %concatenate.104 = f32[1318,896]{1,0:T(8,128)} concatenate(f32[22,896]{1,0:T(8,128)} %collective-permute-done.58, f32[48,896]{1,0:T(8,128)S(1)} %copy-done.79, f32[48,896]{1,0:T(8,128)} %collective-permute-done.56, f32[48,896]{1,0:T(8,128)} %collective-permute-done.55, f32[48,896]{1,0:T(8,128)} %collective-permute-done.54, f32[48,896]{1,0:T(8,128)} %collective-permute-done.53, ...), dimensions={0} | concatenate | bytes 9447424
  1842.0 63.9 %all-reduce.23 = (f32[896]{0:T(1024)S(1)}, f32[896]{0:T(1024)S(1)}, f32[128]{0:T(128)S(1)}, f32[896]{0:T(1024)S(1)}) all-reduce(f32[896]{0:T(1024)S(1)} %add.316, f32[896]{0:T(1024)S(1)} %add.323, f32[128]{0:T(128)S(1)} %add.327, f32[896]{0:T(1024)S(1)} %add.329), channel_id=8, replica_groups=mesh['dp'=8,'ctx'=16] {'dp','ctx'}, use_global_device_ids=true, to_apply=%region_20.21.clone | all-reduce | flops 2816 | bytes 22528
  (612 shorter events, 280.4 us)
Async XLA Ops:
  7.2 300.3 %all-gather.15.cloned.1.call-start = ((), (), s32[]{:S(2)}) async-start(), calls=%async_computation.6 | async-start | bytes 1849344 | tf_op jit(solution)/shard_map/all_gather | solution.py:144
  7.9 323.2 %all-gather.17.cloned.1.call-start = ((), (), s32[]{:S(2)}) async-start(), calls=%async_computation.7 | async-start | bytes 1849344 | tf_op jit(solution)/shard_map/all_gather | solution.py:150
  8.7 333.4 %all-gather.19.cloned.1.call-start = ((), (), s32[]{:S(2)}) async-start(), calls=%async_computation.8 | async-start | bytes 10039296 | tf_op jit(solution)/shard_map/all_gather | solution.py:193
  9.4 346.6 %all-gather.21.cloned.1.call-start = ((), (), s32[]{:S(2)}) async-start(), calls=%async_computation.9 | async-start | bytes 10039296 | tf_op jit(solution)/shard_map/all_gather | solution.py:194
  10.0 368.0 %all-gather.23.cloned.1.call-start = ((), (), s32[]{:S(2)}) async-start(), calls=%async_computation.10 | async-start | bytes 9246720 | tf_op jit(solution)/shard_map/all_gather | solution.py:195
  10.6 1393.7 %reduce-scatter.17.cloned.1.call-start = ((), (), s32[]{:S(2)}) async-start(), calls=%async_computation.5 | async-start | bytes 557056 | tf_op jit(solution)/shard_map/reduce_scatter | solution.py:256
  954.5 479.1 %collective-permute-start.14 = (f32[8,4864]{1,0:T(8,128)}, f32[8,4864]{1,0:T(8,128)}, u32[]{:S(2)}, u32[]{:S(2)}) collective-permute-start(f32[8,4864]{1,0:T(8,128)} %get-tuple-element.114), channel_id=1, source_target_pairs={{0,15},{1,16},{2,17},{3,18},{4,19},{5,20},{6,21},{7,22},{8,23},{9,... | collective-permute-start | bytes 466952
  956.8 479.5 %collective-permute-start.13 = (f32[8,4864]{1,0:T(8,128)}, f32[8,4864]{1,0:T(8,128)}, u32[]{:S(2)}, u32[]{:S(2)}) collective-permute-start(f32[8,4864]{1,0:T(8,128)} %get-tuple-element.114), channel_id=1, source_target_pairs={{0,14},{1,15},{2,16},{3,17},{4,18},{5,19},{6,20},{7,21},{8,22},{9,... | collective-permute-start | bytes 466952
  959.8 445.4 %reduce-scatter.15.cloned.1.call-start = ((), (), s32[]{:S(2)}) async-start(), calls=%async_computation.4 | async-start | bytes 557056 | tf_op jit(solution)/shard_map/reduce_scatter | solution.py:256
  975.5 515.5 %reduce-scatter.19.cloned.1.call-start = ((), (), s32[]{:S(2)}) async-start(), calls=%async_computation.11 | async-start | bytes 557056
  985.3 438.4 %collective-permute-start.31 = (f32[7,4864]{1,0:T(8,128)}, f32[7,4864]{1,0:T(8,128)}, u32[]{:S(2)}, u32[]{:S(2)}) collective-permute-start(f32[7,4864]{1,0:T(8,128)} %slice.105), channel_id=1, source_target_pairs={{0,16},{1,17},{2,18},{3,19},{4,20},{5,21},{6,22},{7,23},{8,24},{9,... | collective-permute-start | bytes 408584
  988.8 438.0 %collective-permute-start.15 = (f32[7,4864]{1,0:T(8,128)}, f32[7,4864]{1,0:T(8,128)}, u32[]{:S(2)}, u32[]{:S(2)}) collective-permute-start(f32[7,4864]{1,0:T(8,128)} %slice.104), channel_id=1, source_target_pairs={{0,16},{1,17},{2,18},{3,19},{4,20},{5,21},{6,22},{7,23},{8,24},{9,... | collective-permute-start | bytes 408584
  1001.5 514.7 %reduce-scatter.21.cloned.1.call-start = ((), (), s32[]{:S(2)}) async-start(), calls=%async_computation.12 | async-start | bytes 557056
  1399.8 509.4 %all-reduce.29.cloned.1.call-start = ((), (), s32[]{:S(2)}) async-start(), calls=%async_computation.13 | async-start | bytes 14811136
  1406.8 32.2 %collective-permute-start.12 = (f32[8,4864]{1,0:T(8,128)}, f32[8,4864]{1,0:T(8,128)S(1)}, u32[]{:S(2)}, u32[]{:S(2)}) collective-permute-start(f32[8,4864]{1,0:T(8,128)} %get-tuple-element.114), channel_id=1, source_target_pairs={{0,13},{1,14},{2,15},{3,16},{4,17},{5,18},{6,19},{7,20},{8,21},{9,... | collective-permute-start | bytes 466952
  1436.4 25.1 %collective-permute-start.8 = (f32[8,4864]{1,0:T(8,128)}, f32[8,4864]{1,0:T(8,128)S(1)}, u32[]{:S(2)}, u32[]{:S(2)}) collective-permute-start(f32[8,4864]{1,0:T(8,128)} %get-tuple-element.114), channel_id=1, source_target_pairs={{0,9},{1,10},{2,11},{3,12},{4,13},{5,14},{6,15},{7,16},{8,17},{9,1... | collective-permute-start | bytes 466952
  1439.0 24.7 %collective-permute-start.7 = (f32[8,4864]{1,0:T(8,128)}, f32[8,4864]{1,0:T(8,128)S(1)}, u32[]{:S(2)}, u32[]{:S(2)}) collective-permute-start(f32[8,4864]{1,0:T(8,128)} %get-tuple-element.114), channel_id=1, source_target_pairs={{0,8},{1,9},{2,10},{3,11},{4,12},{5,13},{6,14},{7,15},{8,16},{9,17... | collective-permute-start | bytes 466952
  1440.9 39.4 %collective-permute-start.6 = (f32[8,4864]{1,0:T(8,128)}, f32[8,4864]{1,0:T(8,128)S(1)}, u32[]{:S(2)}, u32[]{:S(2)}) collective-permute-start(f32[8,4864]{1,0:T(8,128)} %get-tuple-element.114), channel_id=1, source_target_pairs={{0,7},{1,8},{2,9},{3,10},{4,11},{5,12},{6,13},{7,14},{8,15},{9,16}... | collective-permute-start | bytes 466952
  1442.9 39.4 %collective-permute-start.5 = (f32[8,4864]{1,0:T(8,128)}, f32[8,4864]{1,0:T(8,128)S(1)}, u32[]{:S(2)}, u32[]{:S(2)}) collective-permute-start(f32[8,4864]{1,0:T(8,128)} %get-tuple-element.114), channel_id=1, source_target_pairs={{0,6},{1,7},{2,8},{3,9},{4,10},{5,11},{6,12},{7,13},{8,14},{9,15},... | collective-permute-start | bytes 466952
  1446.0 38.7 %collective-permute-start.4 = (f32[8,4864]{1,0:T(8,128)}, f32[8,4864]{1,0:T(8,128)S(1)}, u32[]{:S(2)}, u32[]{:S(2)}) collective-permute-start(f32[8,4864]{1,0:T(8,128)} %get-tuple-element.114), channel_id=1, source_target_pairs={{0,5},{1,6},{2,7},{3,8},{4,9},{5,10},{6,11},{7,12},{8,13},{9,14},{... | collective-permute-start | bytes 466952
  1461.5 55.6 %collective-permute-start.3 = (f32[8,4864]{1,0:T(8,128)}, f32[8,4864]{1,0:T(8,128)}, u32[]{:S(2)}, u32[]{:S(2)}) collective-permute-start(f32[8,4864]{1,0:T(8,128)} %get-tuple-element.114), channel_id=1, source_target_pairs={{0,4},{1,5},{2,6},{3,7},{4,8},{5,9},{6,10},{7,11},{8,12},{9,13},{1... | collective-permute-start | bytes 466952
  1463.7 58.3 %collective-permute-start.2 = (f32[8,4864]{1,0:T(8,128)}, f32[8,4864]{1,0:T(8,128)}, u32[]{:S(2)}, u32[]{:S(2)}) collective-permute-start(f32[8,4864]{1,0:T(8,128)} %get-tuple-element.114), channel_id=1, source_target_pairs={{0,3},{1,4},{2,5},{3,6},{4,7},{5,8},{6,9},{7,10},{8,11},{9,12},{10... | collective-permute-start | bytes 466952
  1480.3 47.4 %collective-permute-start.1 = (f32[8,4864]{1,0:T(8,128)}, f32[8,4864]{1,0:T(8,128)}, u32[]{:S(2)}, u32[]{:S(2)}) collective-permute-start(f32[8,4864]{1,0:T(8,128)} %get-tuple-element.114), channel_id=1, source_target_pairs={{0,2},{1,3},{2,4},{3,5},{4,6},{5,7},{6,8},{7,9},{8,10},{9,11},{10,... | collective-permute-start | bytes 466952
  1482.2 47.4 %collective-permute-start = (f32[8,4864]{1,0:T(8,128)}, f32[8,4864]{1,0:T(8,128)}, u32[]{:S(2)}, u32[]{:S(2)}) collective-permute-start(f32[8,4864]{1,0:T(8,128)} %get-tuple-element.114), channel_id=1, source_target_pairs={{0,1},{1,2},{2,3},{3,4},{4,5},{5,6},{6,7},{7,8},{8,9},{9,10},{10,1... | collective-permute-start | bytes 466952
  1484.8 52.1 %collective-permute-start.30 = (f32[8,4864]{1,0:T(8,128)S(1)}, f32[8,4864]{1,0:T(8,128)}, u32[]{:S(2)}, u32[]{:S(2)}) collective-permute-start(f32[8,4864]{1,0:T(8,128)S(1)} %copy-done.58), channel_id=1, source_target_pairs={{0,15},{1,16},{2,17},{3,18},{4,19},{5,20},{6,21},{7,22},{8,23},{9,... | collective-permute-start | bytes 466952
  1517.1 23.3 %collective-permute-start.29 = (f32[8,4864]{1,0:T(8,128)S(1)}, f32[8,4864]{1,0:T(8,128)S(1)}, u32[]{:S(2)}, u32[]{:S(2)}) collective-permute-start(f32[8,4864]{1,0:T(8,128)S(1)} %copy-done.58), channel_id=1, source_target_pairs={{0,14},{1,15},{2,16},{3,17},{4,18},{5,19},{6,20},{7,21},{8,22},{9,... | collective-permute-start | bytes 466952
  1522.0 21.0 %collective-permute-start.28 = (f32[8,4864]{1,0:T(8,128)S(1)}, f32[8,4864]{1,0:T(8,128)S(1)}, u32[]{:S(2)}, u32[]{:S(2)}) collective-permute-start(f32[8,4864]{1,0:T(8,128)S(1)} %copy-done.58), channel_id=1, source_target_pairs={{0,13},{1,14},{2,15},{3,16},{4,17},{5,18},{6,19},{7,20},{8,21},{9,... | collective-permute-start | bytes 466952
  1529.6 21.1 %collective-permute-start.26 = (f32[8,4864]{1,0:T(8,128)S(1)}, f32[8,4864]{1,0:T(8,128)S(1)}, u32[]{:S(2)}, u32[]{:S(2)}) collective-permute-start(f32[8,4864]{1,0:T(8,128)S(1)} %copy-done.58), channel_id=1, source_target_pairs={{0,11},{1,12},{2,13},{3,14},{4,15},{5,16},{6,17},{7,18},{8,19},{9,... | collective-permute-start | bytes 466952
  1543.0 21.0 %collective-permute-start.23 = (f32[8,4864]{1,0:T(8,128)S(1)}, f32[8,4864]{1,0:T(8,128)S(1)}, u32[]{:S(2)}, u32[]{:S(2)}) collective-permute-start(f32[8,4864]{1,0:T(8,128)S(1)} %copy-done.58), channel_id=1, source_target_pairs={{0,8},{1,9},{2,10},{3,11},{4,12},{5,13},{6,14},{7,15},{8,16},{9,17... | collective-permute-start | bytes 466952
  1545.8 23.1 %collective-permute-start.22 = (f32[8,4864]{1,0:T(8,128)S(1)}, f32[8,4864]{1,0:T(8,128)S(1)}, u32[]{:S(2)}, u32[]{:S(2)}) collective-permute-start(f32[8,4864]{1,0:T(8,128)S(1)} %copy-done.58), channel_id=1, source_target_pairs={{0,7},{1,8},{2,9},{3,10},{4,11},{5,12},{6,13},{7,14},{8,15},{9,16}... | collective-permute-start | bytes 466952
  1568.9 21.1 %collective-permute-start.17 = (f32[8,4864]{1,0:T(8,128)S(1)}, f32[8,4864]{1,0:T(8,128)S(1)}, u32[]{:S(2)}, u32[]{:S(2)}) collective-permute-start(f32[8,4864]{1,0:T(8,128)S(1)} %copy-done.58), channel_id=1, source_target_pairs={{0,2},{1,3},{2,4},{3,5},{4,6},{5,7},{6,8},{7,9},{8,10},{9,11},{10,... | collective-permute-start | bytes 466952
  1570.9 21.7 %collective-permute-start.16 = (f32[8,4864]{1,0:T(8,128)S(1)}, f32[8,4864]{1,0:T(8,128)S(1)}, u32[]{:S(2)}, u32[]{:S(2)}) collective-permute-start(f32[8,4864]{1,0:T(8,128)S(1)} %copy-done.58), channel_id=1, source_target_pairs={{0,1},{1,2},{2,3},{3,4},{4,5},{5,6},{6,7},{7,8},{8,9},{9,10},{10,1... | collective-permute-start | bytes 466952
  1573.4 21.9 %collective-permute-start.57 = (f32[48,896]{1,0:T(8,128)S(1)}, f32[48,896]{1,0:T(8,128)S(1)}, u32[]{:S(2)}, u32[]{:S(2)}) collective-permute-start(f32[48,896]{1,0:T(8,128)S(1)} %fusion.2), channel_id=1, source_target_pairs={{0,26},{1,27},{2,28},{3,29},{4,30},{5,31},{6,32},{7,33},{8,34},{9,... | collective-permute-start | bytes 516104
  1595.3 21.0 %collective-permute-start.52 = (f32[48,896]{1,0:T(8,128)S(1)}, f32[48,896]{1,0:T(8,128)}, u32[]{:S(2)}, u32[]{:S(2)}) collective-permute-start(f32[48,896]{1,0:T(8,128)S(1)} %fusion.2), channel_id=1, source_target_pairs={{0,21},{1,22},{2,23},{3,24},{4,25},{5,26},{6,27},{7,28},{8,29},{9,... | collective-permute-start | bytes 516104
  1598.7 23.7 %collective-permute-start.51 = (f32[48,896]{1,0:T(8,128)S(1)}, f32[48,896]{1,0:T(8,128)S(1)}, u32[]{:S(2)}, u32[]{:S(2)}) collective-permute-start(f32[48,896]{1,0:T(8,128)S(1)} %fusion.2), channel_id=1, source_target_pairs={{0,20},{1,21},{2,22},{3,23},{4,24},{5,25},{6,26},{7,27},{8,28},{9,... | collective-permute-start | bytes 516104
  1602.7 25.6 %collective-permute-start.50 = (f32[48,896]{1,0:T(8,128)S(1)}, f32[48,896]{1,0:T(8,128)S(1)}, u32[]{:S(2)}, u32[]{:S(2)}) collective-permute-start(f32[48,896]{1,0:T(8,128)S(1)} %fusion.2), channel_id=1, source_target_pairs={{0,19},{1,20},{2,21},{3,22},{4,23},{5,24},{6,25},{7,26},{8,27},{9,... | collective-permute-start | bytes 516104
  1607.1 25.8 %collective-permute-start.49 = (f32[48,896]{1,0:T(8,128)S(1)}, f32[48,896]{1,0:T(8,128)S(1)}, u32[]{:S(2)}, u32[]{:S(2)}) collective-permute-start(f32[48,896]{1,0:T(8,128)S(1)} %fusion.2), channel_id=1, source_target_pairs={{0,18},{1,19},{2,20},{3,21},{4,22},{5,23},{6,24},{7,25},{8,26},{9,... | collective-permute-start | bytes 516104
  1611.6 23.2 %collective-permute-start.48 = (f32[48,896]{1,0:T(8,128)S(1)}, f32[48,896]{1,0:T(8,128)S(1)}, u32[]{:S(2)}, u32[]{:S(2)}) collective-permute-start(f32[48,896]{1,0:T(8,128)S(1)} %fusion.2), channel_id=1, source_target_pairs={{0,17},{1,18},{2,19},{3,20},{4,21},{5,22},{6,23},{7,24},{8,25},{9,... | collective-permute-start | bytes 516104
  1622.4 73.8 %collective-permute-start.46 = (f32[48,896]{1,0:T(8,128)S(1)}, f32[48,896]{1,0:T(8,128)S(1)}, u32[]{:S(2)}, u32[]{:S(2)}) collective-permute-start(f32[48,896]{1,0:T(8,128)S(1)} %fusion.2), channel_id=1, source_target_pairs={{0,15},{1,16},{2,17},{3,18},{4,19},{5,20},{6,21},{7,22},{8,23},{9,... | collective-permute-start | bytes 516104
  1628.3 72.1 %collective-permute-start.45 = (f32[48,896]{1,0:T(8,128)S(1)}, f32[48,896]{1,0:T(8,128)S(1)}, u32[]{:S(2)}, u32[]{:S(2)}) collective-permute-start(f32[48,896]{1,0:T(8,128)S(1)} %fusion.2), channel_id=1, source_target_pairs={{0,14},{1,15},{2,16},{3,17},{4,18},{5,19},{6,20},{7,21},{8,22},{9,... | collective-permute-start | bytes 516104
  1632.9 70.2 %collective-permute-start.44 = (f32[48,896]{1,0:T(8,128)S(1)}, f32[48,896]{1,0:T(8,128)S(1)}, u32[]{:S(2)}, u32[]{:S(2)}) collective-permute-start(f32[48,896]{1,0:T(8,128)S(1)} %fusion.2), channel_id=1, source_target_pairs={{0,13},{1,14},{2,15},{3,16},{4,17},{5,18},{6,19},{7,20},{8,21},{9,... | collective-permute-start | bytes 516104
  1634.8 70.7 %collective-permute-start.43 = (f32[48,896]{1,0:T(8,128)S(1)}, f32[48,896]{1,0:T(8,128)S(1)}, u32[]{:S(2)}, u32[]{:S(2)}) collective-permute-start(f32[48,896]{1,0:T(8,128)S(1)} %fusion.2), channel_id=1, source_target_pairs={{0,12},{1,13},{2,14},{3,15},{4,16},{5,17},{6,18},{7,19},{8,20},{9,... | collective-permute-start | bytes 516104
  1636.8 71.5 %collective-permute-start.42 = (f32[48,896]{1,0:T(8,128)S(1)}, f32[48,896]{1,0:T(8,128)S(1)}, u32[]{:S(2)}, u32[]{:S(2)}) collective-permute-start(f32[48,896]{1,0:T(8,128)S(1)} %fusion.2), channel_id=1, source_target_pairs={{0,11},{1,12},{2,13},{3,14},{4,15},{5,16},{6,17},{7,18},{8,19},{9,... | collective-permute-start | bytes 516104
  1696.2 69.9 %collective-permute-start.41 = (f32[48,896]{1,0:T(8,128)S(1)}, f32[48,896]{1,0:T(8,128)S(1)}, u32[]{:S(2)}, u32[]{:S(2)}) collective-permute-start(f32[48,896]{1,0:T(8,128)S(1)} %fusion.2), channel_id=1, source_target_pairs={{0,10},{1,11},{2,12},{3,13},{4,14},{5,15},{6,16},{7,17},{8,18},{9,... | collective-permute-start | bytes 516104
  1700.5 68.2 %collective-permute-start.40 = (f32[48,896]{1,0:T(8,128)S(1)}, f32[48,896]{1,0:T(8,128)S(1)}, u32[]{:S(2)}, u32[]{:S(2)}) collective-permute-start(f32[48,896]{1,0:T(8,128)S(1)} %fusion.2), channel_id=1, source_target_pairs={{0,9},{1,10},{2,11},{3,12},{4,13},{5,14},{6,15},{7,16},{8,17},{9,1... | collective-permute-start | bytes 516104
  1703.0 68.3 %collective-permute-start.39 = (f32[48,896]{1,0:T(8,128)S(1)}, f32[48,896]{1,0:T(8,128)S(1)}, u32[]{:S(2)}, u32[]{:S(2)}) collective-permute-start(f32[48,896]{1,0:T(8,128)S(1)} %fusion.2), channel_id=1, source_target_pairs={{0,8},{1,9},{2,10},{3,11},{4,12},{5,13},{6,14},{7,15},{8,16},{9,17... | collective-permute-start | bytes 516104
  1705.5 71.4 %collective-permute-start.38 = (f32[48,896]{1,0:T(8,128)S(1)}, f32[48,896]{1,0:T(8,128)}, u32[]{:S(2)}, u32[]{:S(2)}) collective-permute-start(f32[48,896]{1,0:T(8,128)S(1)} %fusion.2), channel_id=1, source_target_pairs={{0,7},{1,8},{2,9},{3,10},{4,11},{5,12},{6,13},{7,14},{8,15},{9,16}... | collective-permute-start | bytes 516104
  1708.3 71.0 %collective-permute-start.37 = (f32[48,896]{1,0:T(8,128)S(1)}, f32[48,896]{1,0:T(8,128)}, u32[]{:S(2)}, u32[]{:S(2)}) collective-permute-start(f32[48,896]{1,0:T(8,128)S(1)} %fusion.2), channel_id=1, source_target_pairs={{0,6},{1,7},{2,8},{3,9},{4,10},{5,11},{6,12},{7,13},{8,14},{9,15},... | collective-permute-start | bytes 516104
  (168 other events, 8475.1 us)
Sparse Core Ops, SparseCore 0:
  11.1 68.7 all-gather.14
  82.9 62.4 all-gather.16
  148.2 68.6 all-gather.18
  219.7 70.0 all-gather.20
  292.7 68.7 all-gather.22
  959.9 91.8 reduce-scatter.16
  1055.4 73.5 reduce-scatter.14
  1132.2 73.6 reduce-scatter.18
  1400.0 116.1 reduce-scatter.20
  1598.8 213.4 all-reduce.28
where the time goes:
time: 1940 us; the launch traced here: 1920 us
  blocking collectives  1180 us (61%)
  local copies, waits for them, and re-layouts  253 us (13%)
  starting transfers between devices  241 us (12%)
  matrix products  166 us (9%)
  waiting for transfers between devices  39 us (2%)
  other arithmetic  23.8 us (1%)
    unnamed x5, blocking collectives  983 us
    unnamed x62, starting transfers between devices  241 us
    unnamed x340, local copies, waits for them, and re-layouts  227 us
    dot_general x14, matrix products, matmul_tn(): lax.dot_general(left, right, (((0,), (0,)), ((), ())), preferred_element_...  69.7 us
    all_gather x1, blocking collectives, body(): lax.all_gather(value_weight, ('dp', 'ctx'), axis=0, tiled=True)  60.5 us
    all_gather x1, blocking collectives, body(): lax.all_gather(w_key, ('dp', 'ctx'), axis=0, tiled=True)  58 us
    all_gather x2, blocking collectives, body(): lax.all_gather(narrow_values, 'ctx', axis=0, tiled=True)  41.3 us
    dot_general x14, matrix products, matmul_nt(): lax.dot_general(left, right, (((1,), (1,)), ((), ())), preferred_element_...  39.9 us
  transfers between devices with their start and end apart: 69, of which 5 were waited for; matrix products, arithmetic and copies ran while one was open for 36% of the time, Pallas kernels for 0%

commit v1 on v0

v1 whole, which is shorter than its diff:
```python
import functools

import jax
import jax.numpy as jnp
import numpy as np
from jax import lax
from jax.experimental import pallas as pl
from jax.experimental.pallas import tpu as pltpu
from jax.sharding import PartitionSpec as P

QUERY_HEADS = 14
KEY_VALUE_HEADS = 2
HEAD_SIZE = 64
GROUP = QUERY_HEADS // KEY_VALUE_HEADS
MB = 2
D = 896
DPAD = 1024
EPSILON = 1e-06
THETA_BASE = 1000000.0
F32 = jnp.float32
BF16 = jnp.bfloat16
MESH = pl.DeviceIdType.MESH
DMA = pltpu.SemaphoreType.DMA
VM = pltpu.VMEM


def remote(src, dst, ss, rs, peer):
    return pltpu.make_async_remote_copy(
        src_ref=src, dst_ref=dst, send_sem=ss, recv_sem=rs, device_id=peer, device_id_type=MESH
    )


def barrier(peers):
    sem = pltpu.get_barrier_semaphore()
    for peer in peers:
        pl.semaphore_signal(sem, inc=1, device_id=peer, device_id_type=MESH)
    pl.semaphore_wait(sem, len(peers))


class Place:
    def __init__(self):
        self.dp = lax.axis_index("dp")
        self.ctx = lax.axis_index("ctx")
        self.y, self.x = self.ctx // 4, lax.rem(self.ctx, 4)
        self.z, self.core = self.dp // 2, lax.rem(self.dp, 2)

    def at_x(self, k):
        return lax.rem(self.x + (k + 4), 4)

    def at_y(self, k):
        return lax.rem(self.y + (k + 4), 4)

    def at_z(self, k):
        return lax.rem(self.z + (k + 4), 4)

    def line(self, axis, k):
        return self.y * 4 + self.at_x(k) if axis == 0 else self.at_y(k) * 4 + self.x

    def xpeer(self, k):
        return {"ctx": self.line(0, k)}

    def ypeer(self, k):
        return {"ctx": self.line(1, k)}

    def peer(self, axis, k):
        return {"ctx": self.line(axis, k)}

    def zindex(self, k):
        return self.at_z(k) * 2 + self.core

    def mate(self):
        return self.z * 2 + 1 - self.core

    def dpindex(self, k):
        return lax.rem(self.dp + k, 8)


NEAR = (1, 3, 2)


class GatherCtx:
    SEMS = [DMA((2, 4)), DMA((2, 4)), DMA((2, 4, 4)), DMA((2, 4, 4)), DMA]

    def __init__(self, place, src, dst, sems):
        self.p, self.src, self.dst, self.sems = place, src, dst, sems

    def start(self):
        p, (s1, r1, s2, r2, ls) = self.p, self.sems
        self.local = pltpu.make_async_copy(self.src, self.dst.at[p.ctx], ls)
        self.local.start()
        self.first = {}
        for k in NEAR:
            for h in (0, 1):
                c = remote(self.src.at[h], self.dst.at[p.ctx, h], s1.at[h, k], r1.at[h, k], p.peer(h, k))
                c.start()
                self.first[h, k] = c

    def forward(self):
        p, (s1, r1, s2, r2, ls) = self.p, self.sems
        self.second = []
        for j in (0,) + NEAR:
            for h in (0, 1):
                if j:
                    self.first[h, j].wait_recv()
                block = p.line(h, -j)
                for k in NEAR:
                    src = self.src.at[h] if j == 0 else self.dst.at[block, h]
                    c = remote(src, self.dst.at[block, h], s2.at[h, j, k], r2.at[h, j, k], p.peer(1 - h, k))
                    c.start()
                    self.second.append(c)

    def arrive(self):
        self.local.wait()
        for c in self.second:
            c.wait_recv()

    def finish(self):
        for c in list(self.first.values()) + self.second:
            c.wait_send()


class ReduceCtx:
    SEMS = [DMA((2, 4)), DMA((2, 4)), DMA((2, 4)), DMA((2, 4))]

    @staticmethod
    def scratch(rows, cols):
        return [VM((2, 3, 4, rows, cols), BF16), VM((2, 4, rows, cols), BF16), VM((2, 3, rows, cols), BF16)]

    def __init__(self, place, src, bufs, sems):
        self.p, self.src, self.bufs, self.sems = place, src, bufs, sems

    def start(self):
        p, (s1, r1, s2, r2) = self.p, self.sems
        got = self.bufs[0]
        self.first = {}
        for k in NEAR:
            for h in (0, 1):
                src = self.src.at[p.at_y(k), :, 0] if h == 0 else self.src.at[:, p.at_x(k), 1]
                c = remote(src, got.at[h, k - 1], s1.at[h, k], r1.at[h, k], p.peer(1 - h, k))
                c.start()
                self.first[h, k] = c

    def forward(self):
        p, (s1, r1, s2, r2) = self.p, self.sems
        got, mid, last = self.bufs
        self.second = {}
        for h in (0, 1):
            for k in NEAR:
                self.first[h, k].wait_recv()
            for i in range(4):
                own = self.src[p.y, i, 0] if h == 0 else self.src[i, p.x, 1]
                total = own.astype(F32)
                for k in NEAR:
                    total = total + got[h, k - 1, i].astype(F32)
                mid[h, i] = total.astype(BF16)
            for k in NEAR:
                to = p.at_x(k) if h == 0 else p.at_y(k)
                c = remote(mid.at[h, to], last.at[h, k - 1], s2.at[h, k], r2.at[h, k], p.peer(h, k))
                c.start()
                self.second[h, k] = c

    def result(self, h):
        p = self.p
        got, mid, last = self.bufs
        for k in NEAR:
            self.second[h, k].wait_recv()
        total = mid[h, p.x if h == 0 else p.y].astype(F32)
        for k in NEAR:
            total = total + last[h, k - 1].astype(F32)
        return total

    def finish(self):
        for c in list(self.first.values()) + list(self.second.values()):
            c.wait_send()


class GatherDp:
    SEMS = [DMA((4,)), DMA((4,)), DMA((4,)), DMA((4,)), DMA]

    def __init__(self, place, src, dst, sems):
        self.p, self.src, self.dst, self.sems = place, src, dst, sems

    def start(self):
        p, (s1, r1, s2, r2, ls) = self.p, self.sems
        self.local = pltpu.make_async_copy(self.src, self.dst.at[p.dp], ls)
        self.local.start()
        self.first = {}
        for k in NEAR:
            c = remote(self.src, self.dst.at[p.dp], s1.at[k], r1.at[k], {"dp": p.zindex(k)})
            c.start()
            self.first[k] = c

    def forward(self):
        p, (s1, r1, s2, r2, ls) = self.p, self.sems
        self.second = []
        for j in (0,) + NEAR:
            if j:
                self.first[j].wait_recv()
            block = p.zindex(-j)
            src = self.src if j == 0 else self.dst.at[block]
            c = remote(src, self.dst.at[block], s2.at[j], r2.at[j], {"dp": p.mate()})
            c.start()
            self.second.append(c)

    def arrive(self):
        self.local.wait()
        for c in self.second:
            c.wait_recv()

    def finish(self):
        for c in list(self.first.values()) + self.second:
            c.wait_send()


class ReduceDp:
    SEMS = [DMA((4,)), DMA((4,)), DMA((4,)), DMA((4,))]

    @staticmethod
    def scratch(rows, cols):
        return [VM((4, rows, cols), BF16), VM((4, rows, cols), BF16), VM((3, rows, cols), BF16)]

    def __init__(self, place, src, bufs, sems):
        self.p, self.src, self.bufs, self.sems = place, src, bufs, sems

    def start(self):
        p, (s1, r1, s2, r2) = self.p, self.sems
        self.first = {}
        for k in NEAR + (0,):
            to = p.at_z(k)
            c = remote(self.src.at[to, 1 - p.core], self.bufs[0].at[to], s1.at[k], r1.at[k], {"dp": p.mate()})
            c.start()
            self.first[k] = c

    def forward(self):
        p, (s1, r1, s2, r2) = self.p, self.sems
        got, mid, last = self.bufs
        self.second = {}
        for k in NEAR + (0,):
            to = p.at_z(k)
            self.first[k].wait_recv()
            total = self.src[to, p.core].astype(F32) + got[to].astype(F32)
            mid[to] = total.astype(BF16)
            if k:
                c = remote(mid.at[to], last.at[k - 1], s2.at[k], r2.at[k], {"dp": p.zindex(k)})
                c.start()
                self.second[k] = c

    def result(self):
        got, mid, last = self.bufs
        total = mid[self.p.z].astype(F32)
        for k in NEAR:
            self.second[k].wait_recv()
            total = total + last[k - 1].astype(F32)
        return total

    def finish(self):
        for c in list(self.first.values()) + list(self.second.values()):
            c.wait_send()


def xy_peers(p):
    return [p.peer(axis, k) for axis in (0, 1) for k in NEAR]


def dp_peers(p):
    return [{"dp": p.dpindex(k)} for k in range(1, 8)]


def z_peers(p):
    return [{"dp": p.zindex(k)} for k in NEAR] + [{"dp": p.mate()}]


def comm_call(kernel, args, outs, scratch, cid, name):
    return pl.pallas_call(
        kernel,
        out_shape=outs,
        in_specs=[pl.BlockSpec(memory_space=VM)] * len(args),
        out_specs=jax.tree.map(lambda _: pl.BlockSpec(memory_space=VM), outs),
        scratch_shapes=scratch,
        name=name,
        compiler_params=pltpu.CompilerParams(
            collective_id=cid, has_side_effects=True, vmem_limit_bytes=56 << 20
        ),
    )(*args)


def shape(dims, kind):
    return jax.ShapeDtypeStruct(dims, kind)


def weights_kernel(
    attn, gate_up, down, small, places, cot,
    w_attn, w_gate_up, w_down, small_all, places_all, cot_all,
    attn_in, gu_in, down_in, small_x, small_y, small_dp, places_x, attn_block, gu_block, small_sum,
    s_attn, r_attn, s_gu, r_gu, s_down, r_down, s_down2, r_down2, s_small, r_small, s_place, r_place,
    s_place2, r_place2, s_mate, r_mate, local_sem, local2, *ring_sems,
):
    p = Place()
    barrier(xy_peers(p) + dp_peers(p))
    to_dp = []
    for k in range(1, 8):
        to = p.dpindex(k)
        c = remote(attn, attn_in.at[p.dp], s_attn.at[k], r_attn.at[k], {"dp": to})
        c.start()
        to_dp.append(c)
    for k in range(1, 8):
        to = p.dpindex(k)
        c = remote(gate_up.at[to], gu_in.at[p.dp], s_gu.at[k], r_gu.at[k], {"dp": to})
        c.start()
        to_dp.append(c)
    small_copies = []
    for k in NEAR:
        c = remote(small, small_x.at[k - 1], s_small.at[0, k], r_small.at[0, k], p.xpeer(k))
        c.start()
        small_copies.append(c)
    place_copies = []
    for k in NEAR:
        c = remote(places, places_x.at[p.x], s_place.at[k], r_place.at[k], p.xpeer(k))
        c.start()
        place_copies.append(c)
    down_copies = []
    for k in NEAR:
        c = remote(down, down_in.at[p.x], s_down.at[k], r_down.at[k], p.xpeer(k))
        c.start()
        down_copies.append(c)
    cots = GatherDp(p, cot, cot_all, ring_sems[10:15])
    cots.start()
    attn_in[p.dp] = attn[...]
    gu_in[p.dp] = gate_up[p.dp]
    down_in[p.x] = down[...]
    places_x[p.x] = places[...]
    for c in to_dp[:7]:
        c.wait_recv()
    for half in (0, 1):
        for i in range(2):
            attn_block[half, i] = jnp.concatenate(
                [attn_in[4 * i + d, half] for d in range(4)], axis=0
            ).astype(BF16)
    own = attn_block.at[p.core]
    target = w_attn.at[p.core]
    ring_attn = GatherCtx(p, own, target, ring_sems[0:5])
    ring_attn.start()
    for c in to_dp[7:]:
        c.wait_recv()
    for i in range(2):
        gu_block[i] = jnp.concatenate([gu_in[4 * i + d] for d in range(4)], axis=0).astype(BF16)
    ring_gu = GatherCtx(p, gu_block, w_gate_up, ring_sems[5:10])
    ring_gu.start()
    total = small[...]
    for c in small_copies:
        c.wait_recv()
    for k in NEAR:
        total = total + small_x[k - 1]
    small_sum[0] = total
    small_y_copies = []
    for k in NEAR:
        c = remote(small_sum.at[0], small_y.at[k - 1], s_small.at[1, k], r_small.at[1, k], p.ypeer(k))
        c.start()
        small_y_copies.append(c)
    ring_attn.forward()
    for c in place_copies:
        c.wait_recv()
    place_copies2 = []
    for k in NEAR:
        c = remote(places_x, places_all.at[p.y], s_place2.at[k], r_place2.at[k], p.ypeer(k))
        c.start()
        place_copies2.append(c)
    places_all[p.y] = places_x[...]
    for c in down_copies:
        c.wait_recv()
    w_down[p.y] = jnp.concatenate([down_in[i] for i in range(4)], axis=0).astype(BF16)
    down_copies2 = []
    for k in NEAR:
        c = remote(w_down.at[p.y], w_down.at[p.y], s_down2.at[k], r_down2.at[k], p.ypeer(k))
        c.start()
        down_copies2.append(c)
    for c in small_y_copies:
        c.wait_recv()
    total = small_sum[0]
    for k in NEAR:
        total = total + small_y[k - 1]
    small_sum[1] = total
    small_dp_copies = []
    for k in range(1, 8):
        c = remote(small_sum.at[1], small_dp.at[k - 1], s_small.at[2, k], r_small.at[2, k], {"dp": p.dpindex(k)})
        c.start()
        small_dp_copies.append(c)
    cots.forward()
    ring_gu.forward()
    ring_attn.arrive()
    mate = remote(w_attn.at[p.core], w_attn.at[p.core], s_mate, r_mate, {"dp": p.mate()})
    mate.start()
    total = small_sum[1]
    for k in range(1, 8):
        small_dp_copies[k - 1].wait_recv()
        total = total + small_dp[k - 1]
    small_all[...] = total
    cots.arrive()
    for c in down_copies2 + place_copies2:
        c.wait_recv()
    ring_gu.arrive()
    mate.wait()
    for ring in (ring_attn, ring_gu, cots):
        ring.finish()
    for c in to_dp + small_copies + place_copies + down_copies + place_copies2 + down_copies2 + small_y_copies:
        c.wait_send()
    for c in small_dp_copies:
        c.wait_send()


def gather_weights(attn, gate_up, down, small, places, cot):
    outs = (
        shape((2, 16, 2, 32, 1024), BF16),
        shape((16, 2, 32, 1280), BF16),
        shape((4, 160, D), BF16),
        shape((24, 128), F32),
        shape((4, 4, 8, 128), F32),
        shape((8, 128, D), BF16),
    )
    scratch = [
        VM((8, 2, 8, 1024), F32), VM((8, 8, 1280), F32), VM((4, 40, D), F32), VM((3, 24, 128), F32),
        VM((3, 24, 128), F32), VM((7, 24, 128), F32), VM((4, 8, 128), F32), VM((2, 2, 32, 1024), BF16),
        VM((2, 32, 1280), BF16), VM((2, 24, 128), F32),
        DMA((8,)), DMA((8,)), DMA((8,)), DMA((8,)), DMA((4,)), DMA((4,)), DMA((4,)), DMA((4,)),
        DMA((3, 8)), DMA((3, 8)), DMA((4,)), DMA((4,)), DMA((4,)), DMA((4,)), DMA, DMA, DMA, DMA,
    ] + GatherCtx.SEMS * 2 + GatherDp.SEMS
    return comm_call(
        weights_kernel, (attn, gate_up, down, small, places, cot), outs, scratch, 0, "gather_weights"
    )


def grads_kernel(
    g_attn, g_gu, g_down, small,
    o_attn, o_gu, o_down, o_small,
    mate_in, attn_sum, down_y, down_mid, down_x, attn_out, gu_out, attn_dp, small_x, small_y, small_dp, small_sum,
    *rest,
):
    bufs_attn, bufs_gu, rest = rest[:3], rest[3:6], rest[6:]
    (s_mate, r_mate, s_down, r_down, s_down2, r_down2, s_small, r_small, s_attn, r_attn, s_gu, r_gu) = rest[:12]
    sems_attn, sems_gu = rest[12:16], rest[16:20]
    p = Place()
    barrier(xy_peers(p) + dp_peers(p))
    mate_copies = []
    for y in range(4):
        c = remote(g_attn.at[1 - p.core, y], mate_in.at[y], s_mate.at[y], r_mate.at[y], {"dp": p.mate()})
        c.start()
        mate_copies.append(c)
    small_copies = []
    for k in NEAR:
        c = remote(small, small_x.at[k - 1], s_small.at[0, k], r_small.at[0, k], p.xpeer(k))
        c.start()
        small_copies.append(c)
    ring_gu = ReduceCtx(p, g_gu, bufs_gu, sems_gu)
    ring_gu.start()
    down_copies = []
    for k in NEAR:
        c = remote(g_down.at[p.at_y(k)], down_y.at[k - 1], s_down.at[k], r_down.at[k], p.ypeer(k))
        c.start()
        down_copies.append(c)
    for y in range(4):
        mate_copies[y].wait_recv()
        attn_sum[y] = (g_attn[p.core, y].astype(F32) + mate_in[y].astype(F32)).astype(BF16)
    ring_attn = ReduceCtx(p, attn_sum, bufs_attn, sems_attn)
    ring_attn.start()
    for c in small_copies:
        c.wait_recv()
    small_sum[0] = small[...] + small_x[0] + small_x[1] + small_x[2]
    small_y_copies = []
    for k in NEAR:
        c = remote(small_sum.at[0], small_y.at[k - 1], s_small.at[1, k], r_small.at[1, k], p.ypeer(k))
        c.start()
        small_y_copies.append(c)
    ring_gu.forward()
    for c in down_copies:
        c.wait_recv()
    total = g_down[p.y].astype(F32)
    for k in NEAR:
        total = total + down_y[k - 1].astype(F32)
    for i in range(4):
        down_mid[i] = total[40 * i : 40 * i + 40]
    down_copies2 = []
    for k in NEAR:
        c = remote(down_mid.at[p.at_x(k)], down_x.at[k - 1], s_down2.at[k], r_down2.at[k], p.xpeer(k))
        c.start()
        down_copies2.append(c)
    for c in small_y_copies:
        c.wait_recv()
    small_sum[1] = small_sum[0] + small_y[0] + small_y[1] + small_y[2]
    small_dp_copies = []
    for k in range(1, 8):
        c = remote(small_sum.at[1], small_dp.at[k - 1], s_small.at[2, k], r_small.at[2, k], {"dp": p.dpindex(k)})
        c.start()
        small_dp_copies.append(c)
    ring_attn.forward()
    for h in (0, 1):
        part = ring_gu.result(h)
        for d in range(4):
            gu_out[4 * h + d] = part[8 * d : 8 * d + 8]
    out_copies = []
    for k in range(1, 8):
        to = p.dpindex(k)
        c = remote(gu_out.at[to], o_gu.at[p.dp], s_gu.at[k], r_gu.at[k], {"dp": to})
        c.start()
        out_copies.append(c)
    o_gu[p.dp] = gu_out[p.dp]
    for c in down_copies2:
        c.wait_recv()
    o_down[...] = down_mid[p.x] + down_x[0] + down_x[1] + down_x[2]
    for h in (0, 1):
        part = ring_attn.result(h)
        for d in range(4):
            attn_out[4 * h + d] = part[8 * d : 8 * d + 8]
    for k in range(1, 8):
        to = p.dpindex(k)
        c = remote(attn_out.at[to], attn_dp.at[p.z, p.core], s_attn.at[k], r_attn.at[k], {"dp": to})
        c.start()
        out_copies.append(c)
    attn_dp[p.z, p.core] = attn_out[p.dp]
    total = small_sum[1]
    for k in range(1, 8):
        small_dp_copies[k - 1].wait_recv()
        total = total + small_dp[k - 1]
    o_small[...] = total
    for c in out_copies:
        c.wait_recv()
    for half in (0, 1):
        o_attn[half] = attn_dp[0, half] + attn_dp[1, half] + attn_dp[2, half] + attn_dp[3, half]
    ring_gu.finish()
    ring_attn.finish()
    for c in mate_copies + small_copies + small_y_copies + small_dp_copies + down_copies + down_copies2 + out_copies:
        c.wait_send()


def reduce_grads(g_attn, g_gu, g_down, small):
    outs = (
        shape((2, 8, 1024), F32),
        shape((8, 8, 1280), F32),
        shape((40, D), F32),
        shape((24, 128), F32),
    )
    scratch = [
        VM((4, 4, 2, 32, 1024), BF16), VM((4, 4, 2, 32, 1024), BF16), VM((3, 160, D), BF16), VM((4, 40, D), F32),
        VM((3, 40, D), F32), VM((8, 8, 1024), F32), VM((8, 8, 1280), F32), VM((4, 2, 8, 1024), F32),
        VM((3, 24, 128), F32), VM((3, 24, 128), F32), VM((7, 24, 128), F32), VM((2, 24, 128), F32),
    ] + ReduceCtx.scratch(32, 1024) + ReduceCtx.scratch(32, 1280) + [
        DMA((4,)), DMA((4,)), DMA((4,)), DMA((4,)), DMA((4,)), DMA((4,)), DMA((3, 8)), DMA((3, 8)),
        DMA((8,)), DMA((8,)), DMA((8,)), DMA((8,)),
    ] + ReduceCtx.SEMS * 2
    return comm_call(grads_kernel, (g_attn, g_gu, g_down, small), outs, scratch, 1, "reduce_grads")


def gather_ctx_kernel(src, dst, *sems):
    p = Place()
    barrier(xy_peers(p))
    ring = GatherCtx(p, src, dst, sems)
    ring.start()
    ring.forward()
    ring.arrive()
    ring.finish()


def gather_ctx(src, cid, name):
    return comm_call(
        gather_ctx_kernel, (src,), shape((16,) + src.shape, src.dtype), GatherCtx.SEMS, cid, name
    )


def reduce_ctx_kernel(src, out, b0, b1, b2, *sems):
    p = Place()
    barrier(xy_peers(p))
    ring = ReduceCtx(p, src, (b0, b1, b2), sems)
    ring.start()
    ring.forward()
    for h in (0, 1):
        out[h] = ring.result(h)
    ring.finish()


def reduce_ctx(src, cid, name):
    rows, cols = src.shape[-2:]
    return comm_call(
        reduce_ctx_kernel, (src,), shape((2, rows, cols), F32),
        ReduceCtx.scratch(rows, cols) + ReduceCtx.SEMS, cid, name,
    )


def gather_dp_kernel(src, dst, *sems):
    p = Place()
    barrier(z_peers(p))
    ring = GatherDp(p, src, dst, sems)
    ring.start()
    ring.forward()
    ring.arrive()
    ring.finish()


def gather_dp(src, cid, name):
    return comm_call(gather_dp_kernel, (src,), shape((8,) + src.shape, src.dtype), GatherDp.SEMS, cid, name)


def reduce_dp_kernel(src, out, b0, b1, b2, *sems):
    p = Place()
    barrier(z_peers(p))
    ring = ReduceDp(p, src, (b0, b1, b2), sems)
    ring.start()
    ring.forward()
    out[...] = ring.result()
    ring.finish()


def reduce_dp(src, cid, name):
    rows, cols = src.shape[-2:]
    return comm_call(
        reduce_dp_kernel, (src,), shape((rows, cols), F32), ReduceDp.scratch(rows, cols) + ReduceDp.SEMS, cid, name
    )


def matrix_product(left, right):
    return jnp.dot(left, right, preferred_element_type=F32)


def matmul_tn(left, right):
    return lax.dot_general(left, right, (((0,), (0,)), ((), ())), preferred_element_type=F32)


def matmul_nt(left, right):
    return lax.dot_general(left, right, (((1,), (1,)), ((), ())), preferred_element_type=F32)


def rms_scale(values):
    return lax.rsqrt(jnp.mean(values * values, axis=-1, keepdims=True) + EPSILON)


def rope_tables(places, head_dim):
    freqs = THETA_BASE ** (-jnp.arange(0, head_dim, 2).astype(F32) / head_dim)
    angles = places.astype(F32)[:, None] * freqs[None, :]
    angles = jnp.concatenate([angles, angles], axis=-1)
    return (jnp.cos(angles), jnp.sin(angles))


def apply_rotary(values, cosine_table, sine_table):
    half_dim = values.shape[-1] // 2
    turned = jnp.concatenate([-values[..., half_dim:], values[..., :half_dim]], axis=-1)
    return values * cosine_table[:, None, :] + turned * sine_table[:, None, :]


def inverse_rotary(grads, cosine_table, sine_table):
    half_dim = grads.shape[-1] // 2
    direct = grads * cosine_table[:, None, :]
    turned = grads * sine_table[:, None, :]
    return direct + jnp.concatenate([turned[..., half_dim:], -turned[..., :half_dim]], axis=-1)


def attend(queries, key_all, value_all, query_places, key_places, factor):
    scores = jnp.einsum("bqghd,bkgd->bghqk", queries, key_all, preferred_element_type=F32) * factor
    allowed = key_places[:, None, :] <= query_places[:, :, None]
    scores = jnp.where(allowed[:, None, None], scores, -1e30)
    top = jnp.max(scores, axis=-1, keepdims=True)
    expo = jnp.exp(scores - top)
    probs = (expo / jnp.sum(expo, axis=-1, keepdims=True)).astype(BF16)
    return probs, jnp.einsum("bghqk,bkgd->bqghd", probs, value_all, preferred_element_type=F32)


def attend_back(queries, key_all, value_all, probs, attended_gradient, factor):
    grad_probs = jnp.einsum("bqghd,bkgd->bghqk", attended_gradient, value_all, preferred_element_type=F32)
    wide = probs.astype(F32)
    inner = jnp.sum(wide * grad_probs, axis=-1, keepdims=True)
    grad_scores = (wide * (grad_probs - inner)).astype(BF16)
    grad_query = jnp.einsum("bghqk,bkgd->bqghd", grad_scores, key_all, preferred_element_type=F32) * factor
    grad_key = jnp.einsum("bghqk,bqghd->bkgd", grad_scores, queries, preferred_element_type=F32) * factor
    grad_value = jnp.einsum("bghqk,bqghd->bkgd", probs, attended_gradient, preferred_element_type=F32)
    return grad_query, grad_key, grad_value


def spread(values, kind):
    rows = values.shape[0]
    parts = values.astype(kind).reshape(rows, 8, 16, 7)
    parts = jnp.pad(parts, ((0, 0), (0, 0), (0, 0), (0, 1)))
    return parts.transpose(0, 2, 1, 3).reshape(rows, DPAD)


def unspread(values):
    rows = values.shape[0]
    return values.reshape(rows, 16, 8, 8)[..., :7].transpose(0, 2, 1, 3).reshape(rows, D)


def body(
    hidden_in, positions, norm_attn, w_query, b_query, w_key, b_key, value_weight, value_bias, w_output,
    norm_mlp, w_gate, w_up, w_down, cotangent,
):
    factor = HEAD_SIZE ** (-0.5)
    rows = MB * 64
    me = lax.axis_index("dp") * 16 + lax.axis_index("ctx")
    places = positions[:, 0]
    attn = jnp.pad(
        jnp.stack(
            [jnp.concatenate([w_query, w_key], axis=1), jnp.concatenate([value_weight, w_output], axis=1)]
        ).astype(F32),
        ((0, 0), (0, 1), (0, 0)),
    )

    def slices(w):
        parts = w.astype(F32).reshape(7, 8, 16, 38)
        return jnp.pad(parts, ((0, 1), (0, 0), (0, 0), (0, 2))).transpose(1, 0, 2, 3).reshape(8, 8, 640)

    gate_up = jnp.concatenate([slices(w_gate), slices(w_up)], axis=-1)
    down = jnp.pad(w_down.astype(F32), ((0, 2), (0, 0)))

    def put(vector, width):
        full = jnp.zeros((128, width), F32)
        return lax.dynamic_update_slice(full, vector.astype(F32)[None], (me, 0)).reshape(-1)

    small = jnp.concatenate(
        [put(norm_attn, 7), put(b_query, 7), put(norm_mlp, 7), put(b_key, 1), put(value_bias, 1), jnp.zeros((128,), F32)]
    ).reshape(24, 128)
    place_rows = jnp.pad(jnp.tile(places.astype(F32), (1, 2)), ((0, 6), (0, 0)))
    cot = cotangent.reshape(rows, D)
    w_attn, w_gu, down_full, small_all, places_all, cot_all = gather_weights(
        attn, gate_up, down, small, place_rows, cot
    )
    w_attn = w_attn.reshape(2, DPAD, 1024)
    qk_full, vo_full = w_attn[0], w_attn[1]
    query_full, key_full = qk_full[:, :896], qk_full[:, 896:]
    value_full, output_full = vo_full[:, :128], vo_full[:, 128:]
    w_gu = w_gu.reshape(DPAD, 1280)
    down_full = down_full.reshape(640, D)
    vectors = small_all.reshape(-1)
    gain_attn, bias_query, gain_mlp = vectors[:896], vectors[896:1792], vectors[1792:2688]
    bias_key, bias_value = vectors[2688:2816], vectors[2816:2944]
    key_places = places_all.reshape(16, 8, 128)[:, :2, :64].transpose(1, 0, 2).reshape(2, 1024)
    query_places = places.astype(F32)

    residual = hidden_in.reshape(rows, D).astype(F32)
    inv_rms = rms_scale(residual)
    unit_in = residual * inv_rms
    normed_in = spread((unit_in * gain_attn).astype(BF16), BF16)
    cosine, sine = rope_tables(places.reshape(rows), HEAD_SIZE)
    query_lin = matrix_product(normed_in, query_full) + bias_query
    key_lin = matrix_product(normed_in, key_full) + bias_key
    value_lin = matrix_product(normed_in, value_full) + bias_value
    queries = apply_rotary(query_lin.reshape(rows, QUERY_HEADS, HEAD_SIZE), cosine, sine).astype(BF16)
    queries = queries.reshape(MB, 64, KEY_VALUE_HEADS, GROUP, HEAD_SIZE)
    keys = apply_rotary(key_lin.reshape(rows, KEY_VALUE_HEADS, HEAD_SIZE), cosine, sine).astype(BF16)
    key_value = jnp.concatenate([keys.reshape(rows, 128), value_lin.astype(BF16)], axis=1).reshape(MB, 64, 256)
    kv_all = gather_ctx(key_value, 2, "gather_kv").transpose(1, 0, 2, 3).reshape(MB, 1024, 256)
    key_all = kv_all[..., :128].reshape(MB, 1024, 2, 64)
    value_all = kv_all[..., 128:].reshape(MB, 1024, 2, 64)
    probs, attended = attend(queries, key_all, value_all, query_places, key_places, factor)
    attended_low = spread(attended.reshape(rows, D).astype(BF16), BF16)
    mixed = residual + matrix_product(attended_low, output_full)
    inv_mid = rms_scale(mixed)
    unit_mid = mixed * inv_mid
    normed_mid = spread((unit_mid * gain_mlp).astype(BF16), BF16)

    normed_all = gather_dp(normed_mid, 3, "gather_rows").reshape(1024, DPAD)
    cot_all = cot_all.reshape(1024, D)
    gu_lin = matrix_product(normed_all, w_gu)
    gate_lin, up_lin = gu_lin[:, :640], gu_lin[:, 640:]
    sigmoid_gate = jax.nn.sigmoid(gate_lin)
    hidden_low = (gate_lin * sigmoid_gate * up_lin).astype(BF16)
    part_out = matrix_product(hidden_low, down_full).astype(BF16)
    branch = reduce_dp(part_out.reshape(4, 2, 128, D), 4, "reduce_out")
    layer_out = (mixed + branch).astype(BF16)

    grad_top = cot.astype(F32)
    grad_down_w = matmul_tn(hidden_low, cot_all)
    hidden_back = matmul_nt(cot_all, down_full).astype(BF16).astype(F32)
    grad_gate = (hidden_back * up_lin * sigmoid_gate * (1.0 + gate_lin * (1.0 - sigmoid_gate))).astype(BF16)
    grad_upward = (hidden_back * gate_lin * sigmoid_gate).astype(BF16)
    grad_gu = jnp.concatenate([grad_gate, grad_upward], axis=1)
    part_normed = matmul_nt(grad_gu, w_gu).astype(BF16)
    grad_normed_mid = unspread(reduce_dp(part_normed.reshape(4, 2, 128, DPAD), 5, "reduce_normed"))
    grad_gu_w = matmul_tn(normed_all, grad_gu)
    grad_gain_mid = jnp.sum(grad_normed_mid * unit_mid, axis=0)
    scaled_mid = grad_normed_mid * gain_mlp
    grad_mixed = grad_top + inv_mid * (
        scaled_mid - unit_mid * jnp.mean(scaled_mid * unit_mid, axis=-1, keepdims=True)
    )
    grad_attn_branch = grad_mixed.astype(BF16)
    grad_output_w = matmul_tn(attended_low, grad_attn_branch)
    attended_gradient = unspread(matmul_nt(grad_attn_branch, output_full).astype(BF16))
    attended_gradient = attended_gradient.reshape(MB, 64, KEY_VALUE_HEADS, GROUP, HEAD_SIZE)
    grad_query_rot, grad_key_part, grad_value_part = attend_back(
        queries, key_all, value_all, probs, attended_gradient, factor
    )
    kv_grad = jnp.concatenate(
        [grad_key_part.reshape(MB, 1024, 128), grad_value_part.reshape(MB, 1024, 128)], axis=-1
    ).astype(BF16)
    kv_grad = kv_grad.reshape(MB, 4, 4, 64, 256).transpose(1, 2, 0, 3, 4)
    kv_sum = reduce_ctx(kv_grad, 6, "reduce_kv").reshape(rows, 256)
    grad_query_low = inverse_rotary(grad_query_rot.reshape(rows, QUERY_HEADS, HEAD_SIZE), cosine, sine)
    grad_query_low = grad_query_low.reshape(rows, D).astype(BF16)
    grad_key_low = inverse_rotary(kv_sum[:, :128].reshape(rows, KEY_VALUE_HEADS, HEAD_SIZE), cosine, sine)
    grad_key_low = grad_key_low.reshape(rows, 128).astype(BF16)
    grad_value_low = kv_sum[:, 128:].astype(BF16)
    grad_qk = jnp.concatenate([grad_query_low, grad_key_low], axis=1)
    grad_qk_w = matmul_tn(normed_in, grad_qk)
    grad_vo_w = jnp.concatenate([matmul_tn(normed_in, grad_value_low), grad_output_w], axis=1)
    grad_normed_in = unspread(matmul_nt(grad_qk, qk_full) + matmul_nt(grad_value_low, value_full))
    scaled_in = grad_normed_in * gain_attn
    grad_in = grad_mixed + inv_rms * (
        scaled_in - unit_in * jnp.mean(scaled_in * unit_in, axis=-1, keepdims=True)
    )
    small_grads = jnp.concatenate(
        [
            jnp.sum(grad_normed_in * unit_in, axis=0),
            jnp.sum(grad_query_low.astype(F32), axis=0),
            grad_gain_mid,
            jnp.sum(grad_key_low.astype(F32), axis=0),
            jnp.sum(grad_value_low.astype(F32), axis=0),
            jnp.zeros((128,), F32),
        ]
    ).reshape(24, 128)
    o_attn, o_gu, o_down, o_small = reduce_grads(
        jnp.stack([grad_qk_w, grad_vo_w]).astype(BF16).reshape(2, 4, 4, 2, 32, 1024),
        grad_gu_w.astype(BF16).reshape(4, 4, 2, 32, 1280),
        grad_down_w.astype(BF16).reshape(4, 160, D),
        small_grads,
    )

    def joined(parts):
        return parts[:, :7].reshape(8, 7, 16, 40)[..., :38].transpose(1, 0, 2, 3).reshape(7, 4864)

    sums = o_small.reshape(-1)

    def take(start, width):
        return lax.dynamic_slice(sums, (start + me * width,), (width,))

    return (
        layer_out.reshape(MB, 1, 64, D),
        grad_in.reshape(MB, 1, 64, D),
        take(0, 7),
        o_attn[0, :7, :896],
        take(896, 7),
        o_attn[0, :7, 896:],
        sums[2688:2816],
        o_attn[1, :7, :128],
        take(2816, 1),
        o_attn[1, :7, 128:],
        take(1792, 7),
        joined(o_gu[..., :640]),
        joined(o_gu[..., 640:]),
        o_down[:38],
    )


def solution(mesh):
    rows = P(("dp", "ctx"), None)
    vector = P(("dp", "ctx"))
    tokens = P(None, "dp", "ctx", None)
    in_specs = (
        tokens, P(None, "dp", "ctx"), vector, rows, vector, rows, vector, rows, vector, rows, vector,
        rows, rows, rows, tokens,
    )
    out_specs = (
        tokens, tokens, vector, rows, vector, rows, P(), rows, vector, rows, vector, rows, rows, rows,
    )
    return jax.shard_map(body, mesh=mesh, in_specs=in_specs, out_specs=out_specs, check_vma=False)
```

time: 1940 us -> 377 us (0.19)
  blocking collectives: 1180 us -> 0 us
  starting transfers between devices: 241 us -> 0 us
  Pallas kernels: 0 us -> 220 us
  local copies, waits for them, and re-layouts: 253 us -> 67.2 us
  matrix products: 166 us -> 52.5 us
  waiting for transfers between devices: 39 us -> 0 us
    unnamed x5 -> x0, blocking collectives: 983 us -> none
    unnamed x62 -> x0, starting transfers between devices: 241 us -> none
    pallas_call x0 -> x7, Pallas kernels: none -> 220 us  [comm_call(): pl.pallas_call(kernel, out_shape=outs, in_specs=[pl.BlockSpec(memory_spac...]
    unnamed x340 -> x138, local copies, waits for them, and re-layouts: 227 us -> 9.26 us
    all_gather x6 -> x0, blocking collectives: 197 us -> none  [the longest x1 60.5 us: body(): lax.all_gather(value_weight, ('dp', 'ctx'), axis=0, tiled=True)]
    dot_general x14 -> x5, matrix products: 69.7 us -> 8.79 us  [matmul_tn(): lax.dot_general(left, right, (((0,), (0,)), ((), ())), preferred_element_...]
    unnamed x72 -> x0, waiting for transfers between devices: 38.9 us -> none
    dot_general x26 -> x11, matrix products: 56.7 us -> 26.9 us  [the longest x6 13.6 us: matrix_product(): return jnp.dot(left, right, preferred_element_type=F32)]
  transfers between devices with their start and end apart: 69 -> 0, of which waited for: 5 -> 0; matrix products, arithmetic and copies ran while one was open for 36% -> 0% of each run, Pallas kernels for 0% -> 0%
where the time goes in v1:
time: 377 us; the launch traced here: 371 us
  Pallas kernels  220 us (58%)
  local copies, waits for them, and re-layouts  67.2 us (18%)
  matrix products  52.5 us (14%)
  other arithmetic  26.8 us (7%)
  between operations  3.91 us (1%)
    pallas_call x7, Pallas kernels, comm_call(): pl.pallas_call(kernel, out_shape=outs, in_specs=[pl.BlockSpec(memory_spac...  220 us
    dot_general x6, matrix products, matrix_product(): return jnp.dot(left, right, preferred_element_type=F32)  13.6 us
    dot_general x5, matrix products, matmul_nt(): lax.dot_general(left, right, (((1,), (1,)), ((), ())), preferred_element_...  10.5 us
    unnamed x138, local copies, waits for them, and re-layouts  9.26 us
    dot_general x5, matrix products, matmul_tn(): lax.dot_general(left, right, (((0,), (0,)), ((), ())), preferred_element_...  8.79 us

profile of v1, /device:TPU:1, one launch (start us, length us, event | category | flops | bytes accessed | tf_op | source)
XLA Modules:
  0.0 370.5 jit_solution(9396074241644758087)
XLA Ops:
  2.2 1.5 reshape.434
  4.0 1.5 reshape.432
  10.3 72.7 %gather_weights.1 = (bf16[2,16,2,32,1024]{4,3,2,1,0:T(8,128)(2,1)}, bf16[16,2,32,1280]{3,2,1,0:T(8,128)(2,1)}, bf16[4,160,896]{2,1,0:T(8,128)(2,1)}, f32[24,128]...) custom-call(f32[2,8,1024]{2,1,0:T(8,128)} %fusion.66.attn, ...), custom_call_target="tpu_custom_call" | custom-call | tf_op jit(solution)/shard_map/gather_weights/pallas_call | solution.py:274
  86.7 2.7 fusion.75
  89.4 1.3 copy-done.4
  93.0 12.8 %gather_kv.1 = bf16[16,2,64,256]{3,2,1,0:T(8,128)(2,1)} custom-call(bf16[2,64,256]{2,1,0:T(8,128)(2,1)} %pad_maximum_fusion.9.src), custom_call_target="tpu_custom_call" | custom-call | tf_op jit(solution)/shard_map/gather_kv/pallas_call | solution.py:274
  105.8 1.3 copy.52
  108.3 1.2 copy.53
  111.3 2.0 copy.55
  113.4 1.3 fusion.27
  114.7 1.2 copy.56
  119.1 1.8 fusion.35
  120.9 6.3 %fusion.81 = (f32[2,2,7,64]{3,2,1,0:T(8,128)S(1)}, f32[2,2,7,64,1024]{4,3,2,1,0:T(8,128)}) fusion(pred[2,64,1024]{2,1,0:T(8,128)(4,1)} %broadcast_compare_fusion, bf16[2,1024,2,64,1]{1,3,4,2,0:T(8,128)(2,1)S(1)} %bitcast.274, bf16[2,64,2,7,64]{1,0,4,3,2:T(2,128)(2,1)S(1)} %fusion.35), kind=kOutput, calls=%fused_computation.186 | convolution fusion | flops 242222080 | bytes 8231936 | tf_op jit(solution)/shard_map/sub | solution.py:659
  127.2 4.0 %divide_convert_fusion = bf16[2,2,7,64,1024]{4,3,2,1,0:T(8,128)(2,1)S(1)} fusion(f32[2,2,7,64,1024]{4,3,2,1,0:T(8,128)} %get-tuple-element.107, f32[2,2,7,64]{3,2,1,0:T(8,128)S(1)} %get-tuple-element.106), kind=kLoop, calls=%fused_computation.7 | loop fusion | flops 3670016 | bytes 11017216 | tf_op jit(solution)/shard_map/convert_element_type | solution.py:660
  131.2 1.9 copy-done
  133.1 1.6 fusion.23
  135.6 1.7 multiply_reduce_fusion.4
  141.8 1.8 copy.65.src
  143.6 20.2 %gather_rows.1 = bf16[8,128,1024]{2,1,0:T(8,128)(2,1)} custom-call(bf16[128,1024]{1,0:T(8,128)(2,1)} %copy.65.src), custom_call_target="tpu_custom_call" | custom-call | tf_op jit(solution)/shard_map/gather_rows/pallas_call | solution.py:274
  163.8 5.4 %fusion.86 = f32[1024,1280]{1,0:T(8,128)S(1)} fusion(bf16[1024,1024]{1,0:T(8,128)(2,1)} %bitcast.276, bf16[1024,1280]{1,0:T(8,128)(2,1)} %bitcast.310), kind=kOutput, calls=%fused_computation.187 | convolution fusion | flops 2684354560 | bytes 9961472 | tf_op jit(solution)/shard_map/dot_general | solution.py:619
  169.2 3.6 fusion.9
  172.8 4.2 %convolution_convert_fusion.1 = bf16[1024,1024]{1,0:T(8,128)(2,1)} fusion(bf16[1024,1280]{1,0:T(8,128)(2,1)S(1)} %bitcast.311, bf16[1024,640]{1,0:T(8,128)(2,1)S(1)} %get-tuple-element.69, bf16[1024,640]{1,0:T(8,128)(2,1)S(1)} %get-tuple-element.68), kind=kOutput, calls=%fused_computation.27 | convolution fusion | flops 2690646016 | bytes 7340032 | tf_op jit(solution)/shard_map/dot_general | solution.py:627
  177.0 19.3 %reduce_normed.1 = f32[128,1024]{1,0:T(8,128)} custom-call(bf16[4,2,128,1024]{3,2,1,0:T(8,128)(2,1)} %bitcast.273), custom_call_target="tpu_custom_call" | custom-call | tf_op jit(solution)/shard_map/reduce_normed/pallas_call | solution.py:274
  196.3 1.2 copy.67
  200.4 4.7 %convolution_convert_fusion.3 = bf16[1024,896]{1,0:T(8,128)(2,1)} fusion(bf16[1024,640]{1,0:T(8,128)(2,1)} %get-tuple-element.70, bf16[640,896]{1,0:T(8,128)(2,1)} %bitcast.314), kind=kOutput, calls=%fused_computation.31 | convolution fusion | flops 1175322624 | bytes 4292608 | tf_op jit(solution)/shard_map/dot_general | solution.py:619
  205.2 18.2 %reduce_out.1 = f32[128,896]{1,0:T(8,128)} custom-call(bf16[4,2,128,896]{3,2,1,0:T(8,128)(2,1)} %bitcast.282), custom_call_target="tpu_custom_call" | custom-call | tf_op jit(solution)/shard_map/reduce_out/pallas_call | solution.py:274
  223.4 2.1 multiply_add_fusion
  226.7 3.0 fusion.21
  229.7 1.7 reshape.491
  231.4 2.7 copy.83
  234.0 3.7 %fusion.1 = (f32[2,2,7,64]{3,2,1,0:T(8,128)S(1)}, f32[2,2,1024,64,7]{2,3,4,1,0:T(8,128)S(1)}) fusion(bf16[2,2,7,64,1024]{4,3,2,1,0:T(8,128)(2,1)} %copy-done, bf16[2,1024,2,64,1]{1,3,4,2,0:T(8,128)(2,1)} %bitcast.264, bf16[2,64,2,7,64]{1,0,4,3,2:T(2,128)(2,1)} %copy-done.10), kind=kOutput, calls=%fused_computation.3 | convolution fusion | flops 240384256 | bytes 11770880 | tf_op jit(solution)/shard_map/bqghd,bkgd->bghqk/dot_general | solution.py:665
  237.8 1.3 fusion.2
  239.1 1.8 copy-done.1
  244.4 14.8 %reduce_kv.1 = f32[2,64,256]{2,1,0:T(8,128)} custom-call(bf16[4,4,2,64,256]{4,3,2,1,0:T(8,128)(2,1)} %maximum_bitcast_fusion.src), custom_call_target="tpu_custom_call" | custom-call | tf_op jit(solution)/shard_map/reduce_kv/pallas_call | solution.py:274
  260.3 1.5 convert_reduce_fusion.2
  261.8 4.1 %broadcast_multiply_fusion = (f32[2,64,2,7,64]{4,1,3,2,0:T(8,128)S(1)}, f32[2,64,2,7,64]{4,1,3,2,0:T(8,128)}) fusion(bf16[2,1024,2,64,1]{1,3,4,2,0:T(8,128)(2,1)S(1)} %bitcast.275, bf16[2,2,7,64,1024]{4,3,2,1,0:T(8,128)(2,1)} %copy-done.1), kind=kOutput, calls=%fused_computation.79 | convolution fusion | flops 234995712 | bytes 5111808 | tf_op jit(solution)/shard_map/bghqk,bkgd->bqghd/dot_general | solution.py:669
  270.1 1.2 add_convert_fusion
  272.2 1.2 convolution_add_fusion
  274.6 1.2 copy.89
  279.0 2.6 copy.90
  283.1 2.5 pad_maximum_fusion.g_attn
  287.0 4.5 %convolution_convert_fusion = bf16[1024,1280]{1,0:T(8,128)(2,1)} fusion(bf16[1024,1024]{1,0:T(8,128)(2,1)S(1)} %bitcast.277, bf16[1024,640]{1,0:T(8,128)(2,1)S(1)} %copy-done.59, bf16[1024,640]{1,0:T(8,128)(2,1)S(1)} %copy-done.57), kind=kOutput, calls=%fused_computation.11 | convolution fusion | flops 2690908160 | bytes 7340032 | tf_op jit(solution)/shard_map/dot_general | solution.py:623
  291.5 2.7 convolution_convert_fusion.5
  296.9 62.2 %reduce_grads.1 = (f32[2,8,1024]{2,1,0:T(8,128)}, f32[8,8,1280]{2,1,0:T(8,128)}, f32[40,896]{1,0:T(8,128)}, f32[24,128]{1,0:T(8,128)}) custom-call(bf16[2,4,4,2,32,1024]{5,4,3,2,1,0:T(8,128)(2,1)} %pad_maximum_fusion.g_attn, bf16[4,4,2,32,1280]{4,3,2,1,0:T(8,128)(2,1)} %bitcast.270, bf16[4,160,896]{2,1,0:T(8,128)(2,1)} %bitcast.287, f32[24,128]{1,0:T(8,128)} %bitcast.305), custom_call_target="tpu_custom_call" | custom-call | tf_op jit(solution)/shard_map/reduce_grads/pallas_call | solution.py:274
  359.1 1.4 fusion.80
  360.5 1.4 slice_bitcast_fusion.4
  361.9 1.3 slice_bitcast_fusion.6
  364.4 1.3 dynamic_slice.14
  (276 shorter events, 51.3 us)
Async XLA Ops:
  0.6 5.9 %copy-start.39 = (bf16[38,896]{1,0:T(8,128)(2,1)S(1)}, bf16[38,896]{1,0:T(8,128)(2,1)}, u32[]{:S(2)}) copy-start(bf16[38,896]{1,0:T(8,128)(2,1)} %param.28) | copy-start | bytes 204292
  0.7 6.5 %copy-start.53 = (bf16[7]{0:T(256)(128)(2,1)S(1)}, bf16[7]{0:T(256)(128)(2,1)}, u32[]{:S(2)}) copy-start(bf16[7]{0:T(256)(128)(2,1)} %param.17) | copy-start | bytes 46
  0.7 6.8 %copy-start.54 = (bf16[7]{0:T(256)(128)(2,1)S(1)}, bf16[7]{0:T(256)(128)(2,1)}, u32[]{:S(2)}) copy-start(bf16[7]{0:T(256)(128)(2,1)} %param.19) | copy-start | bytes 46
  0.7 7.1 %copy-start.55 = (bf16[7]{0:T(256)(128)(2,1)S(1)}, bf16[7]{0:T(256)(128)(2,1)}, u32[]{:S(2)}) copy-start(bf16[7]{0:T(256)(128)(2,1)} %param.25) | copy-start | bytes 46
  0.7 8.9 %copy-start.48 = (s32[2,1,64]{2,1,0:T(1,128)S(1)}, s32[2,1,64]{2,1,0:T(1,128)}, u32[]{:S(2)}) copy-start(s32[2,1,64]{2,1,0:T(1,128)} %param.16) | copy-start | bytes 1540
  0.7 82.4 %copy-start.15 = (bf16[2,1,64,896]{3,2,1,0:T(8,128)(2,1)S(1)}, bf16[2,1,64,896]{3,2,1,0:T(8,128)(2,1)}, u32[]{:S(2)}) copy-start(bf16[2,1,64,896]{3,2,1,0:T(8,128)(2,1)} %param.15) | copy-start | bytes 688132
  83.1 2.2 copy-start.43
  86.3 3.1 copy-start.46
  89.4 24.0 %copy-start.2 = (bf16[1,16,2,32,1024]{4,3,2,1,0:T(8,128)(2,1)}, bf16[1,16,2,32,1024]{4,3,2,1,0:T(8,128)(2,1)S(1)}, u32[]{:S(2)}) copy-start(bf16[1,16,2,32,1024]{4,3,2,1,0:T(8,128)(2,1)S(1)} %get-tuple-element.71) | copy-start | bytes 6291460
  109.5 21.6 %copy-start.7 = (bf16[2,1024,128]{1,2,0:T(8,128)(2,1)}, bf16[2,1024,128]{1,2,0:T(8,128)(2,1)S(1)}, u32[]{:S(2)}) copy-start(bf16[2,1024,128]{1,2,0:T(8,128)(2,1)S(1)} %copy.53) | copy-start | bytes 1572868
  116.2 4.7 %copy-start.19 = (bf16[2,1024,128]{1,2,0:T(8,128)(2,1)S(1)}, bf16[2,1024,128]{1,2,0:T(8,128)(2,1)}, u32[]{:S(2)}) copy-start(bf16[2,1024,128]{1,2,0:T(8,128)(2,1)} %copy.55) | copy-start | bytes 1572868
  120.9 6.3 %copy-start.27 = (bf16[2,64,2,7,64]{1,0,4,3,2:T(2,128)(2,1)}, bf16[2,64,2,7,64]{1,0,4,3,2:T(2,128)(2,1)S(1)}, u32[]{:S(2)}) copy-start(bf16[2,64,2,7,64]{1,0,4,3,2:T(2,128)(2,1)S(1)} %fusion.35) | copy-start | bytes 688132
  133.1 2.5 copy-start.5
  135.2 2.1 copy-start.40
  135.6 6.2 %copy-start.17 = (bf16[128,16,8,8]{0,3,2,1:T(8,128)(2,1)}, bf16[128,16,8,8]{0,3,2,1:T(8,128)(2,1)S(1)}, u32[]{:S(2)}) copy-start(bf16[128,16,8,8]{0,3,2,1:T(8,128)(2,1)S(1)} %copy.62) | copy-start | bytes 786436
  163.8 5.4 %copy-start.50 = (bf16[8,128,896]{2,1,0:T(8,128)(2,1)S(1)}, bf16[8,128,896]{2,1,0:T(8,128)(2,1)}, u32[]{:S(2)}) copy-start(bf16[8,128,896]{2,1,0:T(8,128)(2,1)} %get-tuple-element.29) | copy-start | bytes 5505028
  163.8 5.4 %copy-start.52 = (bf16[4,160,896]{2,1,0:T(8,128)(2,1)S(1)}, bf16[4,160,896]{2,1,0:T(8,128)(2,1)}, u32[]{:S(2)}) copy-start(bf16[4,160,896]{2,1,0:T(8,128)(2,1)} %get-tuple-element.28) | copy-start | bytes 3440644
  169.2 3.6 copy-start.49
  172.8 4.2 %copy-start.56 = (bf16[1024,640]{1,0:T(8,128)(2,1)}, bf16[1024,640]{1,0:T(8,128)(2,1)S(1)}, u32[]{:S(2)}) copy-start(bf16[1024,640]{1,0:T(8,128)(2,1)S(1)} %get-tuple-element.68) | copy-start | bytes 3932164
  172.8 4.2 %copy-start.58 = (bf16[1024,640]{1,0:T(8,128)(2,1)}, bf16[1024,640]{1,0:T(8,128)(2,1)S(1)}, u32[]{:S(2)}) copy-start(bf16[1024,640]{1,0:T(8,128)(2,1)S(1)} %get-tuple-element.69) | copy-start | bytes 3932164
  199.6 5.5 %copy-start.13 = (f32[128,896]{1,0:T(8,128)}, f32[128,896]{1,0:T(8,128)S(1)}, u32[]{:S(2)}) copy-start(f32[128,896]{1,0:T(8,128)S(1)} %copy.69) | copy-start | bytes 1376260
  200.4 23.0 %copy-start.30 = (bf16[2,1,64,896]{3,2,1,0:T(8,128)(2,1)S(1)}, bf16[2,1,64,896]{3,2,1,0:T(8,128)(2,1)}, u32[]{:S(2)}) copy-start(bf16[2,1,64,896]{3,2,1,0:T(8,128)(2,1)} %param.29) | copy-start | bytes 688132
  225.4 4.2 %copy-start.11 = (f32[128,896]{1,0:T(8,128)}, f32[128,896]{1,0:T(8,128)S(1)}, u32[]{:S(2)}) copy-start(f32[128,896]{1,0:T(8,128)S(1)} %get-tuple-element.77) | copy-start | bytes 1376260
  226.7 3.0 copy-start.10
  231.4 6.4 %slice-start = ((s8[7340032]{0:T(1024)(128)(4,1)}), s8[3145728]{0:T(1024)(128)(4,1)S(1)}, s32[]{:S(2)}) async-start(s8[7340032]{0:T(1024)(128)(4,1)} %bitcast.248), calls=%async_computation | async-start | bytes 6291456
  234.0 3.8 %slice-start.1 = ((s8[7340032]{0:T(1024)(128)(4,1)}), s8[4194304]{0:T(1024)(128)(4,1)S(1)}, s32[]{:S(2)}) async-start(s8[7340032]{0:T(1024)(128)(4,1)} %bitcast.248), calls=%async_computation.1 | async-start | bytes 8388608
  237.8 3.1 copy-start.28
  242.4 17.7 %copy-start.32 = (f32[128,64]{0,1:T(8,128)S(1)}, f32[128,64]{0,1:T(8,128)}, u32[]{:S(2)}) copy-start(f32[128,64]{0,1:T(8,128)} %copy-done.31) | copy-start | bytes 98308
  242.4 19.4 %copy-start.20 = (bf16[2,1024,128]{1,2,0:T(8,128)(2,1)S(1)}, bf16[2,1024,128]{1,2,0:T(8,128)(2,1)}, u32[]{:S(2)}) copy-start(bf16[2,1024,128]{1,2,0:T(8,128)(2,1)} %copy.55) | copy-start | bytes 1572868
  267.1 2.7 copy-start.35
  268.7 2.6 copy-start.3
  268.7 2.6 copy-start.33
  269.9 2.3 copy-start.29
  272.2 3.6 copy-start.9
  272.2 3.6 copy-start.47
  273.5 3.4 copy-start.12
  273.5 3.4 copy-start.16
  273.5 3.3 copy-start.41
  273.7 4.1 %copy-start.18 = (bf16[128,16,8,8]{0,3,2,1:T(8,128)(2,1)S(1)}, bf16[128,16,8,8]{0,3,2,1:T(8,128)(2,1)}, u32[]{:S(2)}) copy-start(bf16[128,16,8,8]{0,3,2,1:T(8,128)(2,1)} %copy-done.17) | copy-start | bytes 786436
  283.1 2.5 copy-start.21
  283.1 3.5 copy-start.57
  283.1 3.9 %copy-start.59 = (bf16[1024,640]{1,0:T(8,128)(2,1)S(1)}, bf16[1024,640]{1,0:T(8,128)(2,1)}, u32[]{:S(2)}) copy-start(bf16[1024,640]{1,0:T(8,128)(2,1)} %copy-done.58) | copy-start | bytes 3932164
  287.0 4.5 %copy-start.51 = (bf16[8,128,896]{2,1,0:T(8,128)(2,1)S(1)}, bf16[8,128,896]{2,1,0:T(8,128)(2,1)}, u32[]{:S(2)}) copy-start(bf16[8,128,896]{2,1,0:T(8,128)(2,1)} %get-tuple-element.29) | copy-start | bytes 5505028
  287.0 4.5 %copy-start.60 = (bf16[1024,640]{1,0:T(8,128)(2,1)S(1)}, bf16[1024,640]{1,0:T(8,128)(2,1)}, u32[]{:S(2)}) copy-start(bf16[1024,640]{1,0:T(8,128)(2,1)} %get-tuple-element.70) | copy-start | bytes 3932164
  291.5 2.7 copy-start.37
  291.5 2.9 copy-start.26
  291.5 3.5 copy-start.24
  365.6 3.8 %copy-start.38 = (f32[40,896]{1,0:T(8,128)S(1)}, f32[40,896]{1,0:T(8,128)}, u32[]{:S(2)}) copy-start(f32[40,896]{1,0:T(8,128)} %get-tuple-element.33) | copy-start | bytes 430084
  (15 other events, 18.5 us)

commit v2 on v1

v2 whole, which is shorter than its diff:
```python
import types

import jax
import jax.numpy as jnp
from jax import lax
from jax.experimental import pallas as pl
from jax.experimental.pallas import tpu as pltpu
from jax.sharding import PartitionSpec as P

QUERY_HEADS = 14
KEY_VALUE_HEADS = 2
HEAD_SIZE = 64
GROUP = QUERY_HEADS // KEY_VALUE_HEADS
MB = 2
D = 896
DPAD = 1024
EPSILON = 1e-06
THETA_BASE = 1000000.0
F32 = jnp.float32
BF16 = jnp.bfloat16
MESH = pl.DeviceIdType.MESH
DMA = pltpu.SemaphoreType.DMA
VM = pltpu.VMEM


def remote(src, dst, ss, rs, peer):
    return pltpu.make_async_remote_copy(
        src_ref=src, dst_ref=dst, send_sem=ss, recv_sem=rs, device_id=peer, device_id_type=MESH
    )


def barrier(peers):
    sem = pltpu.get_barrier_semaphore()
    for peer in peers:
        pl.semaphore_signal(sem, inc=1, device_id=peer, device_id_type=MESH)
    pl.semaphore_wait(sem, len(peers))


class Place:
    def __init__(self):
        self.dp = lax.axis_index("dp")
        self.ctx = lax.axis_index("ctx")
        self.y, self.x = self.ctx // 4, lax.rem(self.ctx, 4)
        self.z, self.core = self.dp // 2, lax.rem(self.dp, 2)

    def at_x(self, k):
        return lax.rem(self.x + (k + 4), 4)

    def at_y(self, k):
        return lax.rem(self.y + (k + 4), 4)

    def at_z(self, k):
        return lax.rem(self.z + (k + 4), 4)

    def line(self, axis, k):
        return self.y * 4 + self.at_x(k) if axis == 0 else self.at_y(k) * 4 + self.x

    def xpeer(self, k):
        return {"ctx": self.line(0, k)}

    def ypeer(self, k):
        return {"ctx": self.line(1, k)}

    def peer(self, axis, k):
        return {"ctx": self.line(axis, k)}

    def zindex(self, k):
        return self.at_z(k) * 2 + self.core

    def mate(self):
        return self.z * 2 + 1 - self.core

    def dpindex(self, k):
        return lax.rem(self.dp + k, 8)


NEAR = (1, 3, 2)


class GatherCtx:
    SEMS = [DMA((2, 4)), DMA((2, 4)), DMA((2, 4, 4)), DMA((2, 4, 4)), DMA]
    MATE = [DMA((2, 4, 4)), DMA((2, 4, 4))]

    def __init__(self, place, src, dst, sems, mate=None):
        self.p, self.src, self.dst, self.sems, self.mate = place, src, dst, sems, mate
        self.mated = []

    def block(self, h, j, k):
        p = self.p
        return p.at_y(-k) * 4 + p.at_x(-j) if h == 0 else p.at_y(-j) * 4 + p.at_x(-k)

    def share(self, h, j, k):
        if self.mate is None:
            return
        src = self.src.at[h] if j == 0 and k == 0 else self.dst.at[self.block(h, j, k), h]
        dst = self.dst.at[self.block(h, j, k), h]
        c = remote(src, dst, self.mate[0].at[h, j, k], self.mate[1].at[h, j, k], {"dp": self.p.mate()})
        c.start()
        self.mated.append(c)

    def start(self):
        p, (s1, r1, s2, r2, ls) = self.p, self.sems
        self.local = pltpu.make_async_copy(self.src, self.dst.at[p.ctx], ls)
        self.local.start()
        self.first = {}
        for k in NEAR:
            for h in (0, 1):
                c = remote(self.src.at[h], self.dst.at[p.ctx, h], s1.at[h, k], r1.at[h, k], p.peer(h, k))
                c.start()
                self.first[h, k] = c
        for h in (0, 1):
            self.share(h, 0, 0)

    def forward(self):
        p, (s1, r1, s2, r2, ls) = self.p, self.sems
        self.second = {}
        for j in (0,) + NEAR:
            for h in (0, 1):
                if j:
                    self.first[h, j].wait_recv()
                block = p.line(h, -j)
                for k in NEAR:
                    src = self.src.at[h] if j == 0 else self.dst.at[block, h]
                    c = remote(src, self.dst.at[block, h], s2.at[h, j, k], r2.at[h, j, k], p.peer(1 - h, k))
                    c.start()
                    self.second[h, j, k] = c
                if j:
                    self.share(h, j, 0)

    def arrive(self):
        self.local.wait()
        for (h, j, k), c in self.second.items():
            c.wait_recv()
            self.share(h, j, k)
        for c in self.mated:
            c.wait_recv()

    def finish(self):
        for c in list(self.first.values()) + list(self.second.values()) + self.mated:
            c.wait_send()


class ReduceCtx:
    SEMS = [DMA((2, 4)), DMA((2, 4)), DMA((2, 4)), DMA((2, 4))]

    @staticmethod
    def scratch(rows, cols):
        return [VM((2, 3, 4, rows, cols), BF16), VM((2, 4, rows, cols), BF16), VM((2, 3, rows, cols), BF16)]

    def __init__(self, place, src, bufs, sems):
        self.p, self.src, self.bufs, self.sems = place, src, bufs, sems

    def start(self):
        p, (s1, r1, s2, r2) = self.p, self.sems
        got = self.bufs[0]
        self.first = {}
        for k in NEAR:
            for h in (0, 1):
                src = self.src.at[p.at_y(k), :, 0] if h == 0 else self.src.at[:, p.at_x(k), 1]
                c = remote(src, got.at[h, k - 1], s1.at[h, k], r1.at[h, k], p.peer(1 - h, k))
                c.start()
                self.first[h, k] = c

    def forward(self):
        p, (s1, r1, s2, r2) = self.p, self.sems
        got, mid, last = self.bufs
        self.second = {}
        for h in (0, 1):
            for k in NEAR:
                self.first[h, k].wait_recv()
            for i in range(4):
                own = self.src[p.y, i, 0] if h == 0 else self.src[i, p.x, 1]
                total = own.astype(F32)
                for k in NEAR:
                    total = total + got[h, k - 1, i].astype(F32)
                mid[h, i] = total.astype(BF16)
            for k in NEAR:
                to = p.at_x(k) if h == 0 else p.at_y(k)
                c = remote(mid.at[h, to], last.at[h, k - 1], s2.at[h, k], r2.at[h, k], p.peer(h, k))
                c.start()
                self.second[h, k] = c

    def result(self, h):
        p = self.p
        got, mid, last = self.bufs
        for k in NEAR:
            self.second[h, k].wait_recv()
        total = mid[h, p.x if h == 0 else p.y].astype(F32)
        for k in NEAR:
            total = total + last[h, k - 1].astype(F32)
        return total

    def finish(self):
        for c in list(self.first.values()) + list(self.second.values()):
            c.wait_send()


class GatherDp:
    SEMS = [DMA((4,)), DMA((4,)), DMA((4,)), DMA((4,)), DMA]

    def __init__(self, place, src, dst, sems):
        self.p, self.src, self.dst, self.sems = place, src, dst, sems

    def start(self):
        p, (s1, r1, s2, r2, ls) = self.p, self.sems
        self.local = pltpu.make_async_copy(self.src, self.dst.at[p.dp], ls)
        self.local.start()
        self.first = {}
        for k in NEAR:
            c = remote(self.src, self.dst.at[p.dp], s1.at[k], r1.at[k], {"dp": p.zindex(k)})
            c.start()
            self.first[k] = c

    def forward(self):
        p, (s1, r1, s2, r2, ls) = self.p, self.sems
        self.second = []
        for j in (0,) + NEAR:
            if j:
                self.first[j].wait_recv()
            block = p.zindex(-j)
            src = self.src if j == 0 else self.dst.at[block]
            c = remote(src, self.dst.at[block], s2.at[j], r2.at[j], {"dp": p.mate()})
            c.start()
            self.second.append(c)

    def arrive(self):
        self.local.wait()
        for c in self.second:
            c.wait_recv()

    def finish(self):
        for c in list(self.first.values()) + self.second:
            c.wait_send()


class ReduceDp:
    SEMS = [DMA((4,)), DMA((4,)), DMA((4,)), DMA((4,))]

    @staticmethod
    def scratch(rows, cols):
        return [VM((4, rows, cols), BF16), VM((4, rows, cols), BF16), VM((3, rows, cols), BF16)]

    def __init__(self, place, src, bufs, sems):
        self.p, self.src, self.bufs, self.sems = place, src, bufs, sems

    def copy(self, to, k):
        p, (s1, r1, s2, r2) = self.p, self.sems
        return remote(self.src.at[to, 1 - p.core], self.bufs[0].at[to], s1.at[k], r1.at[k], {"dp": p.mate()})

    def send(self, i):
        to = lax.rem(self.p.z + 1 + i, 4)
        self.copy(to, lax.rem(1 + i, 4)).start()

    def forward(self):
        p, (s1, r1, s2, r2) = self.p, self.sems
        got, mid, last = self.bufs
        self.second = {}
        for k in (1, 2, 3, 0):
            to = p.at_z(k)
            self.copy(to, k).wait_recv()
            total = self.src[to, p.core].astype(F32) + got[to].astype(F32)
            mid[to] = total.astype(BF16)
            if k:
                c = remote(mid.at[to], last.at[k - 1], s2.at[k], r2.at[k], {"dp": p.zindex(k)})
                c.start()
                self.second[k] = c

    def result(self):
        got, mid, last = self.bufs
        total = mid[self.p.z].astype(F32)
        for k in NEAR:
            self.second[k].wait_recv()
            total = total + last[k - 1].astype(F32)
        return total

    def sent(self):
        for k in range(4):
            self.copy(self.p.at_z(k), k).wait_send()

    def finish(self):
        for c in self.second.values():
            c.wait_send()


def xy_peers(p):
    return [p.peer(axis, k) for axis in (0, 1) for k in NEAR]


def dp_peers(p):
    return [{"dp": p.dpindex(k)} for k in range(1, 8)]


def shape(dims, kind):
    return jax.ShapeDtypeStruct(dims, kind)


def call(phase, inputs, outs, scratch, cid, name):
    flat, where = [], {}
    for key, entry in scratch.items():
        entries = entry if isinstance(entry, list) else [entry]
        where[key] = (len(flat), len(entries), isinstance(entry, list))
        flat += entries

    def kernel(*refs):
        named = dict(zip(list(inputs) + list(outs), refs))
        tail = refs[len(inputs) + len(outs) :]
        for key, (start, count, many) in where.items():
            named[key] = list(tail[start : start + count]) if many else tail[start]
        phase(types.SimpleNamespace(**named))

    results = pl.pallas_call(
        kernel,
        out_shape=tuple(outs.values()),
        in_specs=[pl.BlockSpec(memory_space=VM)] * len(inputs),
        out_specs=tuple(pl.BlockSpec(memory_space=VM) for _ in outs),
        scratch_shapes=flat,
        name=name,
        compiler_params=pltpu.CompilerParams(
            collective_id=cid, has_side_effects=True, vmem_limit_bytes=60 << 20
        ),
    )(*inputs.values())
    return dict(zip(outs, results))


def dot(left, right):
    return jnp.dot(left, right, preferred_element_type=F32)


def dot_tn(left, right):
    return lax.dot_general(left, right, (((0,), (0,)), ((), ())), preferred_element_type=F32)


def dot_nt(left, right):
    return lax.dot_general(left, right, (((1,), (1,)), ((), ())), preferred_element_type=F32)


def rms_scale(values):
    return lax.rsqrt(jnp.mean(values * values, axis=-1, keepdims=True) + EPSILON)


def row_vector(ref, start):
    return jnp.concatenate([ref[start + i : start + i + 1, :] for i in range(7)], axis=1)


def store_rows(ref, start, vector):
    for i in range(vector.shape[1] // 128):
        ref[start + i : start + i + 1, :] = vector[:, 128 * i : 128 * i + 128]


def build_spread(ref):
    for part in range(7):
        source = lax.broadcasted_iota(jnp.int32, (128, DPAD), 0) + 128 * part
        column = lax.broadcasted_iota(jnp.int32, (128, DPAD), 1)
        inner = column & 7
        wanted = (((column >> 3) & 7) * 16 + (column >> 6)) * 7 + inner
        ref[128 * part : 128 * part + 128, :] = jnp.where(
            (source == wanted) & (inner < 7), 1.0, 0.0
        ).astype(BF16)


def spread(values, matrix):
    return dot(values, matrix).astype(BF16)


def unspread(values, matrix):
    high = values.astype(BF16)
    low = (values - high.astype(F32)).astype(BF16)
    return dot_nt(high, matrix) + dot_nt(low, matrix)


def lanes(rows):
    return lax.broadcasted_iota(jnp.int32, (rows, 128), 1)


def half_turn(tile):
    first = (lanes(tile.shape[0]) & 63) < 32
    return jnp.where(first, pltpu.roll(tile, 96, 1), pltpu.roll(tile, 32, 1))


def rotate(tile, cosine, signed_sine):
    return tile * cosine + half_turn(tile) * signed_sine


def rotate_back(tile, cosine, signed_sine):
    return tile * cosine - half_turn(tile) * signed_sine


def scatter_heads(tile_of, dst):
    for mb in range(MB):
        for head in range(QUERY_HEADS):
            tile = tile_of(mb, head // 2)
            group = head // GROUP
            if head % 2 != group:
                tile = pltpu.roll(tile, 64, 1)
            tile = jnp.where((lanes(64) >= 64) == (group == 1), tile, 0.0)
            at = (head % 2) * 64
            dst[mb * 7 + head // 2, at : at + 64, :] = tile.astype(BF16)


def collect_heads(transposed, t):
    both = jnp.transpose(transposed)
    even, odd = both[:64], both[64:]
    even = jnp.where(t >= 4, pltpu.roll(even, 64, 1), even)
    odd = jnp.where(t <= 2, pltpu.roll(odd, 64, 1), odd)
    return jnp.where(lanes(64) < 64, even, odd)


def start_all(copies):
    for c in copies:
        c.start()
    return copies


def arrive_all(copies):
    for c in copies:
        c.wait_recv()


def sent_all(copies):
    for c in copies:
        c.wait_send()


class SmallSum:
    SCRATCH = [VM((3, 24, 128), F32), VM((3, 24, 128), F32), VM((7, 24, 128), F32), VM((2, 24, 128), F32)]
    SEMS = [DMA((3, 8)), DMA((3, 8))]

    def __init__(self, place, src, bufs, sems):
        self.p, self.src, self.bufs, self.sems = place, src, bufs, sems
        self.copies = []

    def start(self):
        p, (s, r) = self.p, self.sems
        self.x = start_all([remote(self.src, self.bufs[0].at[k - 1], s.at[0, k], r.at[0, k], p.xpeer(k)) for k in NEAR])

    def along_y(self):
        p, (s, r) = self.p, self.sems
        arrive_all(self.x)
        got, sums = self.bufs[0], self.bufs[3]
        sums[0] = self.src[...] + got[0] + got[1] + got[2]
        self.y = start_all(
            [remote(sums.at[0], self.bufs[1].at[k - 1], s.at[1, k], r.at[1, k], p.ypeer(k)) for k in NEAR]
        )

    def along_dp(self):
        p, (s, r) = self.p, self.sems
        arrive_all(self.y)
        got, sums = self.bufs[1], self.bufs[3]
        sums[1] = sums[0] + got[0] + got[1] + got[2]
        self.d = start_all(
            [
                remote(sums.at[1], self.bufs[2].at[k - 1], s.at[2, k], r.at[2, k], {"dp": p.dpindex(k)})
                for k in range(1, 8)
            ]
        )

    def result(self):
        arrive_all(self.d)
        total = self.bufs[3][1]
        for k in range(7):
            total = total + self.bufs[2][k]
        return total

    def finish(self):
        sent_all(self.x + self.y + self.d)


def front(r):
    p = Place()
    barrier(xy_peers(p) + dp_peers(p))
    attn_copies, gu_copies = [], []
    for k in range(1, 8):
        to = p.dpindex(k)
        attn_copies.append(remote(r.attn, r.attn_in.at[p.dp], r.s_attn.at[k], r.r_attn.at[k], {"dp": to}))
    start_all(attn_copies)
    small = SmallSum(p, r.small, r.small_bufs, r.small_sems)
    small.start()
    place_copies = start_all(
        [remote(r.places, r.places_x.at[p.x], r.s_place.at[0, k], r.r_place.at[0, k], p.xpeer(k)) for k in NEAR]
    )
    for k in range(1, 8):
        to = p.dpindex(k)
        gu_copies.append(remote(r.gate_up.at[to], r.gu_in.at[p.dp], r.s_gu.at[k], r.r_gu.at[k], {"dp": to}))
    start_all(gu_copies)
    cots = GatherDp(p, r.cot, r.cot_all, r.cot_sems)
    cots.start()
    r.attn_in[p.dp] = r.attn[...]
    r.gu_in[p.dp] = r.gate_up[p.dp]
    r.places_x[p.x] = r.places[...]
    build_spread(r.spread)
    arrive_all(attn_copies)
    for half in (0, 1):
        for i in range(2):
            r.attn_block[half, i] = jnp.concatenate(
                [r.attn_in[4 * i + d, half] for d in range(4)], axis=0
            ).astype(BF16)
    ring_attn = GatherCtx(p, r.attn_block.at[p.core], r.w_attn.at[p.core], r.attn_sems, r.mate_sems)
    ring_attn.start()
    small.along_y()
    arrive_all(place_copies)
    place_copies2 = start_all(
        [remote(r.places_x, r.places_all.at[p.y], r.s_place.at[1, k], r.r_place.at[1, k], p.ypeer(k)) for k in NEAR]
    )
    r.places_all[p.y] = r.places_x[...]
    ring_attn.forward()
    small.along_dp()
    arrive_all(gu_copies)
    for i in range(2):
        r.gu_block[i] = jnp.concatenate([r.gu_in[4 * i + d] for d in range(4)], axis=0).astype(BF16)
    cots.forward()
    residual = r.hidden[...].astype(F32)
    unit_in = residual * rms_scale(residual)
    arrive_all(place_copies2)
    low_lane = lanes(8) < 64
    for c in range(8):
        a, b = r.places_all[(2 * c) // 4, (2 * c) % 4], r.places_all[(2 * c + 1) // 4, (2 * c + 1) % 4]
        r.key_row[:, 128 * c : 128 * c + 128] = jnp.where(low_lane, a, b)
    for mb in range(MB):
        r.key_places[mb] = jnp.transpose(jnp.broadcast_to(r.key_row[mb : mb + 1, :], (128, 1024)))
    r.small_all[...] = small.result()
    normed = spread((unit_in * row_vector(r.small_all, 0)).astype(BF16), r.spread[...])
    r.normed_in[...] = normed
    bias_query = row_vector(r.small_all, 7)
    ring_attn.arrive()
    cosine, sine = r.cosine[...], r.sine[...]
    lin = dot(normed, r.w_attn[0].reshape(DPAD, 1024))
    query_tiles = []
    for t in range(7):
        tile = lin[:, 128 * t : 128 * t + 128] + bias_query[:, 128 * t : 128 * t + 128]
        query_tiles.append((rotate(tile, cosine, sine).astype(BF16)).astype(F32) * (HEAD_SIZE**-0.5))
    keys = rotate(lin[:, 896:] + r.small_all[21:22, :], cosine, sine).astype(BF16)
    values = dot(normed, r.w_attn[1, :, :, :, :128].reshape(DPAD, 128)) + r.small_all[22:23, :]
    values = values.astype(BF16)
    for mb in range(MB):
        r.kv[mb, :, :128] = keys[64 * mb : 64 * mb + 64]
        r.kv[mb, :, 128:] = values[64 * mb : 64 * mb + 64]
    ring_kv = GatherCtx(p, r.kv, r.kv_all, r.kv_sems)
    ring_kv.start()
    scatter_heads(lambda mb, t: query_tiles[t][64 * mb : 64 * mb + 64], r.heads)
    ring_kv.forward()
    ring_gu = GatherCtx(p, r.gu_block, r.w_gu, r.gu_sems)
    ring_gu.start()
    down_copies = start_all(
        [remote(r.down, r.down_in.at[p.x], r.s_down.at[0, k], r.r_down.at[0, k], p.xpeer(k)) for k in NEAR]
    )
    r.down_in[p.x] = r.down[...]
    ring_kv.arrive()
    for mb in range(MB):
        r.keys[mb] = r.kv_all[:, mb, :, :128].reshape(1024, 128)
        r.values[mb] = r.kv_all[:, mb, :, 128:].reshape(1024, 128)
        r.values_t[mb] = jnp.transpose(r.values[mb].astype(F32)).astype(BF16)

    def attend(mb):
        def step(t, carry):
            i = mb * 7 + t
            scores = dot_nt(r.keys[mb], r.heads[i])
            scores = jnp.where(r.key_places[mb] <= r.places[mb : mb + 1, :], scores, -1e30)
            expo = jnp.exp(scores - jnp.max(scores, axis=0, keepdims=True))
            probs = (expo * (1.0 / jnp.sum(expo, axis=0, keepdims=True))).astype(BF16)
            r.probs[i] = probs
            r.attended[i] = collect_heads(dot(r.values_t[mb], probs), t).astype(BF16)
            return carry

        lax.fori_loop(0, 7, step, 0)

    attend(0)
    ring_gu.forward()
    arrive_all(down_copies)
    r.w_down[pl.ds(pl.multiple_of(160 * p.y, 32), 160), :] = jnp.concatenate(
        [r.down_in[i] for i in range(4)], axis=0
    ).astype(BF16)
    own_down = r.w_down.at[pl.ds(pl.multiple_of(160 * p.y, 32), 160)]
    down_copies2 = start_all(
        [remote(own_down, own_down, r.s_down.at[1, k], r.r_down.at[1, k], p.ypeer(k)) for k in NEAR]
    )
    attend(1)
    attended = jnp.concatenate(
        [jnp.concatenate([r.attended[mb * 7 + t] for t in range(7)], axis=1) for mb in range(MB)], axis=0
    )
    attended_wide = spread(attended, r.spread[...])
    r.attended_wide[...] = attended_wide
    mixed = residual + dot(attended_wide, r.w_attn[1, :, :, :, 128:].reshape(DPAD, D))
    r.mixed[...] = mixed
    unit_mid = mixed * rms_scale(mixed)
    r.normed_mid[...] = spread((unit_mid * row_vector(r.small_all, 14)).astype(BF16), r.spread[...])
    ring_mid = GatherDp(p, r.normed_mid, r.normed_all, r.mid_sems)
    ring_mid.start()
    ring_gu.arrive()
    arrive_all(down_copies2)
    cots.arrive()
    ring_mid.forward()
    for ring in (ring_attn, ring_kv, ring_gu, cots, small):
        ring.finish()
    sent_all(attn_copies + gu_copies + place_copies + place_copies2 + down_copies + down_copies2)
    ring_mid.arrive()
    ring_mid.finish()


FRONT_OUTS = {
    "w_attn": shape((2, 16, 2, 32, 1024), BF16),
    "w_gu": shape((16, 2, 32, 1280), BF16),
    "w_down": shape((640, D), BF16),
    "small_all": shape((24, 128), F32),
    "cot_all": shape((8, 128, D), BF16),
    "normed_all": shape((8, 128, DPAD), BF16),
    "probs": shape((14, 1024, 128), BF16),
    "heads": shape((14, 128, 128), BF16),
    "keys": shape((2, 1024, 128), BF16),
    "values": shape((2, 1024, 128), BF16),
    "attended_wide": shape((128, DPAD), BF16),
    "normed_in": shape((128, DPAD), BF16),
    "mixed": shape((128, D), F32),
    "spread": shape((D, DPAD), BF16),
}
FRONT_SCRATCH = {
    "attn_in": VM((8, 2, 8, 1024), F32),
    "gu_in": VM((8, 8, 1280), F32),
    "down_in": VM((4, 40, D), F32),
    "places_x": VM((4, 8, 128), F32),
    "places_all": VM((4, 4, 8, 128), F32),
    "key_row": VM((8, 1024), F32),
    "key_places": VM((2, 1024, 128), F32),
    "attn_block": VM((2, 2, 32, 1024), BF16),
    "gu_block": VM((2, 32, 1280), BF16),
    "kv": VM((2, 64, 256), BF16),
    "kv_all": VM((16, 2, 64, 256), BF16),
    "values_t": VM((2, 128, 1024), BF16),
    "attended": VM((14, 64, 128), BF16),
    "normed_mid": VM((128, DPAD), BF16),
    "small_bufs": SmallSum.SCRATCH,
    "small_sems": SmallSum.SEMS,
    "s_attn": DMA((8,)), "r_attn": DMA((8,)), "s_gu": DMA((8,)), "r_gu": DMA((8,)),
    "s_place": DMA((2, 4)), "r_place": DMA((2, 4)), "s_down": DMA((2, 4)), "r_down": DMA((2, 4)),
    "attn_sems": GatherCtx.SEMS, "mate_sems": GatherCtx.MATE, "kv_sems": GatherCtx.SEMS,
    "gu_sems": GatherCtx.SEMS, "cot_sems": GatherDp.SEMS, "mid_sems": GatherDp.SEMS,
}


def back(r):
    p = Place()
    barrier(xy_peers(p) + dp_peers(p))
    red_normed = ReduceDp(p, r.part_normed, r.normed_bufs, r.normed_sems)
    red_out = ReduceDp(p, r.part_normed.at[:, :, :, pl.ds(0, D)], r.out_bufs, r.out_sems)

    def rows_of(ref, to):
        return ref[pl.ds(2 * to, 2)].reshape(256, ref.shape[-1])

    def feed(i, carry):
        to = lax.rem(p.z + 1 + i, 4)
        at = pl.ds(pl.multiple_of(256 * to, 256), 256)
        lin = dot(rows_of(r.normed_all, to), r.w_gu[...].reshape(DPAD, 1280))
        gate, up = lin[:, :640], lin[:, 640:]
        sig = 1.0 / (1.0 + jnp.exp(-gate))
        silu = gate * sig
        hidden = (silu * up).astype(BF16)
        back_hidden = dot_nt(rows_of(r.cot_all, to), r.w_down[...]).astype(BF16).astype(F32)
        grad_gate = (back_hidden * up * sig * (1.0 + gate * (1.0 - sig))).astype(BF16)
        grad_up = (back_hidden * silu).astype(BF16)
        for t in range(5):
            r.big[t, at, :] = grad_gate[:, 128 * t : 128 * t + 128]
            r.big[5 + t, at, :] = grad_up[:, 128 * t : 128 * t + 128]
            r.big[10 + t, at, :] = hidden[:, 128 * t : 128 * t + 128]
        part = dot_nt(jnp.concatenate([grad_gate, grad_up], axis=1), r.w_gu[...].reshape(DPAD, 1280))
        r.part_normed[to] = part.astype(BF16).reshape(2, 128, DPAD)
        red_normed.send(i)
        return carry

    lax.fori_loop(0, 4, feed, 0)
    red_normed.forward()

    def project(i, carry):
        to = lax.rem(p.z + 1 + i, 4)
        at = pl.ds(pl.multiple_of(256 * to, 256), 256)
        hidden = jnp.concatenate([r.big[10 + t, at, :] for t in range(5)], axis=1)
        r.part_normed[to, :, :, :D] = dot(hidden, r.w_down[...]).astype(BF16).reshape(2, 128, D)
        red_out.send(i)
        return carry

    def grad_gate_up(i, carry):
        at = pl.ds(pl.multiple_of(256 * i, 256), 256)
        left = r.normed_all[:, :, at].reshape(1024, 256)
        right = jnp.concatenate([r.big[t] for t in range(10)], axis=1)
        r.g_gu[i] = dot_tn(left, right).astype(BF16).reshape(4, 2, 32, 1280)
        return carry

    lax.fori_loop(0, 4, grad_gate_up, 0)
    ring_gu = ReduceCtx(p, r.g_gu, r.gu_bufs, r.gu_sems)
    ring_gu.start()

    def grad_down(t, carry):
        at = pl.ds(pl.multiple_of(128 * t, 128), 128)
        r.g_down[at, :] = dot_tn(r.big[10 + t], r.cot_all[...].reshape(1024, D)).astype(BF16)
        return carry

    lax.fori_loop(0, 5, grad_down, 0)
    down_copies = start_all(
        [
            remote(
                r.g_down.at[pl.ds(pl.multiple_of(160 * p.at_y(k), 32), 160)],
                r.down_y.at[k - 1], r.s_down.at[0, k], r.r_down.at[0, k], p.ypeer(k),
            )
            for k in NEAR
        ]
    )
    red_normed.sent()
    lax.fori_loop(0, 4, project, 0)
    gain_mlp = row_vector(r.small_all, 14)
    mixed = r.mixed[...]
    inv_mid = rms_scale(mixed)
    unit_mid = mixed * inv_mid
    r.held[...] = unspread(red_normed.result(), r.spread[...])
    grad_normed = r.held[...]
    store_rows(r.small_grads, 14, jnp.sum(grad_normed * unit_mid, axis=0, keepdims=True))
    scaled = grad_normed * gain_mlp
    grad_mixed = r.cot[...].astype(F32) + inv_mid * (
        scaled - unit_mid * jnp.mean(scaled * unit_mid, axis=-1, keepdims=True)
    )
    r.grad_mixed[...] = grad_mixed
    grad_branch = grad_mixed.astype(BF16)
    wide = dot_nt(grad_branch, r.w_attn[1, :, :, :, 128:].reshape(DPAD, D)).astype(BF16)
    grad_attended = dot_nt(wide, r.spread[...])
    scatter_heads(
        lambda mb, t: grad_attended[64 * mb : 64 * mb + 64, 128 * t : 128 * t + 128], r.grad_heads
    )
    for mb in range(MB):
        r.keys_t[mb] = jnp.transpose(r.keys[mb].astype(F32)).astype(BF16)
    red_out.forward()

    def attend_back(mb):
        def step(t, carry):
            i = mb * 7 + t
            grad_probs = dot_nt(r.values[mb], r.grad_heads[i])
            probs = r.probs[i].astype(F32)
            weighted = probs * grad_probs
            inner = jnp.sum(weighted, axis=0, keepdims=True)
            grad_scores = (weighted - probs * inner).astype(BF16)
            r.big[i] = grad_scores
            r.grad_query[i] = collect_heads(dot(r.keys_t[mb], grad_scores), t)
            return carry

        lax.fori_loop(0, 7, step, 0)

    def grad_key_value(i, carry):
        mb, y = i // 4, lax.rem(i, 4)
        at = pl.ds(pl.multiple_of(256 * y, 256), 256)
        scores = jnp.concatenate([r.big[mb * 7 + t, at, :] for t in range(7)], axis=1)
        probs = jnp.concatenate([r.probs[mb * 7 + t, at, :] for t in range(7)], axis=1)
        grad_keys = dot(scores, r.heads[pl.ds(7 * mb, 7)].reshape(896, 128))
        grad_values = dot(probs, r.grad_heads[pl.ds(7 * mb, 7)].reshape(896, 128))
        r.g_kv[y, :, mb, :, :128] = grad_keys.astype(BF16).reshape(4, 64, 128)
        r.g_kv[y, :, mb, :, 128:] = grad_values.astype(BF16).reshape(4, 64, 128)
        return carry

    attend_back(0)
    attend_back(1)
    lax.fori_loop(0, 8, grad_key_value, 0)
    ring_kv = ReduceCtx(p, r.g_kv, r.kv_bufs, r.kv_sems)
    ring_kv.start()
    cosine, sine = r.cosine[...], r.sine[...]
    tiles = []
    for t in range(7):
        tile = jnp.concatenate([r.grad_query[t], r.grad_query[7 + t]], axis=0) * (HEAD_SIZE**-0.5)
        tiles.append(rotate_back(tile, cosine, sine).astype(BF16))
    grad_query = jnp.concatenate(tiles, axis=1)
    store_rows(r.small_grads, 7, jnp.sum(grad_query.astype(F32), axis=0, keepdims=True))
    ring_kv.forward()
    r.low_a[...] = grad_query
    r.low_b[...] = grad_branch

    def grad_query_output(y, carry):
        at = pl.ds(pl.multiple_of(256 * y, 256), 256)
        part = dot_tn(r.normed_in[:, at], r.low_a[...])
        r.g_attn[0, y, :, :, :, :896] = part.astype(BF16).reshape(4, 2, 32, 896)
        part = dot_tn(r.attended_wide[:, at], r.low_b[...])
        r.g_attn[1, y, :, :, :, 128:] = part.astype(BF16).reshape(4, 2, 32, D)
        return carry

    lax.fori_loop(0, 4, grad_query_output, 0)
    kv_sum = jnp.concatenate([ring_kv.result(0), ring_kv.result(1)], axis=0)
    grad_key = rotate_back(kv_sum[:, :128], cosine, sine).astype(BF16)
    grad_value = kv_sum[:, 128:].astype(BF16)
    for y in range(4):
        left = r.normed_in[:, 256 * y : 256 * y + 256]
        part = dot_tn(left, jnp.concatenate([grad_key, grad_value], axis=1)).astype(BF16)
        r.g_attn[0, y, :, :, :, 896:] = part[:, :128].reshape(4, 2, 32, 128)
        r.g_attn[1, y, :, :, :, :128] = part[:, 128:].reshape(4, 2, 32, 128)
    mate_copies = start_all(
        [
            remote(r.g_attn.at[1 - p.core, y], r.mate_in.at[y], r.s_mate.at[y], r.r_mate.at[y], {"dp": p.mate()})
            for y in range(4)
        ]
    )
    store_rows(r.small_grads, 21, jnp.sum(grad_key.astype(F32), axis=0, keepdims=True))
    store_rows(r.small_grads, 22, jnp.sum(grad_value.astype(F32), axis=0, keepdims=True))
    r.small_grads[23:24, :] = jnp.zeros((1, 128), F32)
    grad_normed_wide = dot_nt(
        jnp.concatenate([grad_query, grad_key], axis=1), r.w_attn[0].reshape(DPAD, 1024)
    ) + dot_nt(grad_value, r.w_attn[1, :, :, :, :128].reshape(DPAD, 128))
    grad_normed_in = unspread(grad_normed_wide, r.spread[...])
    residual = r.hidden[...].astype(F32)
    inv_rms = rms_scale(residual)
    unit_in = residual * inv_rms
    store_rows(r.small_grads, 0, jnp.sum(grad_normed_in * unit_in, axis=0, keepdims=True))
    small = SmallSum(p, r.small_grads, r.small_bufs, r.small_sems)
    small.start()
    for y in range(4):
        mate_copies[y].wait_recv()
        r.mate_in[y] = (r.g_attn[p.core, y].astype(F32) + r.mate_in[y].astype(F32)).astype(BF16)
    ring_attn = ReduceCtx(p, r.mate_in, r.attn_bufs, r.attn_sems)
    ring_attn.start()
    scaled = grad_normed_in * row_vector(r.small_all, 0)
    r.grad_in[...] = r.grad_mixed[...] + inv_rms * (
        scaled - unit_in * jnp.mean(scaled * unit_in, axis=-1, keepdims=True)
    )
    r.layer_out[...] = (mixed + red_out.result()).astype(BF16)
    ring_gu.forward()
    arrive_all(down_copies)
    total = r.g_down[pl.ds(pl.multiple_of(160 * p.y, 32), 160), :].astype(F32)
    for k in NEAR:
        total = total + r.down_y[k - 1].astype(F32)
    for i in range(4):
        r.down_mid[i] = total[40 * i : 40 * i + 40]
    down_copies2 = start_all(
        [
            remote(r.down_mid.at[p.at_x(k)], r.down_x.at[k - 1], r.s_down.at[1, k], r.r_down.at[1, k], p.xpeer(k))
            for k in NEAR
        ]
    )
    small.along_y()
    ring_attn.forward()
    small.along_dp()
    for h in (0, 1):
        part = ring_gu.result(h)
        for d in range(4):
            r.gu_out[4 * h + d] = part[8 * d : 8 * d + 8]
    out_copies = []
    for k in range(1, 8):
        to = p.dpindex(k)
        out_copies.append(remote(r.gu_out.at[to], r.o_gu.at[p.dp], r.s_gu.at[k], r.r_gu.at[k], {"dp": to}))
    start_all(out_copies)
    r.o_gu[p.dp] = r.gu_out[p.dp]
    arrive_all(down_copies2)
    r.o_down[...] = r.down_mid[p.x] + r.down_x[0] + r.down_x[1] + r.down_x[2]
    for h in (0, 1):
        part = ring_attn.result(h)
        for d in range(4):
            r.attn_out[4 * h + d] = part[8 * d : 8 * d + 8]
    attn_copies = []
    for k in range(1, 8):
        to = p.dpindex(k)
        attn_copies.append(
            remote(r.attn_out.at[to], r.attn_dp.at[p.z, p.core], r.s_attn.at[k], r.r_attn.at[k], {"dp": to})
        )
    start_all(attn_copies)
    r.attn_dp[p.z, p.core] = r.attn_out[p.dp]
    r.o_small[...] = small.result()
    arrive_all(out_copies + attn_copies)
    for half in (0, 1):
        r.o_attn[half] = r.attn_dp[0, half] + r.attn_dp[1, half] + r.attn_dp[2, half] + r.attn_dp[3, half]
    red_out.sent()
    for ring in (red_normed, red_out, ring_gu, ring_kv, ring_attn, small):
        ring.finish()
    sent_all(mate_copies + down_copies + down_copies2 + out_copies + attn_copies)


BACK_OUTS = {
    "layer_out": shape((128, D), BF16),
    "grad_in": shape((128, D), F32),
    "o_attn": shape((2, 8, 1024), F32),
    "o_gu": shape((8, 8, 1280), F32),
    "o_down": shape((40, D), F32),
    "o_small": shape((24, 128), F32),
}
BACK_SCRATCH = {
    "big": VM((15, 1024, 128), BF16),
    "part_normed": VM((4, 2, 128, DPAD), BF16),
    "normed_bufs": ReduceDp.scratch(128, DPAD), "normed_sems": ReduceDp.SEMS,
    "out_bufs": ReduceDp.scratch(128, D), "out_sems": ReduceDp.SEMS,
    "g_gu": VM((4, 4, 2, 32, 1280), BF16),
    "gu_bufs": ReduceCtx.scratch(32, 1280), "gu_sems": ReduceCtx.SEMS,
    "g_down": VM((640, D), BF16),
    "down_y": VM((3, 160, D), BF16), "down_mid": VM((4, 40, D), F32), "down_x": VM((3, 40, D), F32),
    "grad_mixed": VM((128, D), F32),
    "held": VM((128, D), F32),
    "low_a": VM((128, D), BF16),
    "low_b": VM((128, D), BF16),
    "grad_heads": VM((14, 128, 128), BF16),
    "keys_t": VM((2, 128, 1024), BF16),
    "grad_query": VM((14, 64, 128), F32),
    "g_kv": VM((4, 4, 2, 64, 256), BF16),
    "kv_bufs": ReduceCtx.scratch(64, 256), "kv_sems": ReduceCtx.SEMS,
    "g_attn": VM((2, 4, 4, 2, 32, 1024), BF16),
    "mate_in": VM((4, 4, 2, 32, 1024), BF16),
    "attn_bufs": ReduceCtx.scratch(32, 1024), "attn_sems": ReduceCtx.SEMS,
    "small_grads": VM((24, 128), F32),
    "small_bufs": SmallSum.SCRATCH, "small_sems": SmallSum.SEMS,
    "gu_out": VM((8, 8, 1280), F32), "attn_out": VM((8, 8, 1024), F32), "attn_dp": VM((4, 2, 8, 1024), F32),
    "s_mate": DMA((4,)), "r_mate": DMA((4,)), "s_down": DMA((2, 4)), "r_down": DMA((2, 4)),
    "s_gu": DMA((8,)), "r_gu": DMA((8,)), "s_attn": DMA((8,)), "r_attn": DMA((8,)),
}


def body(
    hidden_in, positions, norm_attn, w_query, b_query, w_key, b_key, value_weight, value_bias, w_output,
    norm_mlp, w_gate, w_up, w_down, cotangent,
):
    rows = MB * 64
    me = lax.axis_index("dp") * 16 + lax.axis_index("ctx")
    places = positions[:, 0]
    attn = jnp.pad(
        jnp.stack(
            [jnp.concatenate([w_query, w_key], axis=1), jnp.concatenate([value_weight, w_output], axis=1)]
        ).astype(F32),
        ((0, 0), (0, 1), (0, 0)),
    )

    def slices(w):
        parts = w.astype(F32).reshape(7, 8, 16, 38)
        return jnp.pad(parts, ((0, 1), (0, 0), (0, 0), (0, 2))).transpose(1, 0, 2, 3).reshape(8, 8, 640)

    def put(vector, width):
        full = jnp.zeros((128, width), F32)
        return lax.dynamic_update_slice(full, vector.astype(F32)[None], (me, 0)).reshape(-1)

    small = jnp.concatenate(
        [put(norm_attn, 7), put(b_query, 7), put(norm_mlp, 7), put(b_key, 1), put(value_bias, 1), jnp.zeros((128,), F32)]
    ).reshape(24, 128)
    freqs = THETA_BASE ** (-jnp.arange(0, HEAD_SIZE, 2).astype(F32) / HEAD_SIZE)
    angles = places.reshape(rows).astype(F32)[:, None] * jnp.tile(freqs, 4)[None, :]
    sign = jnp.tile(jnp.repeat(jnp.array([-1.0, 1.0], F32), HEAD_SIZE // 2), 2)
    own = {
        "hidden": hidden_in.reshape(rows, D),
        "cot": cotangent.reshape(rows, D),
        "cosine": jnp.cos(angles),
        "sine": jnp.sin(angles) * sign,
    }
    sent = {
        "attn": attn,
        "gate_up": jnp.concatenate([slices(w_gate), slices(w_up)], axis=-1),
        "down": jnp.pad(w_down.astype(F32), ((0, 2), (0, 0))),
        "small": small,
        "places": jnp.pad(jnp.tile(places.astype(F32), (1, 2)), ((0, 6), (0, 0))),
    }
    kept = call(front, {**own, **sent}, FRONT_OUTS, FRONT_SCRATCH, 0, "front")
    done = call(back, {**own, **kept}, BACK_OUTS, BACK_SCRATCH, 1, "back")
    o_attn, o_gu = done["o_attn"], done["o_gu"]

    def joined(parts):
        return parts[:, :7].reshape(8, 7, 16, 40)[..., :38].transpose(1, 0, 2, 3).reshape(7, 4864)

    sums = done["o_small"].reshape(-1)

    def take(start, width):
        return lax.dynamic_slice(sums, (start + me * width,), (width,))

    return (
        done["layer_out"].reshape(MB, 1, 64, D),
        done["grad_in"].reshape(MB, 1, 64, D),
        take(0, 7),
        o_attn[0, :7, :896],
        take(896, 7),
        o_attn[0, :7, 896:],
        sums[2688:2816],
        o_attn[1, :7, :128],
        take(2816, 1),
        o_attn[1, :7, 128:],
        take(1792, 7),
        joined(o_gu[..., :640]),
        joined(o_gu[..., 640:]),
        done["o_down"][:38],
    )


def solution(mesh):
    rows = P(("dp", "ctx"), None)
    vector = P(("dp", "ctx"))
    tokens = P(None, "dp", "ctx", None)
    in_specs = (
        tokens, P(None, "dp", "ctx"), vector, rows, vector, rows, vector, rows, vector, rows, vector,
        rows, rows, rows, tokens,
    )
    out_specs = (
        tokens, tokens, vector, rows, vector, rows, P(), rows, vector, rows, vector, rows, rows, rows,
    )
    return jax.shard_map(body, mesh=mesh, in_specs=in_specs, out_specs=out_specs, check_vma=False)
```

time: 377 us -> 221 us (0.59); the launches traced: 371 us -> 221 us
  matrix products: 52.5 us -> 0 us
  local copies, waits for them, and re-layouts: 67.2 us -> 17 us
  Pallas kernels: 220 us -> 195 us
  other arithmetic: 26.8 us -> 6.71 us
    dot_general x21 -> x0, matrix products: 46.2 us -> none  [the longest x6 13.6 us: matrix_product(): return jnp.dot(left, right, preferred_element_type=F32)]
    pallas_call x7 -> x2, Pallas kernels: 220 us -> 195 us  [call(): pl.pallas_call(kernel, out_shape=tuple(outs.values()), in_specs=[pl.Block...]
    concatenate x14 -> x0, local copies, waits for them, and re-layouts: 12.1 us -> none  [the longest x4 5.83 us: body(): jnp.concatenate([grad_key_part.reshape(MB, 1024, 128), grad_value_part.re...]
    convert_element_type x10 -> x2, other arithmetic: 10.2 us -> 0.7 us  [body(): places.reshape(rows).astype(F32)[:, None] * jnp.tile(freqs, 4)[None, :]]
    reshape x10 -> x0, local copies, waits for them, and re-layouts: 9.36 us -> none  [the longest x4 4.08 us: unspread(): values.reshape(rows, 16, 8, 8)[..., :7].transpose(0, 2, 1, 3)]
    slice x7 -> x0, local copies, waits for them, and re-layouts: 8.99 us -> none  [the longest x2 3.21 us: body(): key_all = kv_all[..., :128].reshape(MB, 1024, 2, 64)]
    unnamed x138 -> x22, local copies, waits for them, and re-layouts: 9.26 us -> 2.18 us
    sub x1 -> x0, matrix products: 6.28 us -> none  [attend(): expo = jnp.exp(scores - top)]
where the time goes in v2:
time: 221 us
  Pallas kernels  195 us (88%)
  local copies, waits for them, and re-layouts  17 us (8%)
  other arithmetic  6.71 us (3%)
  between operations  2.22 us (1%)
    pallas_call x2, Pallas kernels, call(): pl.pallas_call(kernel, out_shape=tuple(outs.values()), in_specs=[pl.Block...  195 us

profile of v2, /device:TPU:1, one launch (start us, length us, event | category | flops | bytes accessed | tf_op | source)
XLA Modules:
  0.0 220.7 jit_solution(811413239344535247)
XLA Ops:
  0.6 0.0 copy-start.6
  0.7 0.0 copy-start.3
  0.7 0.7 bitcast_convert_fusion.2
  1.4 0.2 reshape.126
  1.6 0.7 bitcast_convert_fusion.1
  2.3 0.2 reshape.127
  2.5 0.7 bitcast_convert_fusion
  3.2 0.2 reshape.128
  4.1 0.1 convert_dynamic-update-slice_fusion.1
  4.9 0.1 convert_dynamic-update-slice_fusion
  5.0 0.0 copy-start.5
  5.0 0.1 mul.46
  5.1 0.7 broadcast_in_dim.25
  5.9 0.1 tile.11
  5.9 0.1 mul.49
  6.0 0.7 convert_reduce_fusion
  6.7 0.1 convert_element_type.48
  6.8 1.0 fusion
  7.8 0.8 maximum_bitcast_fusion
  8.5 0.6 fusion.4.refs_4_
  9.2 1.5 reshape.122
  10.7 0.1 pad_bitcast_fusion.1
  10.7 0.3 reshape.123
  11.0 1.5 reshape.124
  12.5 0.1 pad_bitcast_fusion
  12.5 0.3 reshape.125
  12.8 0.7 maximum_convert_fusion.refs_5_
  13.5 0.0 copy-done.3
  13.5 0.7 pad_convert_fusion.refs_6_
  14.2 0.0 copy-done.6
  14.2 0.1 tile.26
  14.3 0.6 pad.31.refs_8_
  14.9 0.0 copy-done.5
  14.9 93.9 %front.1 = (bf16[2,16,2,32,1024]{4,3,2,1,0:T(8,128)(2,1)}, bf16[16,2,32,1280]{3,2,1,0:T(8,128)(2,1)}, bf16[640,896]{1,0:T(8,128)(2,1)}, f32[24,128]{1,0:T(8,128)...) custom-call(bf16[128,896]{1,0:T(8,128)(2,1)} %bitcast.55, ...), custom_call_target="tpu_custom_call" | custom-call | tf_op jit(solution)/shard_map/front/pallas_call | solution.py:311
  108.8 101.0 %back.1 = (bf16[128,896]{1,0:T(8,128)(2,1)}, f32[128,896]{1,0:T(8,128)}, f32[2,8,1024]{2,1,0:T(8,128)}, f32[8,8,1280]{2,1,0:T(8,128)}, f32[40,896]{1,0:T(8,128)}, /*index=5*/f32[24,128]{1,0:T(8,128)}) custom-call(bf16[128,896]{1,0:T(8,128)(2,1)} %bitcast.56, bf16[128,896]{1,0:T(8,128)(2,1)} %bitcast.58, f32[128,128]{1,0:T(8,128)} %get-tuple-element.92.refs_2_, ...), custom_call_target="tpu_custom_call" | custom-call | tf_op jit(solution)/shard_map/back/pallas_call | solution.py:311
  209.7 1.0 fusion.5
  210.8 0.3 reshape.134
  211.2 1.0 reshape.135
  212.2 0.3 reshape.136
  212.6 1.0 reshape.137
  213.5 0.6 slice_bitcast_fusion.2
  214.1 1.4 fusion.6
  215.5 1.3 dynamic_slice.14
  216.8 0.6 slice_bitcast_fusion.4
  217.4 1.2 slice_bitcast_fusion.6
  218.6 0.7 copy.63
  219.3 0.8 copy.64
  220.1 0.7 copy.65
  (32 shorter events, 0.3 us)
Async XLA Ops:
  0.6 13.6 %copy-start.6 = (s32[2,1,64]{2,1,0:T(1,128)S(1)}, s32[2,1,64]{2,1,0:T(1,128)}, u32[]{:S(2)}) copy-start(s32[2,1,64]{2,1,0:T(1,128)} %param.17) | copy-start | bytes 1540
  0.7 12.9 %copy-start.3 = (bf16[38,896]{1,0:T(8,128)(2,1)S(1)}, bf16[38,896]{1,0:T(8,128)(2,1)}, u32[]{:S(2)}) copy-start(bf16[38,896]{1,0:T(8,128)(2,1)} %param.29) | copy-start | bytes 204292
  5.0 9.9 %copy-start.5 = (f32[3072]{0:T(1024)}, f32[3072]{0:T(1024)S(1)}, u32[]{:S(2)}) copy-start(f32[3072]{0:T(1024)S(1)} %constant_dynamic-update-slice_fusion) | copy-start | bytes 36868
  211.1 2.4 %copy-start.4 = (f32[2,8,1024]{2,1,0:T(8,128)S(1)}, f32[2,8,1024]{2,1,0:T(8,128)}, u32[]{:S(2)}) copy-start(f32[2,8,1024]{2,1,0:T(8,128)} %get-tuple-element.51) | copy-start | bytes 196612
  211.1 7.5 %copy-start.1 = (bf16[128,896]{1,0:T(8,128)(2,1)S(1)}, bf16[128,896]{1,0:T(8,128)(2,1)}, u32[]{:S(2)}) copy-start(bf16[128,896]{1,0:T(8,128)(2,1)} %get-tuple-element.48) | copy-start | bytes 688132
  211.1 8.1 %copy-start = (f32[128,896]{1,0:T(8,128)S(1)}, f32[128,896]{1,0:T(8,128)}, u32[]{:S(2)}) copy-start(f32[128,896]{1,0:T(8,128)} %get-tuple-element.49) | copy-start | bytes 1376260
  212.1 7.9 %copy-start.2 = (f32[40,896]{1,0:T(8,128)S(1)}, f32[40,896]{1,0:T(8,128)}, u32[]{:S(2)}) copy-start(f32[40,896]{1,0:T(8,128)} %get-tuple-element.53) | copy-start | bytes 430084

commit v3 on v2

v3 whole, which is shorter than its diff:
```python
import types

import jax
import jax.numpy as jnp
from jax import lax
from jax.experimental import pallas as pl
from jax.experimental.pallas import tpu as pltpu
from jax.sharding import PartitionSpec as P

QUERY_HEADS = 14
KEY_VALUE_HEADS = 2
HEAD_SIZE = 64
GROUP = QUERY_HEADS // KEY_VALUE_HEADS
MB = 2
D = 896
DPAD = 1024
EPSILON = 1e-06
THETA_BASE = 1000000.0
F32 = jnp.float32
BF16 = jnp.bfloat16
MESH = pl.DeviceIdType.MESH
DMA = pltpu.SemaphoreType.DMA
VM = pltpu.VMEM


def remote(src, dst, ss, rs, peer):
    return pltpu.make_async_remote_copy(
        src_ref=src, dst_ref=dst, send_sem=ss, recv_sem=rs, device_id=peer, device_id_type=MESH
    )


def barrier(peers):
    sem = pltpu.get_barrier_semaphore()
    for peer in peers:
        pl.semaphore_signal(sem, inc=1, device_id=peer, device_id_type=MESH)
    pl.semaphore_wait(sem, len(peers))


class Place:
    def __init__(self):
        self.dp = lax.axis_index("dp")
        self.ctx = lax.axis_index("ctx")
        self.y, self.x = self.ctx // 4, lax.rem(self.ctx, 4)
        self.z, self.core = self.dp // 2, lax.rem(self.dp, 2)

    def at_x(self, k):
        return lax.rem(self.x + (k + 4), 4)

    def at_y(self, k):
        return lax.rem(self.y + (k + 4), 4)

    def at_z(self, k):
        return lax.rem(self.z + (k + 4), 4)

    def line(self, axis, k):
        return self.y * 4 + self.at_x(k) if axis == 0 else self.at_y(k) * 4 + self.x

    def xpeer(self, k):
        return {"ctx": self.line(0, k)}

    def ypeer(self, k):
        return {"ctx": self.line(1, k)}

    def peer(self, axis, k):
        return {"ctx": self.line(axis, k)}

    def zindex(self, k):
        return self.at_z(k) * 2 + self.core

    def mate(self):
        return self.z * 2 + 1 - self.core

    def dpindex(self, k):
        return lax.rem(self.dp + k, 8)


NEAR = (1, 3, 2)


class GatherCtx:
    SEMS = [DMA((2, 4)), DMA((2, 4)), DMA((2, 4, 4)), DMA((2, 4, 4)), DMA((2,))]
    MATE = [DMA((2, 4, 4)), DMA((2, 4, 4))]

    def __init__(self, place, src, dst_at, sems, mate=None):
        self.p, self.src, self.dst_at, self.sems, self.mate = place, src, dst_at, sems, mate
        self.mated = []

    def block(self, h, j, k):
        p = self.p
        return p.at_y(-k) * 4 + p.at_x(-j) if h == 0 else p.at_y(-j) * 4 + p.at_x(-k)

    def share(self, h, j, k):
        if self.mate is None:
            return
        dst = self.dst_at(self.block(h, j, k), h)
        src = self.src.at[h] if j == 0 and k == 0 else dst
        c = remote(src, dst, self.mate[0].at[h, j, k], self.mate[1].at[h, j, k], {"dp": self.p.mate()})
        c.start()
        self.mated.append(c)

    def start(self):
        p, (s1, r1, s2, r2, ls) = self.p, self.sems
        self.local = []
        for h in (0, 1):
            c = pltpu.make_async_copy(self.src.at[h], self.dst_at(p.ctx, h), ls.at[h])
            c.start()
            self.local.append(c)
        self.first = {}
        for k in NEAR:
            for h in (0, 1):
                c = remote(self.src.at[h], self.dst_at(p.ctx, h), s1.at[h, k], r1.at[h, k], p.peer(h, k))
                c.start()
                self.first[h, k] = c
        for h in (0, 1):
            self.share(h, 0, 0)

    def forward(self):
        p, (s1, r1, s2, r2, ls) = self.p, self.sems
        self.second = {}
        for j in (0,) + NEAR:
            for h in (0, 1):
                if j:
                    self.first[h, j].wait_recv()
                dst = self.dst_at(p.line(h, -j), h)
                src = self.src.at[h] if j == 0 else dst
                for k in NEAR:
                    c = remote(src, dst, s2.at[h, j, k], r2.at[h, j, k], p.peer(1 - h, k))
                    c.start()
                    self.second[h, j, k] = c
                if j:
                    self.share(h, j, 0)

    def arrive(self):
        for c in self.local:
            c.wait()
        for (h, j, k), c in self.second.items():
            c.wait_recv()
            self.share(h, j, k)
        for c in self.mated:
            c.wait_recv()

    def finish(self):
        for c in list(self.first.values()) + list(self.second.values()) + self.mated:
            c.wait_send()


class ReduceCtx:
    SEMS = [DMA((2, 4)), DMA((2, 4)), DMA((2, 4)), DMA((2, 4))]

    @staticmethod
    def scratch(rows, cols):
        return [VM((2, 3, 4, rows, cols), BF16), VM((2, 3, rows, cols), BF16)]

    def __init__(self, place, src_at, bufs, sems):
        self.p, self.src_at, self.bufs, self.sems = place, src_at, bufs, sems

    def start(self):
        p, (s1, r1, s2, r2) = self.p, self.sems
        got = self.bufs[0]
        every = slice(None)
        self.first = {}
        for k in NEAR:
            for h in (0, 1):
                src = self.src_at(0, p.at_y(k), every) if h == 0 else self.src_at(1, every, p.at_x(k))
                c = remote(src, got.at[h, k - 1], s1.at[h, k], r1.at[h, k], p.peer(1 - h, k))
                c.start()
                self.first[h, k] = c

    def forward(self):
        p, (s1, r1, s2, r2) = self.p, self.sems
        got, last = self.bufs
        self.second = {}
        for h in (0, 1):
            for k in NEAR:
                self.first[h, k].wait_recv()
            for i in range(4):
                own = self.src_at(0, p.y, i) if h == 0 else self.src_at(1, i, p.x)
                total = own[...].astype(F32)
                for k in NEAR:
                    total = total + got[h, k - 1, i].astype(F32)
                got[h, 0, i] = total.astype(BF16)
            for k in NEAR:
                to = p.at_x(k) if h == 0 else p.at_y(k)
                c = remote(got.at[h, 0, to], last.at[h, k - 1], s2.at[h, k], r2.at[h, k], p.peer(h, k))
                c.start()
                self.second[h, k] = c

    def result(self, h):
        p = self.p
        got, last = self.bufs
        for k in NEAR:
            self.second[h, k].wait_recv()
        total = got[h, 0, p.x if h == 0 else p.y].astype(F32)
        for k in NEAR:
            total = total + last[h, k - 1].astype(F32)
        return total

    def finish(self):
        for c in list(self.first.values()) + list(self.second.values()):
            c.wait_send()


class GatherDp:
    SEMS = [DMA((4,)), DMA((4,)), DMA((4,)), DMA((4,)), DMA]

    def __init__(self, place, src, dst, sems):
        self.p, self.src, self.dst, self.sems = place, src, dst, sems

    def start(self):
        p, (s1, r1, s2, r2, ls) = self.p, self.sems
        self.local = pltpu.make_async_copy(self.src, self.dst.at[p.dp], ls)
        self.local.start()
        self.first = {}
        for k in NEAR:
            c = remote(self.src, self.dst.at[p.dp], s1.at[k], r1.at[k], {"dp": p.zindex(k)})
            c.start()
            self.first[k] = c

    def forward(self):
        p, (s1, r1, s2, r2, ls) = self.p, self.sems
        self.second = []
        for j in (0,) + NEAR:
            if j:
                self.first[j].wait_recv()
            block = p.zindex(-j)
            src = self.src if j == 0 else self.dst.at[block]
            c = remote(src, self.dst.at[block], s2.at[j], r2.at[j], {"dp": p.mate()})
            c.start()
            self.second.append(c)

    def arrive(self):
        self.local.wait()
        for c in self.second:
            c.wait_recv()

    def finish(self):
        for c in list(self.first.values()) + self.second:
            c.wait_send()


class ReduceDp:
    SEMS = [DMA((4,)), DMA((4,)), DMA((4,)), DMA((4,))]

    @staticmethod
    def scratch(rows, cols):
        return [VM((4, rows, cols), BF16), VM((3, rows, cols), BF16)]

    def __init__(self, place, src, bufs, sems):
        self.p, self.src, self.bufs, self.sems = place, src, bufs, sems

    def copy(self, to, k):
        p, (s1, r1, s2, r2) = self.p, self.sems
        return remote(self.src.at[to, 1 - p.core], self.bufs[0].at[to], s1.at[k], r1.at[k], {"dp": p.mate()})

    def send(self, i):
        to = lax.rem(self.p.z + 1 + i, 4)
        self.copy(to, lax.rem(1 + i, 4)).start()

    def forward(self):
        p, (s1, r1, s2, r2) = self.p, self.sems
        got, last = self.bufs
        self.second = {}
        for k in (1, 2, 3, 0):
            to = p.at_z(k)
            self.copy(to, k).wait_recv()
            total = self.src[to, p.core].astype(F32) + got[to].astype(F32)
            got[to] = total.astype(BF16)
            if k:
                c = remote(got.at[to], last.at[k - 1], s2.at[k], r2.at[k], {"dp": p.zindex(k)})
                c.start()
                self.second[k] = c

    def result(self):
        got, last = self.bufs
        total = got[self.p.z].astype(F32)
        for k in NEAR:
            self.second[k].wait_recv()
            total = total + last[k - 1].astype(F32)
        return total

    def sent(self):
        for k in range(4):
            self.copy(self.p.at_z(k), k).wait_send()

    def finish(self):
        for c in self.second.values():
            c.wait_send()


def xy_peers(p):
    return [p.peer(axis, k) for axis in (0, 1) for k in NEAR]


def dp_peers(p):
    return [{"dp": p.dpindex(k)} for k in range(1, 8)]


def shape(dims, kind):
    return jax.ShapeDtypeStruct(dims, kind)


def call(phase, inputs, outs, scratch, cid, name):
    flat, where = [], {}
    for key, entry in scratch.items():
        entries = entry if isinstance(entry, list) else [entry]
        where[key] = (len(flat), len(entries), isinstance(entry, list))
        flat += entries

    def kernel(*refs):
        named = dict(zip(list(inputs) + list(outs), refs))
        tail = refs[len(inputs) + len(outs) :]
        for key, (start, count, many) in where.items():
            named[key] = list(tail[start : start + count]) if many else tail[start]
        phase(types.SimpleNamespace(**named))

    results = pl.pallas_call(
        kernel,
        out_shape=tuple(outs.values()),
        in_specs=[pl.BlockSpec(memory_space=VM)] * len(inputs),
        out_specs=tuple(pl.BlockSpec(memory_space=VM) for _ in outs),
        scratch_shapes=flat,
        name=name,
        compiler_params=pltpu.CompilerParams(
            collective_id=cid, has_side_effects=True, vmem_limit_bytes=63 << 20
        ),
    )(*inputs.values())
    return dict(zip(outs, results))


def dot(left, right):
    return jnp.dot(left, right, preferred_element_type=F32)


def dot_tn(left, right):
    return lax.dot_general(left, right, (((0,), (0,)), ((), ())), preferred_element_type=F32)


def dot_nt(left, right):
    return lax.dot_general(left, right, (((1,), (1,)), ((), ())), preferred_element_type=F32)


def rms_scale(values):
    return lax.rsqrt(jnp.mean(values * values, axis=-1, keepdims=True) + EPSILON)


def row_vector(ref, start):
    return jnp.concatenate([ref[start + i : start + i + 1, :] for i in range(7)], axis=1)


def store_rows(ref, start, vector):
    for i in range(vector.shape[1] // 128):
        ref[start + i : start + i + 1, :] = vector[:, 128 * i : 128 * i + 128]


def build_spread(ref):
    for part in range(7):
        source = lax.broadcasted_iota(jnp.int32, (128, DPAD), 0) + 128 * part
        column = lax.broadcasted_iota(jnp.int32, (128, DPAD), 1)
        inner = column & 7
        owner = ((column >> 3) & 3) * 2 + (column >> 9)
        wanted = (owner * 16 + ((column >> 5) & 15)) * 7 + inner
        ref[128 * part : 128 * part + 128, :] = jnp.where(
            (source == wanted) & (inner < 7), 1.0, 0.0
        ).astype(BF16)


def spread(values, matrix):
    return dot(values, matrix).astype(BF16)


def unspread(values, matrix):
    high = values.astype(BF16)
    low = (values - high.astype(F32)).astype(BF16)
    return dot_nt(high, matrix) + dot_nt(low, matrix)


def lanes(rows):
    return lax.broadcasted_iota(jnp.int32, (rows, 128), 1)


def half_turn(tile):
    first = (lanes(tile.shape[0]) & 63) < 32
    return jnp.where(first, pltpu.roll(tile, 96, 1), pltpu.roll(tile, 32, 1))


def rotate(tile, cosine, signed_sine):
    return tile * cosine + half_turn(tile) * signed_sine


def rotate_back(tile, cosine, signed_sine):
    return tile * cosine - half_turn(tile) * signed_sine


def scatter_heads(tile_of, dst):
    for mb in range(MB):
        for head in range(QUERY_HEADS):
            tile = tile_of(mb, head // 2)
            group = head // GROUP
            if head % 2 != group:
                tile = pltpu.roll(tile, 64, 1)
            tile = jnp.where((lanes(64) >= 64) == (group == 1), tile, 0.0)
            at = (head % 2) * 64
            dst[mb * 7 + head // 2, at : at + 64, :] = tile.astype(BF16)


def collect_heads(transposed, t):
    both = jnp.transpose(transposed)
    even, odd = both[:64], both[64:]
    even = jnp.where(t >= 4, pltpu.roll(even, 64, 1), even)
    odd = jnp.where(t <= 2, pltpu.roll(odd, 64, 1), odd)
    return jnp.where(lanes(64) < 64, even, odd)


def start_all(copies):
    for c in copies:
        c.start()
    return copies


def arrive_all(copies):
    for c in copies:
        c.wait_recv()


def sent_all(copies):
    for c in copies:
        c.wait_send()


class SmallSum:
    SCRATCH = [VM((3, 24, 128), F32), VM((3, 24, 128), F32), VM((7, 24, 128), F32), VM((2, 24, 128), F32)]
    SEMS = [DMA((3, 8)), DMA((3, 8))]

    def __init__(self, place, src, bufs, sems):
        self.p, self.src, self.bufs, self.sems = place, src, bufs, sems
        self.copies = []

    def start(self):
        p, (s, r) = self.p, self.sems
        self.x = start_all([remote(self.src, self.bufs[0].at[k - 1], s.at[0, k], r.at[0, k], p.xpeer(k)) for k in NEAR])

    def along_y(self):
        p, (s, r) = self.p, self.sems
        arrive_all(self.x)
        got, sums = self.bufs[0], self.bufs[3]
        sums[0] = self.src[...] + got[0] + got[1] + got[2]
        self.y = start_all(
            [remote(sums.at[0], self.bufs[1].at[k - 1], s.at[1, k], r.at[1, k], p.ypeer(k)) for k in NEAR]
        )

    def along_dp(self):
        p, (s, r) = self.p, self.sems
        arrive_all(self.y)
        got, sums = self.bufs[1], self.bufs[3]
        sums[1] = sums[0] + got[0] + got[1] + got[2]
        self.d = start_all(
            [
                remote(sums.at[1], self.bufs[2].at[k - 1], s.at[2, k], r.at[2, k], {"dp": p.dpindex(k)})
                for k in range(1, 8)
            ]
        )

    def result(self):
        arrive_all(self.d)
        total = self.bufs[3][1]
        for k in range(7):
            total = total + self.bufs[2][k]
        return total

    def finish(self):
        sent_all(self.x + self.y + self.d)


class ZSum:
    SEMS = [DMA((4,)), DMA((4,))]

    @staticmethod
    def scratch(cols):
        return [VM((4, 8, cols), F32), VM((4, 8, cols), F32)]

    def __init__(self, place, ring, bufs, sems):
        self.p, self.ring, self.bufs, self.sems = place, ring, bufs, sems

    def start(self):
        p, (s, r), (out, got) = self.p, self.sems, self.bufs
        for h in (0, 1):
            part = self.ring.result(h)
            out[2 * h], out[2 * h + 1] = part[:8], part[8:]
        self.copies = start_all(
            [remote(out.at[p.at_z(k)], got.at[p.z], s.at[k], r.at[k], {"dp": p.zindex(k)}) for k in NEAR]
        )
        got[p.z] = out[p.z]

    def result(self):
        arrive_all(self.copies)
        got = self.bufs[1]
        return got[0] + got[1] + got[2] + got[3]

    def finish(self):
        sent_all(self.copies)


def build_columns(big):
    for t in range(5):
        column = lax.broadcasted_iota(jnp.int32, (640, 128), 1) + 128 * t
        source = lax.broadcasted_iota(jnp.int32, (640, 128), 0)
        owner = (column * 1639) >> 16
        inner = column - owner * 40
        big[t, :640, :] = jnp.where((source == owner * 38 + inner) & (inner < 38), 1.0, 0.0).astype(BF16)


def columns_of(big):
    return jnp.concatenate([big[t, :640, :] for t in range(5)], axis=1)


def front(r, p):
    r.attn_src[...] = jnp.zeros_like(r.attn_src)
    r.stage[...] = jnp.zeros_like(r.stage)
    r.down[...] = jnp.zeros_like(r.down)
    r.down[:38, :] = r.w_down_own[...].astype(F32)
    r.attn_src[:7, :896] = r.w_query[...].astype(F32)
    r.attn_src[:7, 896:1024] = r.w_key[...].astype(F32)
    r.attn_src[:7, 1024:1152] = r.w_value[...].astype(F32)
    r.attn_src[:7, 1152:] = r.w_output[...].astype(F32)
    r.small[...] = jnp.zeros_like(r.small)
    me = p.dp * 16 + p.ctx
    flat = lax.broadcasted_iota(jnp.int32, (7, 128), 0) * 128 + lax.broadcasted_iota(jnp.int32, (7, 128), 1)
    for n in range(3):
        total = jnp.zeros((7, 128), F32)
        for i in range(7):
            value = r.vectors[0:1, 7 * n + i : 7 * n + i + 1]
            total = total + jnp.where(flat == me * 7 + i, value, 0.0)
        r.small[7 * n : 7 * n + 7, :] = total
    for n in range(2):
        value = r.vectors[0:1, 21 + n : 22 + n]
        r.small[21 + n : 22 + n, :] = jnp.where(flat[:1] == me, value, 0.0)
    barrier(xy_peers(p) + dp_peers(p))
    attn_copies = start_all(
        [remote(r.attn_src, r.attn_in.at[p.z], r.s_attn.at[k], r.r_attn.at[k], {"dp": p.zindex(k)}) for k in NEAR]
    )
    small = SmallSum(p, r.small, r.small_bufs, r.small_sems)
    small.start()
    place_copies = start_all(
        [remote(r.places, r.places_x.at[p.x], r.s_place.at[0, k], r.r_place.at[0, k], p.xpeer(k)) for k in NEAR]
    )
    r.attn_in[p.z] = r.attn_src[...]
    r.places_x[p.x] = r.places[...]
    build_columns(r.big)
    for n, ref in enumerate((r.w_gate, r.w_up)):
        whole = ref[...].astype(F32)
        for d in range(8):
            r.stage[8 * d : 8 * d + 7, :608] = whole[:, 608 * d : 608 * d + 608]
        wide = dot(r.stage[...].astype(BF16), columns_of(r.big))
        for d in range(8):
            r.gate_up[d, :, 640 * n : 640 * n + 640] = wide[8 * d : 8 * d + 8]
    gu_copies = []
    for k in range(1, 8):
        to = p.dpindex(k)
        gu_copies.append(
            remote(r.gate_up.at[to], r.gu_in.at[p.core, p.z], r.s_gu.at[k], r.r_gu.at[k], {"dp": to})
        )
    start_all(gu_copies)
    r.gu_in[p.core, p.z] = r.gate_up[p.dp]
    cots = GatherDp(p, r.cot, r.cot_all, r.cot_sems)
    cots.start()
    arrive_all(attn_copies)
    for h in (0, 1):
        pair = jnp.concatenate([r.attn_in[2 * h], r.attn_in[2 * h + 1]], axis=0).astype(BF16)
        r.qkv_block[h] = pair[:, :1152]
        r.o_block[h] = pair[:, 1152:]
    ring_qkv = GatherCtx(p, r.qkv_block, lambda b, h: r.w_qkv.at[p.core, b, h], r.qkv_sems, r.qkv_mate)
    ring_qkv.start()
    build_spread(r.spread)
    small.along_y()
    arrive_all(place_copies)
    place_copies2 = start_all(
        [remote(r.places_x, r.places_all.at[p.y], r.s_place.at[1, k], r.r_place.at[1, k], p.ypeer(k)) for k in NEAR]
    )
    r.places_all[p.y] = r.places_x[...]
    ring_qkv.forward()
    ring_o = GatherCtx(p, r.o_block, lambda b, h: r.w_o.at[p.core, b, h], r.o_sems, r.o_mate)
    ring_o.start()
    small.along_dp()
    arrive_all(gu_copies)
    for c in (0, 1):
        r.gu_block[c] = jnp.concatenate([r.gu_in[c, z] for z in range(4)], axis=0).astype(BF16)
    cots.forward()
    residual = r.hidden[...].astype(F32)
    unit_in = residual * rms_scale(residual)
    arrive_all(place_copies2)
    low_lane = lanes(8) < 64
    for c in range(8):
        a, b = r.places_all[(2 * c) // 4, (2 * c) % 4], r.places_all[(2 * c + 1) // 4, (2 * c + 1) % 4]
        r.key_row[:, 128 * c : 128 * c + 128] = jnp.where(low_lane, a, b)
    for mb in range(MB):
        key_places = jnp.transpose(jnp.broadcast_to(r.key_row[mb : mb + 1, :], (128, 1024)))
        r.masked[mb] = jnp.where(key_places <= r.places[mb : mb + 1, :], 0.0, -1e30).astype(BF16)
    r.small_all[...] = small.result()
    r.normed_in[...] = spread((unit_in * row_vector(r.small_all, 0)).astype(BF16), r.spread[...])
    bias_query = row_vector(r.small_all, 7)
    ring_qkv.arrive()
    ring_o.forward()
    cosine, sine = r.cosine[...], r.sine[...]
    lin = dot(r.normed_in[...], r.w_qkv[...].reshape(DPAD, 1152))
    keys = rotate(lin[:, 896:1024] + r.small_all[21:22, :], cosine, sine).astype(BF16)
    values = (lin[:, 1024:] + r.small_all[22:23, :]).astype(BF16)
    for mb in range(MB):
        r.kv[mb, :, :128] = keys[64 * mb : 64 * mb + 64]
        r.kv[mb, :, 128:] = values[64 * mb : 64 * mb + 64]
    ring_kv = GatherCtx(p, r.kv, lambda b, h: r.kv_all.at[h, b // 4, lax.rem(b, 4)], r.kv_sems)
    ring_kv.start()
    query_tiles = []
    for t in range(7):
        tile = lin[:, 128 * t : 128 * t + 128] + bias_query[:, 128 * t : 128 * t + 128]
        query_tiles.append((rotate(tile, cosine, sine).astype(BF16)).astype(F32) * (HEAD_SIZE**-0.5))
    scatter_heads(lambda mb, t: query_tiles[t][64 * mb : 64 * mb + 64], r.heads)
    ring_kv.forward()
    ring_gu = GatherCtx(p, r.gu_block, lambda b, h: r.w_gu.at[h, b], r.gu_sems)
    ring_gu.start()
    down_copies = start_all(
        [remote(r.down, r.down_in.at[p.x], r.s_down.at[0, k], r.r_down.at[0, k], p.xpeer(k)) for k in NEAR]
    )
    r.down_in[p.x] = r.down[...]
    ring_kv.arrive()
    for mb in range(MB):
        r.keys[mb] = r.kv_all[mb, :, :, :, :128].reshape(1024, 128)
        r.values[mb] = r.kv_all[mb, :, :, :, 128:].reshape(1024, 128)
        r.values_t[mb] = jnp.transpose(r.values[mb].astype(F32)).astype(BF16)

    def attend(mb):
        def step(t, carry):
            i = mb * 7 + t
            scores = dot_nt(r.keys[mb], r.heads[i]) + r.masked[mb].astype(F32)
            expo = jnp.exp(scores - jnp.max(scores, axis=0, keepdims=True))
            probs = (expo * (1.0 / jnp.sum(expo, axis=0, keepdims=True))).astype(BF16)
            r.probs[i] = probs
            r.attended[i] = collect_heads(dot(r.values_t[mb], probs), t).astype(BF16)
            return carry

        lax.fori_loop(0, 7, step, 0)

    attend(0)
    ring_gu.forward()
    arrive_all(down_copies)
    own_down = r.w_down.at[pl.ds(pl.multiple_of(160 * p.y, 32), 160)]
    own_down[...] = jnp.concatenate([r.down_in[i] for i in range(4)], axis=0).astype(BF16)
    down_copies2 = start_all(
        [remote(own_down, own_down, r.s_down.at[1, k], r.r_down.at[1, k], p.ypeer(k)) for k in NEAR]
    )
    attend(1)
    attended = jnp.concatenate(
        [jnp.concatenate([r.attended[mb * 7 + t] for t in range(7)], axis=1) for mb in range(MB)], axis=0
    )
    r.attended_wide[...] = spread(attended, r.spread[...])
    ring_o.arrive()
    mixed = residual + dot(r.attended_wide[...], r.w_o[...].reshape(DPAD, D))
    r.mixed[...] = mixed
    unit_mid = mixed * rms_scale(mixed)
    r.normed_mid[...] = spread((unit_mid * row_vector(r.small_all, 14)).astype(BF16), r.spread[...])
    ring_mid = GatherDp(p, r.normed_mid, r.normed_all, r.mid_sems)
    ring_mid.start()
    ring_gu.arrive()
    arrive_all(down_copies2)
    cots.arrive()
    ring_mid.forward()
    for ring in (ring_qkv, ring_o, ring_kv, ring_gu, cots, small):
        ring.finish()
    sent_all(attn_copies + gu_copies + place_copies + place_copies2 + down_copies + down_copies2)
    ring_mid.arrive()
    ring_mid.finish()


FRONT_SCRATCH = {
    "attn_src": VM((8, 2048), F32),
    "stage": VM((64, 640), F32),
    "gate_up": VM((8, 8, 1280), F32),
    "down": VM((40, D), F32),
    "small": VM((24, 128), F32),
    "attn_in": VM((4, 8, 2048), F32),
    "gu_in": VM((2, 4, 8, 1280), F32),
    "down_in": VM((4, 40, D), F32),
    "places_x": VM((4, 8, 128), F32),
    "places_all": VM((4, 4, 8, 128), F32),
    "key_row": VM((8, 1024), F32),
    "masked": VM((2, 1024, 128), BF16),
    "qkv_block": VM((2, 16, 1152), BF16),
    "o_block": VM((2, 16, D), BF16),
    "gu_block": VM((2, 32, 1280), BF16),
    "kv": VM((2, 64, 256), BF16),
    "kv_all": VM((2, 4, 4, 64, 256), BF16),
    "values_t": VM((2, 128, 1024), BF16),
    "attended": VM((14, 64, 128), BF16),
    "normed_mid": VM((128, DPAD), BF16),
    "w_qkv": VM((2, 16, 2, 16, 1152), BF16),
    "w_o": VM((2, 16, 2, 16, D), BF16),
    "w_gu": VM((2, 16, 32, 1280), BF16),
    "w_down": VM((640, D), BF16),
    "small_all": VM((24, 128), F32),
    "cot_all": VM((8, 128, D), BF16),
    "normed_all": VM((8, 128, DPAD), BF16),
    "probs": VM((14, 1024, 128), BF16),
    "heads": VM((14, 128, 128), BF16),
    "keys": VM((2, 1024, 128), BF16),
    "values": VM((2, 1024, 128), BF16),
    "attended_wide": VM((128, DPAD), BF16),
    "normed_in": VM((128, DPAD), BF16),
    "mixed": VM((128, D), F32),
    "spread": VM((D, DPAD), BF16),
    "small_bufs": SmallSum.SCRATCH,
    "small_sems": SmallSum.SEMS,
    "s_attn": DMA((4,)), "r_attn": DMA((4,)), "s_gu": DMA((8,)), "r_gu": DMA((8,)),
    "s_place": DMA((2, 4)), "r_place": DMA((2, 4)), "s_down": DMA((2, 4)), "r_down": DMA((2, 4)),
    "qkv_sems": GatherCtx.SEMS, "qkv_mate": GatherCtx.MATE, "o_sems": GatherCtx.SEMS, "o_mate": GatherCtx.MATE,
    "kv_sems": GatherCtx.SEMS, "gu_sems": GatherCtx.SEMS, "cot_sems": GatherDp.SEMS, "mid_sems": GatherDp.SEMS,
}


def back(r, p):
    red_normed = ReduceDp(p, r.part_normed, r.normed_bufs, r.normed_sems)
    red_out = ReduceDp(p, r.part_normed.at[:, :, :, pl.ds(0, D)], r.out_bufs, r.out_sems)

    def rows_of(ref, to):
        return ref[pl.ds(2 * to, 2)].reshape(256, ref.shape[-1])

    def feed(i, carry):
        to = lax.rem(p.z + 1 + i, 4)
        at = pl.ds(pl.multiple_of(256 * to, 256), 256)
        lin = dot(rows_of(r.normed_all, to), r.w_gu[...].reshape(DPAD, 1280))
        gate, up = lin[:, :640], lin[:, 640:]
        sig = 1.0 / (1.0 + jnp.exp(-gate))
        silu = gate * sig
        hidden = (silu * up).astype(BF16)
        back_hidden = dot_nt(rows_of(r.cot_all, to), r.w_down[...]).astype(BF16).astype(F32)
        grad_gate = (back_hidden * up * sig * (1.0 + gate * (1.0 - sig))).astype(BF16)
        grad_up = (back_hidden * silu).astype(BF16)
        for t in range(5):
            r.big[t, at, :] = grad_gate[:, 128 * t : 128 * t + 128]
            r.big[5 + t, at, :] = grad_up[:, 128 * t : 128 * t + 128]
            r.big[10 + t, at, :] = hidden[:, 128 * t : 128 * t + 128]
        part = dot_nt(jnp.concatenate([grad_gate, grad_up], axis=1), r.w_gu[...].reshape(DPAD, 1280))
        r.part_normed[to] = part.astype(BF16).reshape(2, 128, DPAD)
        red_normed.send(i)
        return carry

    lax.fori_loop(0, 4, feed, 0)
    red_normed.forward()

    def project(i, carry):
        to = lax.rem(p.z + 1 + i, 4)
        at = pl.ds(pl.multiple_of(256 * to, 256), 256)
        hidden = jnp.concatenate([r.big[10 + t, at, :] for t in range(5)], axis=1)
        r.part_normed[to, :, :, :D] = dot(hidden, r.w_down[...]).astype(BF16).reshape(2, 128, D)
        red_out.send(i)
        return carry

    def grad_gate_up(i, carry):
        at = pl.ds(pl.multiple_of(256 * i, 256), 256)
        left = r.normed_all[:, :, at].reshape(1024, 256)
        right = jnp.concatenate([r.big[t] for t in range(10)], axis=1)
        part = dot_tn(left, right).astype(BF16).reshape(2, 4, 32, 1280)
        r.g_gu[i // 2, pl.ds(2 * lax.rem(i, 2), 2)] = part
        return carry

    lax.fori_loop(0, 4, grad_gate_up, 0)
    ring_gu = ReduceCtx(p, lambda h, y, x: r.g_gu.at[h, y, x], r.gu_bufs, r.gu_red_sems)
    ring_gu.start()

    def grad_down(t, carry):
        at = pl.ds(pl.multiple_of(128 * t, 128), 128)
        r.g_down[at, :] = dot_tn(r.big[10 + t], r.cot_all[...].reshape(1024, D)).astype(BF16)
        return carry

    lax.fori_loop(0, 5, grad_down, 0)
    down_copies = start_all(
        [
            remote(
                r.g_down.at[pl.ds(pl.multiple_of(160 * p.at_y(k), 32), 160)],
                r.down_y.at[k - 1], r.s_gdown.at[0, k], r.r_gdown.at[0, k], p.ypeer(k),
            )
            for k in NEAR
        ]
    )
    red_normed.sent()
    lax.fori_loop(0, 4, project, 0)
    gain_mlp = row_vector(r.small_all, 14)
    mixed = r.mixed[...]
    inv_mid = rms_scale(mixed)
    unit_mid = mixed * inv_mid
    r.held[...] = unspread(red_normed.result(), r.spread[...])
    grad_normed = r.held[...]
    store_rows(r.small_grads, 14, jnp.sum(grad_normed * unit_mid, axis=0, keepdims=True))
    scaled = grad_normed * gain_mlp
    r.grad_mixed[...] = r.cot[...].astype(F32) + inv_mid * (
        scaled - unit_mid * jnp.mean(scaled * unit_mid, axis=-1, keepdims=True)
    )
    r.low_b[...] = r.grad_mixed[...].astype(BF16)
    wide = dot_nt(r.low_b[...], r.w_o[...].reshape(DPAD, D)).astype(BF16)
    r.held[...] = dot_nt(wide, r.spread[...])
    scatter_heads(lambda mb, t: r.held[64 * mb : 64 * mb + 64, 128 * t : 128 * t + 128], r.grad_heads)
    for mb in range(MB):
        r.values_t[mb] = jnp.transpose(r.keys[mb].astype(F32)).astype(BF16)
    red_out.forward()

    def attend_back(mb):
        def step(t, carry):
            i = mb * 7 + t
            grad_probs = dot_nt(r.values[mb], r.grad_heads[i])
            probs = r.probs[i].astype(F32)
            weighted = probs * grad_probs
            inner = jnp.sum(weighted, axis=0, keepdims=True)
            grad_scores = (weighted - probs * inner).astype(BF16)
            r.big[i] = grad_scores
            r.grad_query[i] = collect_heads(dot(r.values_t[mb], grad_scores), t)
            return carry

        lax.fori_loop(0, 7, step, 0)

    def grad_key_value(i, carry):
        mb, y = i // 4, lax.rem(i, 4)
        at = pl.ds(pl.multiple_of(256 * y, 256), 256)
        scores = jnp.concatenate([r.big[mb * 7 + t, at, :] for t in range(7)], axis=1)
        probs = jnp.concatenate([r.probs[mb * 7 + t, at, :] for t in range(7)], axis=1)
        grad_keys = dot(scores, r.heads[pl.ds(7 * mb, 7)].reshape(896, 128))
        grad_values = dot(probs, r.grad_heads[pl.ds(7 * mb, 7)].reshape(896, 128))
        r.kv_all[mb, y, :, :, :128] = grad_keys.astype(BF16).reshape(4, 64, 128)
        r.kv_all[mb, y, :, :, 128:] = grad_values.astype(BF16).reshape(4, 64, 128)
        return carry

    attend_back(0)
    attend_back(1)
    lax.fori_loop(0, 8, grad_key_value, 0)

    ring_kv = ReduceCtx(p, lambda h, y, x: r.kv_all.at[h, y, x], r.kv_bufs, r.kv_red_sems)
    ring_kv.start()

    def weight_gradient(left, right, out):
        def step(i, carry):
            at = pl.ds(pl.multiple_of(256 * i, 256), 256)
            part = dot_tn(left[:, at], right[...]).astype(BF16)
            out[i // 2, pl.ds(2 * lax.rem(i, 2), 2)] = part.reshape(2, 4, 2, 16, part.shape[-1])
            return carry

        lax.fori_loop(0, 4, step, 0)

    def to_mate(n, grads, got):
        c = remote(grads.at[1 - p.core], got, r.s_mate.at[n], r.r_mate.at[n], {"dp": p.mate()})
        c.start()
        return c

    def with_mate(c, grads, got):
        c.wait_recv()
        for y in range(4):
            got[y] = (grads[p.core, y].astype(F32) + got[y].astype(F32)).astype(BF16)

    weight_gradient(r.attended_wide, r.low_b, r.g_wo)
    mate_wo = to_mate(0, r.g_wo, r.m_wo)
    cosine, sine = r.cosine[...], r.sine[...]
    for t in range(7):
        tile = jnp.concatenate([r.grad_query[t], r.grad_query[7 + t]], axis=0) * (HEAD_SIZE**-0.5)
        r.low_a[:, 128 * t : 128 * t + 128] = rotate_back(tile, cosine, sine).astype(BF16)
    weight_gradient(r.normed_in, r.low_a, r.g_wq)
    mate_wq = to_mate(1, r.g_wq, r.m_wq)
    ring_gu.forward()
    ring_kv.forward()
    with_mate(mate_wo, r.g_wo, r.m_wo)
    ring_wo = ReduceCtx(p, lambda h, y, x: r.m_wo.at[y, x, h], r.wo_bufs, r.wo_sems)
    ring_wo.start()
    with_mate(mate_wq, r.g_wq, r.m_wq)
    ring_wq = ReduceCtx(p, lambda h, y, x: r.m_wq.at[y, x, h], r.wq_bufs, r.wq_sems)
    ring_wq.start()
    store_rows(r.small_grads, 7, jnp.sum(r.low_a[...].astype(F32), axis=0, keepdims=True))
    kv_sum = jnp.concatenate([ring_kv.result(0), ring_kv.result(1)], axis=0)
    grad_key = rotate_back(kv_sum[:, :128], cosine, sine).astype(BF16)
    r.low_kv[:, :128] = grad_key
    r.low_kv[:, 128:] = kv_sum[:, 128:].astype(BF16)
    weight_gradient(r.normed_in, r.low_kv, r.g_wkv)
    mate_wkv = to_mate(2, r.g_wkv, r.m_wkv)
    bias_kv = jnp.sum(r.low_kv[...].astype(F32), axis=0, keepdims=True)
    store_rows(r.small_grads, 21, bias_kv)
    r.small_grads[23:24, :] = jnp.zeros((1, 128), F32)
    lowered = jnp.concatenate([r.low_a[...], r.low_kv[...]], axis=1)
    r.held[...] = unspread(dot_nt(lowered, r.w_qkv[...].reshape(DPAD, 1152)), r.spread[...])
    residual = r.hidden[...].astype(F32)
    inv_rms = rms_scale(residual)
    unit_in = residual * inv_rms
    store_rows(r.small_grads, 0, jnp.sum(r.held[...] * unit_in, axis=0, keepdims=True))
    small = SmallSum(p, r.small_grads, r.small_bufs2, r.small_sems2)
    small.start()
    with_mate(mate_wkv, r.g_wkv, r.m_wkv)
    ring_wkv = ReduceCtx(p, lambda h, y, x: r.m_wkv.at[y, x, h], r.wkv_bufs, r.wkv_sems)
    ring_wkv.start()
    arrive_all(down_copies)
    total = r.g_down[pl.ds(pl.multiple_of(160 * p.y, 32), 160), :].astype(F32)
    for k in NEAR:
        total = total + r.down_y[k - 1].astype(F32)
    for i in range(4):
        r.down_mid[i] = total[40 * i : 40 * i + 40]
    down_copies2 = start_all(
        [
            remote(r.down_mid.at[p.at_x(k)], r.down_x.at[k - 1], r.s_gdown.at[1, k], r.r_gdown.at[1, k], p.xpeer(k))
            for k in NEAR
        ]
    )
    for h in (0, 1):
        part = ring_gu.result(h)
        for z in range(4):
            r.gu_out[z, h] = part[8 * z : 8 * z + 8]
    gu_copies = []
    for k in range(1, 8):
        to = p.dpindex(k)
        gu_copies.append(
            remote(
                r.gu_out.at[to // 2, lax.rem(to, 2)], r.gu_got.at[p.dp], r.s_ggu.at[k], r.r_ggu.at[k], {"dp": to}
            )
        )
    start_all(gu_copies)
    r.gu_got[p.dp] = r.gu_out[p.z, p.core]
    ring_wo.forward()
    ring_wq.forward()
    small.along_y()
    ring_wkv.forward()
    scaled = r.held[...] * row_vector(r.small_all, 0)
    r.grad_in[...] = r.grad_mixed[...] + inv_rms * (
        scaled - unit_in * jnp.mean(scaled * unit_in, axis=-1, keepdims=True)
    )
    r.layer_out[...] = (mixed + red_out.result()).astype(BF16)
    small.along_dp()
    sum_wo = ZSum(p, ring_wo, r.zo_bufs, r.zo_sems)
    sum_wo.start()
    sum_wq = ZSum(p, ring_wq, r.zq_bufs, r.zq_sems)
    sum_wq.start()
    sum_wkv = ZSum(p, ring_wkv, r.zkv_bufs, r.zkv_sems)
    sum_wkv.start()
    build_columns(r.big)
    arrive_all(gu_copies)
    for n, out in enumerate((r.o_gate, r.o_up)):
        for d in range(8):
            r.stage[8 * d : 8 * d + 8, :] = r.gu_got[d, :, 640 * n : 640 * n + 640]
        wide = r.stage[...]
        high = wide.astype(BF16)
        low = (wide - high.astype(F32)).astype(BF16)
        packed = dot_nt(high, columns_of(r.big)) + dot_nt(low, columns_of(r.big))
        for d in range(8):
            out[:, 608 * d : 608 * d + 608] = packed[8 * d : 8 * d + 7, :608]
    arrive_all(down_copies2)
    final = r.down_mid[p.x] + r.down_x[0] + r.down_x[1] + r.down_x[2]
    r.o_down[...] = final[:38]
    r.o_output[...] = sum_wo.result()[:7]
    r.o_query[...] = sum_wq.result()[:7]
    part = sum_wkv.result()
    r.o_key[...] = part[:7, :128]
    r.o_value[...] = part[:7, 128:]
    total = small.result()
    r.o_small[...] = total
    me = p.dp * 16 + p.ctx
    flat = lax.broadcasted_iota(jnp.int32, (7, 128), 0) * 128 + lax.broadcasted_iota(jnp.int32, (7, 128), 1)
    lane = lax.broadcasted_iota(jnp.int32, (1, 128), 1)

    def pick(block, where):
        return jnp.sum(jnp.sum(jnp.where(where, block, 0.0), axis=0, keepdims=True), axis=1, keepdims=True)

    r.o_mine[...] = jnp.zeros_like(r.o_mine)
    for n in range(3):
        row = jnp.zeros((1, 128), F32)
        for i in range(7):
            row = row + jnp.where(lane == i, pick(total[7 * n : 7 * n + 7], flat == me * 7 + i), 0.0)
        r.o_mine[n : n + 1, :] = row
    r.o_mine[3:4, :] = jnp.broadcast_to(pick(total[22:23], lane == me), (1, 128))
    red_out.sent()
    for ring in (red_normed, red_out, ring_gu, ring_kv, ring_wo, ring_wq, ring_wkv, small, sum_wo, sum_wq, sum_wkv):
        ring.finish()
    sent_all([mate_wo, mate_wq, mate_wkv] + down_copies + down_copies2 + gu_copies)


LAYER_OUTS = {
    "layer_out": shape((128, D), BF16),
    "grad_in": shape((128, D), F32),
    "o_query": shape((7, D), F32),
    "o_key": shape((7, 128), F32),
    "o_value": shape((7, 128), F32),
    "o_output": shape((7, D), F32),
    "o_gate": shape((7, 4864), F32),
    "o_up": shape((7, 4864), F32),
    "o_down": shape((38, D), F32),
    "o_small": shape((24, 128), F32),
    "o_mine": shape((8, 128), F32),
}
BACK_SCRATCH = {
    "big": VM((15, 1024, 128), BF16),
    "part_normed": VM((4, 2, 128, DPAD), BF16),
    "normed_bufs": ReduceDp.scratch(128, DPAD), "normed_sems": ReduceDp.SEMS,
    "out_bufs": ReduceDp.scratch(128, D), "out_sems": ReduceDp.SEMS,
    "g_gu": VM((2, 4, 4, 32, 1280), BF16),
    "gu_bufs": ReduceCtx.scratch(32, 1280), "gu_red_sems": ReduceCtx.SEMS,
    "g_down": VM((640, D), BF16),
    "down_y": VM((3, 160, D), BF16), "down_mid": VM((4, 40, D), F32), "down_x": VM((3, 40, D), F32),
    "grad_mixed": VM((128, D), F32),
    "held": VM((128, D), F32),
    "low_a": VM((128, D), BF16),
    "low_b": VM((128, D), BF16),
    "low_kv": VM((128, 256), BF16),
    "grad_heads": VM((14, 128, 128), BF16),
    "grad_query": VM((14, 64, 128), F32),
    "kv_bufs": ReduceCtx.scratch(64, 256), "kv_red_sems": ReduceCtx.SEMS,
    "g_wo": VM((2, 4, 4, 2, 16, D), BF16), "m_wo": VM((4, 4, 2, 16, D), BF16),
    "g_wq": VM((2, 4, 4, 2, 16, D), BF16), "m_wq": VM((4, 4, 2, 16, D), BF16),
    "g_wkv": VM((2, 4, 4, 2, 16, 256), BF16), "m_wkv": VM((4, 4, 2, 16, 256), BF16),
    "wo_bufs": ReduceCtx.scratch(16, D), "wo_sems": ReduceCtx.SEMS,
    "wq_bufs": ReduceCtx.scratch(16, D), "wq_sems": ReduceCtx.SEMS,
    "wkv_bufs": ReduceCtx.scratch(16, 256), "wkv_sems": ReduceCtx.SEMS,
    "zo_bufs": ZSum.scratch(D), "zo_sems": ZSum.SEMS,
    "zq_bufs": ZSum.scratch(D), "zq_sems": ZSum.SEMS,
    "zkv_bufs": ZSum.scratch(256), "zkv_sems": ZSum.SEMS,
    "small_grads": VM((24, 128), F32),
    "small_bufs2": SmallSum.SCRATCH, "small_sems2": SmallSum.SEMS,
    "gu_out": VM((4, 2, 8, 1280), F32), "gu_got": VM((8, 8, 1280), F32),
    "s_mate": DMA((3,)), "r_mate": DMA((3,)), "s_gdown": DMA((2, 4)), "r_gdown": DMA((2, 4)),
    "s_ggu": DMA((8,)), "r_ggu": DMA((8,)),
}


def layer(r):
    p = Place()
    front(r, p)
    back(r, p)


def body(
    hidden_in, positions, norm_attn, w_query, b_query, w_key, b_key, value_weight, value_bias, w_output,
    norm_mlp, w_gate, w_up, w_down, cotangent,
):
    rows = MB * 64
    places = positions[:, 0]
    freqs = THETA_BASE ** (-jnp.arange(0, HEAD_SIZE, 2).astype(F32) / HEAD_SIZE)
    angles = places.reshape(rows).astype(F32)[:, None] * jnp.tile(freqs, 4)[None, :]
    sign = jnp.tile(jnp.repeat(jnp.array([-1.0, 1.0], F32), HEAD_SIZE // 2), 2)
    vectors = jnp.concatenate([norm_attn, b_query, norm_mlp, b_key, value_bias]).astype(F32)
    inputs = {
        "hidden": hidden_in.reshape(rows, D),
        "cot": cotangent.reshape(rows, D),
        "cosine": jnp.cos(angles),
        "sine": jnp.sin(angles) * sign,
        "w_query": w_query, "w_key": w_key, "w_value": value_weight, "w_output": w_output,
        "w_gate": w_gate, "w_up": w_up, "w_down_own": w_down,
        "vectors": jnp.pad(vectors, (0, 105))[None],
        "places": jnp.pad(jnp.tile(places.astype(F32), (1, 2)), ((0, 6), (0, 0))),
    }
    done = call(layer, inputs, LAYER_OUTS, {**FRONT_SCRATCH, **BACK_SCRATCH}, 0, "layer")
    mine = done["o_mine"]
    return (
        done["layer_out"].reshape(MB, 1, 64, D),
        done["grad_in"].reshape(MB, 1, 64, D),
        mine[0, :7],
        done["o_query"],
        mine[1, :7],
        done["o_key"],
        done["o_small"][21],
        done["o_value"],
        mine[3, :1],
        done["o_output"],
        mine[2, :7],
        done["o_gate"],
        done["o_up"],
        done["o_down"],
    )


def solution(mesh):
    rows = P(("dp", "ctx"), None)
    vector = P(("dp", "ctx"))
    tokens = P(None, "dp", "ctx", None)
    in_specs = (
        tokens, P(None, "dp", "ctx"), vector, rows, vector, rows, vector, rows, vector, rows, vector,
        rows, rows, rows, tokens,
    )
    out_specs = (
        tokens, tokens, vector, rows, vector, rows, P(), rows, vector, rows, vector, rows, rows, rows,
    )
    return jax.shard_map(body, mesh=mesh, in_specs=in_specs, out_specs=out_specs, check_vma=False)
```

time: 221 us -> 188 us (0.85)
  Pallas kernels: 195 us -> 170 us
  other arithmetic: 6.71 us -> 1.52 us
  local copies, waits for them, and re-layouts: 17 us -> 13.6 us
    pallas_call x2 -> x1, Pallas kernels: 195 us -> 170 us  [call(): pl.pallas_call(kernel, out_shape=tuple(outs.values()), in_specs=[pl.Block...]
    reshape x13 -> x0, local copies, waits for them, and re-layouts: 6.61 us -> none  [the longest x2 2.93 us: slices(): parts = w.astype(F32).reshape(7, 8, 16, 38)]
    unnamed x22 -> x35, local copies, waits for them, and re-layouts: 2.18 us -> 8.76 us
    dynamic_slice x2 -> x0, local copies, waits for them, and re-layouts: 2.66 us -> none  [take(): return lax.dynamic_slice(sums, (start + me * width,), (width,))]
where the time goes in v3:
time: 188 us; the launch traced here: 187 us
  Pallas kernels  170 us (90%)
  local copies, waits for them, and re-layouts  13.6 us (7%)
  between operations  2.08 us (1%)
    pallas_call x1, Pallas kernels, call(): pl.pallas_call(kernel, out_shape=tuple(outs.values()), in_specs=[pl.Block...  170 us
    unnamed x35, local copies, waits for them, and re-layouts  8.76 us

profile of v3, /device:TPU:1, one launch (start us, length us, event | category | flops | bytes accessed | tf_op | source)
XLA Modules:
  0.0 187.4 jit_solution(4309524097755662073)
XLA Ops:
  0.7 0.0 copy-start.12
  0.7 0.1 mul.38
  0.8 0.6 copy-done.12
  1.3 0.1 broadcast_in_dim.9
  1.4 0.1 tile.11
  1.5 0.0 copy-start.8
  1.5 0.1 mul.41
  1.6 0.6 copy-done.8
  2.2 0.1 convert_element_type.31
  2.3 1.0 fusion
  3.2 0.1 tile.26
  3.3 0.6 pad.10.refs_12_
  4.6 0.0 copy-start.9
  4.6 0.0 copy-start.10
  4.6 0.0 copy-start.11
  5.3 0.0 copy-done.9
  5.3 0.0 copy-done.10
  5.3 0.0 copy-done.11
  5.3 0.1 concatenate.3
  5.4 0.5 bitcast_convert_fusion.refs_11_
  6.0 170.1 %layer.1 = (bf16[128,896]{1,0:T(8,128)(2,1)}, f32[128,896]{1,0:T(8,128)}, f32[7,896]{1,0:T(8,128)}, f32[7,128]{1,0:T(8,128)}, f32[7,128]{1,0:T(8,128)}, /*index=...) custom-call(bf16[128,896]{1,0:T(8,128)(2,1)} %bitcast.23, ...), custom_call_target="tpu_custom_call" | custom-call | tf_op jit(solution)/shard_map/layer/pallas_call | solution.py:316
  176.1 0.0 copy-start
  176.1 1.3 slice_bitcast_fusion
  177.4 1.2 slice.18
  178.6 1.2 slice_bitcast_fusion.1
  179.8 1.6 copy.43
  181.4 0.0 copy-done
  181.4 0.0 copy-start.5
  181.4 0.0 copy-start.2
  181.4 0.8 copy.44
  182.2 0.0 copy-done.5
  182.2 0.0 copy-start.7
  182.2 0.0 copy-start.4
  182.2 0.6 copy.45
  182.8 0.1 copy-done.7
  182.9 0.0 copy-start.6
  182.9 0.6 copy.46
  183.5 0.1 copy-done.6
  183.5 0.6 copy.47
  184.1 0.0 copy-done.4
  184.1 0.6 copy.48
  184.8 0.0 copy-done.2
  184.8 0.0 copy-start.1
  184.8 0.7 copy.49
  185.4 0.3 copy-done.1
  185.7 0.7 copy.50
  186.4 0.3 copy-done.3
  186.7 0.7 copy.51
  (7 shorter events, 0.0 us)
Async XLA Ops:
  0.7 0.7 copy-start.12
  1.5 0.7 copy-start.8
  4.6 0.7 copy-start.9
  4.6 0.7 copy-start.10
  4.6 0.7 copy-start.11
  176.1 5.3 %copy-start = (f32[128,896]{1,0:T(8,128)S(1)}, f32[128,896]{1,0:T(8,128)}, u32[]{:S(2)}) copy-start(f32[128,896]{1,0:T(8,128)} %get-tuple-element.26) | copy-start | bytes 1376260
  181.4 0.8 copy-start.5
  181.4 3.3 %copy-start.2 = (f32[7,4864]{1,0:T(8,128)S(1)}, f32[7,4864]{1,0:T(8,128)}, u32[]{:S(2)}) copy-start(f32[7,4864]{1,0:T(8,128)} %get-tuple-element.80) | copy-start | bytes 408580
  182.2 0.7 copy-start.7
  182.2 2.0 %copy-start.4 = (f32[7,896]{1,0:T(8,128)S(1)}, f32[7,896]{1,0:T(8,128)}, u32[]{:S(2)}) copy-start(f32[7,896]{1,0:T(8,128)} %get-tuple-element.78) | copy-start | bytes 75268
  182.9 0.7 copy-start.6
  184.8 1.0 copy-start.1
  185.7 1.0 copy-start.3

commit v4 on v3

--- a/solution.py
+++ b/solution.py
@@ -1,3 +1,4 @@
+import math
 import types
 
 import jax
@@ -29,11 +30,14 @@
     )
 
 
-def barrier(peers):
+def greet(peers):
     sem = pltpu.get_barrier_semaphore()
     for peer in peers:
         pl.semaphore_signal(sem, inc=1, device_id=peer, device_id_type=MESH)
-    pl.semaphore_wait(sem, len(peers))
+
+
+def meet(peers):
+    pl.semaphore_wait(pltpu.get_barrier_semaphore(), len(peers))
 
 
 class Place:
@@ -153,14 +157,14 @@
 
     def __init__(self, place, src_at, bufs, sems):
         self.p, self.src_at, self.bufs, self.sems = place, src_at, bufs, sems
-
-    def start(self):
+        self.first = {}
+
+    def start(self, halves=(0, 1)):
         p, (s1, r1, s2, r2) = self.p, self.sems
         got = self.bufs[0]
         every = slice(None)
-        self.first = {}
         for k in NEAR:
-            for h in (0, 1):
+            for h in halves:
                 src = self.src_at(0, p.at_y(k), every) if h == 0 else self.src_at(1, every, p.at_x(k))
                 c = remote(src, got.at[h, k - 1], s1.at[h, k], r1.at[h, k], p.peer(1 - h, k))
                 c.start()
@@ -203,38 +207,48 @@
 class GatherDp:
     SEMS = [DMA((4,)), DMA((4,)), DMA((4,)), DMA((4,)), DMA]
 
-    def __init__(self, place, src, dst, sems):
-        self.p, self.src, self.dst, self.sems = place, src, dst, sems
+    def __init__(self, place, src, dst_at, sems):
+        self.p, self.src, self.dst_at, self.sems = place, src, dst_at, sems
+        rows = src.shape[0]
+        self.halves = {1: pl.ds(0, rows // 2), 3: pl.ds(rows // 2, rows // 2)}
 
     def start(self):
         p, (s1, r1, s2, r2, ls) = self.p, self.sems
-        self.local = pltpu.make_async_copy(self.src, self.dst.at[p.dp], ls)
+        self.local = pltpu.make_async_copy(self.src, self.dst_at(p.dp), ls)
         self.local.start()
-        self.first = {}
-        for k in NEAR:
-            c = remote(self.src, self.dst.at[p.dp], s1.at[k], r1.at[k], {"dp": p.zindex(k)})
+        self.first, self.second, self.relayed = {}, {}, {}
+        for k in (1, 3):
+            c = remote(self.src, self.dst_at(p.dp), s1.at[k], r1.at[k], {"dp": p.zindex(k)})
             c.start()
             self.first[k] = c
 
-    def forward(self):
+    def relay(self):
         p, (s1, r1, s2, r2, ls) = self.p, self.sems
-        self.second = []
-        for j in (0,) + NEAR:
-            if j:
-                self.first[j].wait_recv()
-            block = p.zindex(-j)
-            src = self.src if j == 0 else self.dst.at[block]
-            c = remote(src, self.dst.at[block], s2.at[j], r2.at[j], {"dp": p.mate()})
+        for k in (1, 3):
+            self.first[k].wait_recv()
+            part = self.dst_at(p.zindex(-k)).at[self.halves[k]]
+            c = remote(part, part, s1.at[k - 1], r1.at[k - 1], {"dp": p.zindex(k)})
             c.start()
-            self.second.append(c)
-
-    def arrive(self):
-        self.local.wait()
-        for c in self.second:
-            c.wait_recv()
+            self.relayed[k] = c
+
+    def forward(self, j):
+        p, (s1, r1, s2, r2, ls) = self.p, self.sems
+        if j == 2:
+            for c in self.relayed.values():
+                c.wait_recv()
+        block = p.zindex(-j)
+        src = self.dst_at(block) if j else self.src
+        c = remote(src, self.dst_at(block), s2.at[j], r2.at[j], {"dp": p.mate()})
+        c.start()
+        self.second[j] = c
+
+    def arrive(self, j):
+        if j == 0:
+            self.local.wait()
+        self.second[j].wait_recv()
 
     def finish(self):
-        for c in list(self.first.values()) + self.second:
+        for c in list(self.first.values()) + list(self.second.values()) + list(self.relayed.values()):
             c.wait_send()
 
 
@@ -247,28 +261,26 @@
 
     def __init__(self, place, src, bufs, sems):
         self.p, self.src, self.bufs, self.sems = place, src, bufs, sems
-
-    def copy(self, to, k):
+        self.first, self.second = {}, {}
+
+    def send(self, k):
         p, (s1, r1, s2, r2) = self.p, self.sems
-        return remote(self.src.at[to, 1 - p.core], self.bufs[0].at[to], s1.at[k], r1.at[k], {"dp": p.mate()})
-
-    def send(self, i):
-        to = lax.rem(self.p.z + 1 + i, 4)
-        self.copy(to, lax.rem(1 + i, 4)).start()
-
-    def forward(self):
+        to = p.at_z(k)
+        c = remote(self.src.at[to, 1 - p.core], self.bufs[0].at[to], s1.at[k], r1.at[k], {"dp": p.mate()})
+        c.start()
+        self.first[k] = c
+
+    def forward(self, k):
         p, (s1, r1, s2, r2) = self.p, self.sems
         got, last = self.bufs
-        self.second = {}
-        for k in (1, 2, 3, 0):
-            to = p.at_z(k)
-            self.copy(to, k).wait_recv()
-            total = self.src[to, p.core].astype(F32) + got[to].astype(F32)
-            got[to] = total.astype(BF16)
-            if k:
-                c = remote(got.at[to], last.at[k - 1], s2.at[k], r2.at[k], {"dp": p.zindex(k)})
-                c.start()
-                self.second[k] = c
+        to = p.at_z(k)
+        self.first[k].wait_recv()
+        total = self.src[to, p.core].astype(F32) + got[to].astype(F32)
+        got[to] = total.astype(BF16)
+        if k:
+            c = remote(got.at[to], last.at[k - 1], s2.at[k], r2.at[k], {"dp": p.zindex(k)})
+            c.start()
+            self.second[k] = c
 
     def result(self):
         got, last = self.bufs
@@ -279,8 +291,8 @@
         return total
 
     def sent(self):
-        for k in range(4):
-            self.copy(self.p.at_z(k), k).wait_send()
+        for c in self.first.values():
+            c.wait_send()
 
     def finish(self):
         for c in self.second.values():
@@ -514,6 +526,8 @@
 
 
 def front(r, p):
+    peers = xy_peers(p) + dp_peers(p)
+    greet(peers)
     r.attn_src[...] = jnp.zeros_like(r.attn_src)
     r.stage[...] = jnp.zeros_like(r.stage)
     r.down[...] = jnp.zeros_like(r.down)
@@ -525,16 +539,18 @@
     r.small[...] = jnp.zeros_like(r.small)
     me = p.dp * 16 + p.ctx
     flat = lax.broadcasted_iota(jnp.int32, (7, 128), 0) * 128 + lax.broadcasted_iota(jnp.int32, (7, 128), 1)
-    for n in range(3):
+    for n, ref in enumerate((r.norm_attn, r.b_query, r.norm_mlp)):
+        vector = ref[...].astype(F32)[None]
         total = jnp.zeros((7, 128), F32)
         for i in range(7):
-            value = r.vectors[0:1, 7 * n + i : 7 * n + i + 1]
-            total = total + jnp.where(flat == me * 7 + i, value, 0.0)
+            total = total + jnp.where(flat == me * 7 + i, vector[:, i : i + 1], 0.0)
         r.small[7 * n : 7 * n + 7, :] = total
-    for n in range(2):
-        value = r.vectors[0:1, 21 + n : 22 + n]
-        r.small[21 + n : 22 + n, :] = jnp.where(flat[:1] == me, value, 0.0)
-    barrier(xy_peers(p) + dp_peers(p))
+    for n, ref in enumerate((r.b_key, r.value_bias)):
+        r.small[21 + n : 22 + n, :] = jnp.where(flat[:1] == me, ref[...].astype(F32)[None], 0.0)
+    r.places[...] = jnp.zeros_like(r.places)
+    for at in (0, 64):
+        r.places[:MB, at : at + 64] = r.positions[:, 0].astype(F32)
+    meet(peers)
     attn_copies = start_all(
         [remote(r.attn_src, r.attn_in.at[p.z], r.s_attn.at[k], r.r_attn.at[k], {"dp": p.zindex(k)}) for k in NEAR]
     )
@@ -561,7 +577,7 @@
         )
     start_all(gu_copies)
     r.gu_in[p.core, p.z] = r.gate_up[p.dp]
-    cots = GatherDp(p, r.cot, r.cot_all, r.cot_sems)
+    cots = GatherDp(p, r.cot, lambda b: r.cot_all.at[b], r.cot_sems)
     cots.start()
     arrive_all(attn_copies)
     for h in (0, 1):
@@ -570,7 +586,6 @@
         r.o_block[h] = pair[:, 1152:]
     ring_qkv = GatherCtx(p, r.qkv_block, lambda b, h: r.w_qkv.at[p.core, b, h], r.qkv_sems, r.qkv_mate)
     ring_qkv.start()
-    build_spread(r.spread)
     small.along_y()
     arrive_all(place_copies)
     place_copies2 = start_all(
@@ -580,11 +595,21 @@
     ring_qkv.forward()
     ring_o = GatherCtx(p, r.o_block, lambda b, h: r.w_o.at[p.core, b, h], r.o_sems, r.o_mate)
     ring_o.start()
+    build_spread(r.spread)
+    inner = lanes(1) & 63
+    freqs = jnp.exp((inner & 31).astype(F32) * (-math.log(THETA_BASE) / 32))
+    sign = jnp.where(inner < 32, -1.0, 1.0)
+    for mb in range(MB):
+        angles = jnp.transpose(jnp.broadcast_to(r.places[mb : mb + 1, :], (128, 128)))[:64] * freqs
+        r.cosine[64 * mb : 64 * mb + 64, :] = jnp.cos(angles)
+        r.sine[64 * mb : 64 * mb + 64, :] = jnp.sin(angles) * sign
     small.along_dp()
     arrive_all(gu_copies)
     for c in (0, 1):
         r.gu_block[c] = jnp.concatenate([r.gu_in[c, z] for z in range(4)], axis=0).astype(BF16)
-    cots.forward()
+    cots.relay()
+    for j in (0, 1, 3):
+        cots.forward(j)
     residual = r.hidden[...].astype(F32)
     unit_in = residual * rms_scale(residual)
     arrive_all(place_copies2)
@@ -600,27 +625,35 @@
     bias_query = row_vector(r.small_all, 7)
     ring_qkv.arrive()
     ring_o.forward()
+    ring_gu = GatherCtx(p, r.gu_block, lambda b, h: r.w_gu.at[h, b], r.gu_sems)
+    ring_gu.start()
+    down_copies = start_all(
+        [remote(r.down, r.down_in.at[p.x], r.s_down.at[0, k], r.r_down.at[0, k], p.xpeer(k)) for k in NEAR]
+    )
+    r.down_in[p.x] = r.down[...]
     cosine, sine = r.cosine[...], r.sine[...]
-    lin = dot(r.normed_in[...], r.w_qkv[...].reshape(DPAD, 1152))
-    keys = rotate(lin[:, 896:1024] + r.small_all[21:22, :], cosine, sine).astype(BF16)
-    values = (lin[:, 1024:] + r.small_all[22:23, :]).astype(BF16)
+    lin = dot(r.normed_in[...], r.w_qkv[:, :, :, :, 896:].reshape(DPAD, 256))
+    keys = rotate(lin[:, :128] + r.small_all[21:22, :], cosine, sine).astype(BF16)
+    values = (lin[:, 128:] + r.small_all[22:23, :]).astype(BF16)
     for mb in range(MB):
         r.kv[mb, :, :128] = keys[64 * mb : 64 * mb + 64]
         r.kv[mb, :, 128:] = values[64 * mb : 64 * mb + 64]
     ring_kv = GatherCtx(p, r.kv, lambda b, h: r.kv_all.at[h, b // 4, lax.rem(b, 4)], r.kv_sems)
     ring_kv.start()
+    lin = dot(r.normed_in[...], r.w_qkv[:, :, :, :, :896].reshape(DPAD, D))
     query_tiles = []
     for t in range(7):
         tile = lin[:, 128 * t : 128 * t + 128] + bias_query[:, 128 * t : 128 * t + 128]
         query_tiles.append((rotate(tile, cosine, sine).astype(BF16)).astype(F32) * (HEAD_SIZE**-0.5))
     scatter_heads(lambda mb, t: query_tiles[t][64 * mb : 64 * mb + 64], r.heads)
     ring_kv.forward()
-    ring_gu = GatherCtx(p, r.gu_block, lambda b, h: r.w_gu.at[h, b], r.gu_sems)
-    ring_gu.start()
-    down_copies = start_all(
-        [remote(r.down, r.down_in.at[p.x], r.s_down.at[0, k], r.r_down.at[0, k], p.xpeer(k)) for k in NEAR]
-    )
-    r.down_in[p.x] = r.down[...]
+    ring_gu.forward()
+    arrive_all(down_copies)
+    own_down = r.w_down.at[pl.ds(pl.multiple_of(160 * p.y, 32), 160)]
+    own_down[...] = jnp.concatenate([r.down_in[i] for i in range(4)], axis=0).astype(BF16)
+    down_copies2 = start_all(
+        [remote(own_down, own_down, r.s_down.at[1, k], r.r_down.at[1, k], p.ypeer(k)) for k in NEAR]
+    )
     ring_kv.arrive()
     for mb in range(MB):
         r.keys[mb] = r.kv_all[mb, :, :, :, :128].reshape(1024, 128)
@@ -639,38 +672,43 @@
 
         lax.fori_loop(0, 7, step, 0)
 
+    gain_mlp = row_vector(r.small_all, 14)
+    rings = []
+
+    def finish_rows(mb):
+        at = slice(64 * mb, 64 * mb + 64)
+        attended = jnp.concatenate([r.attended[mb * 7 + t] for t in range(7)], axis=1)
+        r.attended_wide[at, :] = spread(attended, r.spread[...])
+        mixed = residual[at] + dot(r.attended_wide[at, :], r.w_o[...].reshape(DPAD, D))
+        r.mixed[at, :] = mixed
+        unit_mid = mixed * rms_scale(mixed)
+        r.normed_mid[mb] = spread((unit_mid * gain_mlp).astype(BF16), r.spread[...])
+        ring = GatherDp(p, r.normed_mid.at[mb], lambda b: r.normed_all.at[b, mb], r.mid_sems[5 * mb : 5 * mb + 5])
+        ring.start()
+        ring.forward(0)
+        rings.append(ring)
+
     attend(0)
-    ring_gu.forward()
-    arrive_all(down_copies)
-    own_down = r.w_down.at[pl.ds(pl.multiple_of(160 * p.y, 32), 160)]
-    own_down[...] = jnp.concatenate([r.down_in[i] for i in range(4)], axis=0).astype(BF16)
-    down_copies2 = start_all(
-        [remote(own_down, own_down, r.s_down.at[1, k], r.r_down.at[1, k], p.ypeer(k)) for k in NEAR]
-    )
+    ring_o.arrive()
+    finish_rows(0)
+    cots.forward(2)
     attend(1)
-    attended = jnp.concatenate(
-        [jnp.concatenate([r.attended[mb * 7 + t] for t in range(7)], axis=1) for mb in range(MB)], axis=0
-    )
-    r.attended_wide[...] = spread(attended, r.spread[...])
-    ring_o.arrive()
-    mixed = residual + dot(r.attended_wide[...], r.w_o[...].reshape(DPAD, D))
-    r.mixed[...] = mixed
-    unit_mid = mixed * rms_scale(mixed)
-    r.normed_mid[...] = spread((unit_mid * row_vector(r.small_all, 14)).astype(BF16), r.spread[...])
-    ring_mid = GatherDp(p, r.normed_mid, r.normed_all, r.mid_sems)
-    ring_mid.start()
+    finish_rows(1)
+    rings[0].relay()
     ring_gu.arrive()
     arrive_all(down_copies2)
-    cots.arrive()
-    ring_mid.forward()
+    for j in range(4):
+        cots.arrive(j)
     for ring in (ring_qkv, ring_o, ring_kv, ring_gu, cots, small):
         ring.finish()
     sent_all(attn_copies + gu_copies + place_copies + place_copies2 + down_copies + down_copies2)
-    ring_mid.arrive()
-    ring_mid.finish()
+    return rings
 
 
 FRONT_SCRATCH = {
+    "places": VM((8, 128), F32),
+    "cosine": VM((128, 128), F32),
+    "sine": VM((128, 128), F32),
     "attn_src": VM((8, 2048), F32),
     "stage": VM((64, 640), F32),
     "gate_up": VM((8, 8, 1280), F32),
@@ -690,14 +728,14 @@
     "kv_all": VM((2, 4, 4, 64, 256), BF16),
     "values_t": VM((2, 128, 1024), BF16),
     "attended": VM((14, 64, 128), BF16),
-    "normed_mid": VM((128, DPAD), BF16),
+    "normed_mid": VM((2, 64, DPAD), BF16),
     "w_qkv": VM((2, 16, 2, 16, 1152), BF16),
     "w_o": VM((2, 16, 2, 16, D), BF16),
     "w_gu": VM((2, 16, 32, 1280), BF16),
     "w_down": VM((640, D), BF16),
     "small_all": VM((24, 128), F32),
     "cot_all": VM((8, 128, D), BF16),
-    "normed_all": VM((8, 128, DPAD), BF16),
+    "normed_all": VM((8, 2, 64, DPAD), BF16),
     "probs": VM((14, 1024, 128), BF16),
     "heads": VM((14, 128, 128), BF16),
     "keys": VM((2, 1024, 128), BF16),
@@ -711,19 +749,19 @@
     "s_attn": DMA((4,)), "r_attn": DMA((4,)), "s_gu": DMA((8,)), "r_gu": DMA((8,)),
     "s_place": DMA((2, 4)), "r_place": DMA((2, 4)), "s_down": DMA((2, 4)), "r_down": DMA((2, 4)),
     "qkv_sems": GatherCtx.SEMS, "qkv_mate": GatherCtx.MATE, "o_sems": GatherCtx.SEMS, "o_mate": GatherCtx.MATE,
-    "kv_sems": GatherCtx.SEMS, "gu_sems": GatherCtx.SEMS, "cot_sems": GatherDp.SEMS, "mid_sems": GatherDp.SEMS,
+    "kv_sems": GatherCtx.SEMS, "gu_sems": GatherCtx.SEMS, "cot_sems": GatherDp.SEMS, "mid_sems": GatherDp.SEMS * 2,
 }
 
 
-def back(r, p):
+def back(r, p, rings):
     red_normed = ReduceDp(p, r.part_normed, r.normed_bufs, r.normed_sems)
     red_out = ReduceDp(p, r.part_normed.at[:, :, :, pl.ds(0, D)], r.out_bufs, r.out_sems)
 
     def rows_of(ref, to):
         return ref[pl.ds(2 * to, 2)].reshape(256, ref.shape[-1])
 
-    def feed(i, carry):
-        to = lax.rem(p.z + 1 + i, 4)
+    def feed(k, carry):
+        to = lax.rem(p.z + k, 4)
         at = pl.ds(pl.multiple_of(256 * to, 256), 256)
         lin = dot(rows_of(r.normed_all, to), r.w_gu[...].reshape(DPAD, 1280))
         gate, up = lin[:, :640], lin[:, 640:]
@@ -739,23 +777,42 @@
             r.big[10 + t, at, :] = hidden[:, 128 * t : 128 * t + 128]
         part = dot_nt(jnp.concatenate([grad_gate, grad_up], axis=1), r.w_gu[...].reshape(DPAD, 1280))
         r.part_normed[to] = part.astype(BF16).reshape(2, 128, DPAD)
-        red_normed.send(i)
         return carry
 
-    lax.fori_loop(0, 4, feed, 0)
-    red_normed.forward()
-
-    def project(i, carry):
-        to = lax.rem(p.z + 1 + i, 4)
+    def feed_block(j):
+        k = (4 - j) % 4
+        for ring in rings:
+            ring.arrive(j)
+        lax.fori_loop(k, k + 1, feed, 0)
+        red_normed.send(k)
+
+    def pass_on(j):
+        for ring in rings:
+            ring.forward(j)
+
+    feed_block(0)
+    rings[1].relay()
+    pass_on(1)
+    pass_on(3)
+    feed_block(1)
+    feed_block(3)
+    pass_on(2)
+    red_normed.forward(3)
+    red_normed.forward(1)
+    feed_block(2)
+    red_normed.forward(2)
+    red_normed.forward(0)
+
+    def project(k, carry):
+        to = lax.rem(p.z + k, 4)
         at = pl.ds(pl.multiple_of(256 * to, 256), 256)
         hidden = jnp.concatenate([r.big[10 + t, at, :] for t in range(5)], axis=1)
         r.part_normed[to, :, :, :D] = dot(hidden, r.w_down[...]).astype(BF16).reshape(2, 128, D)
-        red_out.send(i)
         return carry
 
     def grad_gate_up(i, carry):
         at = pl.ds(pl.multiple_of(256 * i, 256), 256)
-        left = r.normed_all[:, :, at].reshape(1024, 256)
+        left = r.normed_all[:, :, :, at].reshape(1024, 256)
         right = jnp.concatenate([r.big[t] for t in range(10)], axis=1)
         part = dot_tn(left, right).astype(BF16).reshape(2, 4, 32, 1280)
         r.g_gu[i // 2, pl.ds(2 * lax.rem(i, 2), 2)] = part
@@ -781,7 +838,9 @@
         ]
     )
     red_normed.sent()
-    lax.fori_loop(0, 4, project, 0)
+    for k in NEAR + (0,):
+        lax.fori_loop(k, k + 1, project, 0)
+        red_out.send(k)
     gain_mlp = row_vector(r.small_all, 14)
     mixed = r.mixed[...]
     inv_mid = rms_scale(mixed)
@@ -799,7 +858,8 @@
     scatter_heads(lambda mb, t: r.held[64 * mb : 64 * mb + 64, 128 * t : 128 * t + 128], r.grad_heads)
     for mb in range(MB):
         r.values_t[mb] = jnp.transpose(r.keys[mb].astype(F32)).astype(BF16)
-    red_out.forward()
+    for k in NEAR + (0,):
+        red_out.forward(k)
 
     def attend_back(mb):
         def step(t, carry):
@@ -826,12 +886,12 @@
         r.kv_all[mb, y, :, :, 128:] = grad_values.astype(BF16).reshape(4, 64, 128)
         return carry
 
-    attend_back(0)
-    attend_back(1)
-    lax.fori_loop(0, 8, grad_key_value, 0)
-
     ring_kv = ReduceCtx(p, lambda h, y, x: r.kv_all.at[h, y, x], r.kv_bufs, r.kv_red_sems)
-    ring_kv.start()
+    for mb in range(MB):
+        attend_back(mb)
+        lax.fori_loop(4 * mb, 4 * mb + 4, grad_key_value, 0)
+        ring_kv.start((mb,))
+    ring_gu.forward()
 
     def weight_gradient(left, right, out):
         def step(i, carry):
@@ -854,14 +914,15 @@
 
     weight_gradient(r.attended_wide, r.low_b, r.g_wo)
     mate_wo = to_mate(0, r.g_wo, r.m_wo)
+    ring_kv.forward()
+    build_columns(r.big)
+    r.layer_out[...] = (mixed + red_out.result()).astype(BF16)
     cosine, sine = r.cosine[...], r.sine[...]
     for t in range(7):
         tile = jnp.concatenate([r.grad_query[t], r.grad_query[7 + t]], axis=0) * (HEAD_SIZE**-0.5)
         r.low_a[:, 128 * t : 128 * t + 128] = rotate_back(tile, cosine, sine).astype(BF16)
     weight_gradient(r.normed_in, r.low_a, r.g_wq)
     mate_wq = to_mate(1, r.g_wq, r.m_wq)
-    ring_gu.forward()
-    ring_kv.forward()
     with_mate(mate_wo, r.g_wo, r.m_wo)
     ring_wo = ReduceCtx(p, lambda h, y, x: r.m_wo.at[y, x, h], r.wo_bufs, r.wo_sems)
     ring_wo.start()
@@ -875,6 +936,10 @@
     r.low_kv[:, 128:] = kv_sum[:, 128:].astype(BF16)
     weight_gradient(r.normed_in, r.low_kv, r.g_wkv)
     mate_wkv = to_mate(2, r.g_wkv, r.m_wkv)
+    ring_wo.forward()
+    with_mate(mate_wkv, r.g_wkv, r.m_wkv)
+    ring_wkv = ReduceCtx(p, lambda h, y, x: r.m_wkv.at[y, x, h], r.wkv_bufs, r.wkv_sems)
+    ring_wkv.start()
     bias_kv = jnp.sum(r.low_kv[...].astype(F32), axis=0, keepdims=True)
     store_rows(r.small_grads, 21, bias_kv)
     r.small_grads[23:24, :] = jnp.zeros((1, 128), F32)
@@ -886,21 +951,8 @@
     store_rows(r.small_grads, 0, jnp.sum(r.held[...] * unit_in, axis=0, keepdims=True))
     small = SmallSum(p, r.small_grads, r.small_bufs2, r.small_sems2)
     small.start()
-    with_mate(mate_wkv, r.g_wkv, r.m_wkv)
-    ring_wkv = ReduceCtx(p, lambda h, y, x: r.m_wkv.at[y, x, h], r.wkv_bufs, r.wkv_sems)
-    ring_wkv.start()
-    arrive_all(down_copies)
-    total = r.g_down[pl.ds(pl.multiple_of(160 * p.y, 32), 160), :].astype(F32)
-    for k in NEAR:
-        total = total + r.down_y[k - 1].astype(F32)
-    for i in range(4):
-        r.down_mid[i] = total[40 * i : 40 * i + 40]
-    down_copies2 = start_all(
-        [
-            remote(r.down_mid.at[p.at_x(k)], r.down_x.at[k - 1], r.s_gdown.at[1, k], r.r_gdown.at[1, k], p.xpeer(k))
-            for k in NEAR
-        ]
-    )
+    ring_wkv.forward()
+    ring_wq.forward()
     for h in (0, 1):
         part = ring_gu.result(h)
         for z in range(4):
@@ -915,15 +967,23 @@
         )
     start_all(gu_copies)
     r.gu_got[p.dp] = r.gu_out[p.z, p.core]
-    ring_wo.forward()
-    ring_wq.forward()
     small.along_y()
-    ring_wkv.forward()
+    arrive_all(down_copies)
+    total = r.g_down[pl.ds(pl.multiple_of(160 * p.y, 32), 160), :].astype(F32)
+    for k in NEAR:
+        total = total + r.down_y[k - 1].astype(F32)
+    for i in range(4):
+        r.down_mid[i] = total[40 * i : 40 * i + 40]
+    down_copies2 = start_all(
+        [
+            remote(r.down_mid.at[p.at_x(k)], r.down_x.at[k - 1], r.s_gdown.at[1, k], r.r_gdown.at[1, k], p.xpeer(k))
+            for k in NEAR
+        ]
+    )
     scaled = r.held[...] * row_vector(r.small_all, 0)
     r.grad_in[...] = r.grad_mixed[...] + inv_rms * (
         scaled - unit_in * jnp.mean(scaled * unit_in, axis=-1, keepdims=True)
     )
-    r.layer_out[...] = (mixed + red_out.result()).astype(BF16)
     small.along_dp()
     sum_wo = ZSum(p, ring_wo, r.zo_bufs, r.zo_sems)
     sum_wo.start()
@@ -931,7 +991,6 @@
     sum_wq.start()
     sum_wkv = ZSum(p, ring_wkv, r.zkv_bufs, r.zkv_sems)
     sum_wkv.start()
-    build_columns(r.big)
     arrive_all(gu_copies)
     for n, out in enumerate((r.o_gate, r.o_up)):
         for d in range(8):
@@ -967,7 +1026,7 @@
         r.o_mine[n : n + 1, :] = row
     r.o_mine[3:4, :] = jnp.broadcast_to(pick(total[22:23], lane == me), (1, 128))
     red_out.sent()
-    for ring in (red_normed, red_out, ring_gu, ring_kv, ring_wo, ring_wq, ring_wkv, small, sum_wo, sum_wq, sum_wkv):
+    for ring in (*rings, red_normed, red_out, ring_gu, ring_kv, ring_wo, ring_wq, ring_wkv, small, sum_wo, sum_wq, sum_wkv):
         ring.finish()
     sent_all([mate_wo, mate_wq, mate_wkv] + down_copies + down_copies2 + gu_copies)
 
@@ -1019,10 +1078,37 @@
 }
 
 
+WHOLE = ("layer_out", "grad_in", "o_query", "o_key", "o_value", "o_output", "o_gate", "o_up", "o_down")
+VECTORS = {"norm_attn": 7, "b_query": 7, "norm_mlp": 7, "b_value": 1, "b_key": 128}
+
+
+def finish(done):
+    def kernel(*refs):
+        count = len(WHOLE)
+        sources, (mine, sums) = refs[:count], refs[count : count + 2]
+        targets, vectors = refs[count + 2 : 2 * count + 2], refs[2 * count + 2 :]
+        for source, target in zip(sources, targets):
+            target[...] = source[...]
+        for n in range(3):
+            vectors[n][...] = mine[n, :7]
+        vectors[3][...] = mine[3, :1]
+        vectors[4][...] = sums[21]
+
+    fast = pl.BlockSpec(memory_space=VM)
+    results = pl.pallas_call(
+        kernel,
+        out_shape=tuple(LAYER_OUTS[key] for key in WHOLE) + tuple(shape((n,), F32) for n in VECTORS.values()),
+        in_specs=[fast] * (len(WHOLE) + 2),
+        out_specs=tuple([fast] * (len(WHOLE) + len(VECTORS))),
+        name="finish",
+        compiler_params=pltpu.CompilerParams(vmem_limit_bytes=63 << 20),
+    )(*(done[key] for key in WHOLE), done["o_mine"], done["o_small"])
+    return dict(zip(WHOLE + tuple(VECTORS), results))
+
+
 def layer(r):
     p = Place()
-    front(r, p)
-    back(r, p)
+    back(r, p, front(r, p))
 
 
 def body(
@@ -1030,35 +1116,28 @@
     norm_mlp, w_gate, w_up, w_down, cotangent,
 ):
     rows = MB * 64
-    places = positions[:, 0]
-    freqs = THETA_BASE ** (-jnp.arange(0, HEAD_SIZE, 2).astype(F32) / HEAD_SIZE)
-    angles = places.reshape(rows).astype(F32)[:, None] * jnp.tile(freqs, 4)[None, :]
-    sign = jnp.tile(jnp.repeat(jnp.array([-1.0, 1.0], F32), HEAD_SIZE // 2), 2)
-    vectors = jnp.concatenate([norm_attn, b_query, norm_mlp, b_key, value_bias]).astype(F32)
     inputs = {
         "hidden": hidden_in.reshape(rows, D),
         "cot": cotangent.reshape(rows, D),
-        "cosine": jnp.cos(angles),
-        "sine": jnp.sin(angles) * sign,
+        "positions": positions,
+        "norm_attn": norm_attn, "b_query": b_query, "norm_mlp": norm_mlp, "b_key": b_key, "value_bias": value_bias,
         "w_query": w_query, "w_key": w_key, "w_value": value_weight, "w_output": w_output,
         "w_gate": w_gate, "w_up": w_up, "w_down_own": w_down,
-        "vectors": jnp.pad(vectors, (0, 105))[None],
-        "places": jnp.pad(jnp.tile(places.astype(F32), (1, 2)), ((0, 6), (0, 0))),
     }
     done = call(layer, inputs, LAYER_OUTS, {**FRONT_SCRATCH, **BACK_SCRATCH}, 0, "layer")
-    mine = done["o_mine"]
+    done = finish(done)
     return (
         done["layer_out"].reshape(MB, 1, 64, D),
         done["grad_in"].reshape(MB, 1, 64, D),
-        mine[0, :7],
+        done["norm_attn"],
         done["o_query"],
-        mine[1, :7],
+        done["b_query"],
         done["o_key"],
-        done["o_small"][21],
+        done["b_key"],
         done["o_value"],
-        mine[3, :1],
+        done["b_value"],
         done["o_output"],
-        mine[2, :7],
+        done["norm_mlp"],
         done["o_gate"],
         done["o_up"],
         done["o_down"],

time: 188 us -> 172 us (0.915)
  local copies, waits for them, and re-layouts: 13.6 us -> 0 us
    unnamed x35 -> x0, local copies, waits for them, and re-layouts: 8.76 us -> none
    pallas_call x1, Pallas kernels: 170 us -> 167 us  [call(): pl.pallas_call(kernel, out_shape=tuple(outs.values()), in_specs=[pl.Block...]
    squeeze x2 -> x0, local copies, waits for them, and re-layouts: 2.5 us -> none  [the longest x1 1.31 us: body(): mine[2, :7]]
    pallas_call x0 -> x1, Pallas kernels: none -> 2.38 us  [finish(): pl.pallas_call(kernel, out_shape=tuple((LAYER_OUTS[key] for key in WHOLE)...]
where the time goes in v4:
time: 172 us
  Pallas kernels  170 us (99%)
  between operations  2.16 us (1%)
    pallas_call x1, Pallas kernels, call(): pl.pallas_call(kernel, out_shape=tuple(outs.values()), in_specs=[pl.Block...  167 us

profile of v4, /device:TPU:1, one launch (start us, length us, event | category | flops | bytes accessed | tf_op | source)
XLA Modules:
  0.0 172.0 jit_solution(1756406659850559660)
XLA Ops:
  2.0 167.4 %layer.1 = (bf16[128,896]{1,0:T(8,128)(2,1)}, f32[128,896]{1,0:T(8,128)}, f32[7,896]{1,0:T(8,128)}, f32[7,128]{1,0:T(8,128)}, f32[7,128]{1,0:T(8,128)}, /*index=...) custom-call(bf16[128,896]{1,0:T(8,128)(2,1)} %bitcast.8, ...), custom_call_target="tpu_custom_call" | custom-call | tf_op jit(solution)/shard_map/layer/pallas_call | solution.py:328
  169.4 2.4 %finish.1 = (bf16[128,896]{1,0:T(8,128)(2,1)}, f32[128,896]{1,0:T(8,128)}, f32[7,896]{1,0:T(8,128)}, f32[7,128]{1,0:T(8,128)}, f32[7,128]{1,0:T(8,128)}, /*index...) custom-call(bf16[128,896]{1,0:T(8,128)(2,1)} %get-tuple-element.39.r, ...), custom_call_target="tpu_custom_call" | custom-call | tf_op jit(solution)/shard_map/finish/pallas_call | solution.py:1098

commit v5 on v4

--- a/solution.py
+++ b/solution.py
@@ -607,6 +607,12 @@
     arrive_all(gu_copies)
     for c in (0, 1):
         r.gu_block[c] = jnp.concatenate([r.gu_in[c, z] for z in range(4)], axis=0).astype(BF16)
+    ring_gu = GatherCtx(p, r.gu_block, lambda b, h: r.w_gu.at[h, b], r.gu_sems)
+    ring_gu.start()
+    down_copies = start_all(
+        [remote(r.down, r.down_in.at[p.x], r.s_down.at[0, k], r.r_down.at[0, k], p.xpeer(k)) for k in NEAR]
+    )
+    r.down_in[p.x] = r.down[...]
     cots.relay()
     for j in (0, 1, 3):
         cots.forward(j)
@@ -625,12 +631,6 @@
     bias_query = row_vector(r.small_all, 7)
     ring_qkv.arrive()
     ring_o.forward()
-    ring_gu = GatherCtx(p, r.gu_block, lambda b, h: r.w_gu.at[h, b], r.gu_sems)
-    ring_gu.start()
-    down_copies = start_all(
-        [remote(r.down, r.down_in.at[p.x], r.s_down.at[0, k], r.r_down.at[0, k], p.xpeer(k)) for k in NEAR]
-    )
-    r.down_in[p.x] = r.down[...]
     cosine, sine = r.cosine[...], r.sine[...]
     lin = dot(r.normed_in[...], r.w_qkv[:, :, :, :, 896:].reshape(DPAD, 256))
     keys = rotate(lin[:, :128] + r.small_all[21:22, :], cosine, sine).astype(BF16)

time: 172 us -> 166 us (0.965)
  Pallas kernels: 170 us -> 164 us
    pallas_call x1, Pallas kernels: 167 us -> 162 us  [call(): pl.pallas_call(kernel, out_shape=tuple(outs.values()), in_specs=[pl.Block...]
where the time goes in v5:
time: 166 us
  Pallas kernels  164 us (99%)
  between operations  2.16 us (1%)
    pallas_call x1, Pallas kernels, call(): pl.pallas_call(kernel, out_shape=tuple(outs.values()), in_specs=[pl.Block...  162 us

profile of v5, /device:TPU:1, one launch (start us, length us, event | category | flops | bytes accessed | tf_op | source)
XLA Modules:
  0.0 166.3 jit_solution(10781200517640882468)
XLA Ops:
  2.0 161.7 %layer.1 = (bf16[128,896]{1,0:T(8,128)(2,1)}, f32[128,896]{1,0:T(8,128)}, f32[7,896]{1,0:T(8,128)}, f32[7,128]{1,0:T(8,128)}, f32[7,128]{1,0:T(8,128)}, /*index=...) custom-call(bf16[128,896]{1,0:T(8,128)(2,1)} %bitcast.8, ...), custom_call_target="tpu_custom_call" | custom-call | tf_op jit(solution)/shard_map/layer/pallas_call | solution.py:328
  163.7 2.4 %finish.1 = (bf16[128,896]{1,0:T(8,128)(2,1)}, f32[128,896]{1,0:T(8,128)}, f32[7,896]{1,0:T(8,128)}, f32[7,128]{1,0:T(8,128)}, f32[7,128]{1,0:T(8,128)}, /*index...) custom-call(bf16[128,896]{1,0:T(8,128)(2,1)} %get-tuple-element.39.r, ...), custom_call_target="tpu_custom_call" | custom-call | tf_op jit(solution)/shard_map/finish/pallas_call | solution.py:1098

commit v6 on v5

--- a/solution.py
+++ b/solution.py
@@ -818,9 +818,10 @@
         r.g_gu[i // 2, pl.ds(2 * lax.rem(i, 2), 2)] = part
         return carry
 
-    lax.fori_loop(0, 4, grad_gate_up, 0)
     ring_gu = ReduceCtx(p, lambda h, y, x: r.g_gu.at[h, y, x], r.gu_bufs, r.gu_red_sems)
-    ring_gu.start()
+    for half in (0, 1):
+        lax.fori_loop(2 * half, 2 * half + 2, grad_gate_up, 0)
+        ring_gu.start((half,))
 
     def grad_down(t, carry):
         at = pl.ds(pl.multiple_of(128 * t, 128), 128)

time: 166 us -> 165 us (level)
  Pallas kernels: 164 us -> 162 us
    pallas_call x1, Pallas kernels: 162 us -> 160 us  [call(): pl.pallas_call(kernel, out_shape=tuple(outs.values()), in_specs=[pl.Block...]
where the time goes in v6:
time: 165 us; the launch traced here: 164 us
  Pallas kernels  162 us (98%)
  between operations  2.16 us (1%)
    pallas_call x1, Pallas kernels, call(): pl.pallas_call(kernel, out_shape=tuple(outs.values()), in_specs=[pl.Block...  160 us

profile of v6, /device:TPU:1, one launch (start us, length us, event | category | flops | bytes accessed | tf_op | source)
XLA Modules:
  0.0 164.5 jit_solution(9085008623276879620)
XLA Ops:
  2.0 159.9 %layer.1 = (bf16[128,896]{1,0:T(8,128)(2,1)}, f32[128,896]{1,0:T(8,128)}, f32[7,896]{1,0:T(8,128)}, f32[7,128]{1,0:T(8,128)}, f32[7,128]{1,0:T(8,128)}, /*index=...) custom-call(bf16[128,896]{1,0:T(8,128)(2,1)} %bitcast.8, ...), custom_call_target="tpu_custom_call" | custom-call | tf_op jit(solution)/shard_map/layer/pallas_call | solution.py:328
  161.9 2.4 %finish.1 = (bf16[128,896]{1,0:T(8,128)(2,1)}, f32[128,896]{1,0:T(8,128)}, f32[7,896]{1,0:T(8,128)}, f32[7,128]{1,0:T(8,128)}, f32[7,128]{1,0:T(8,128)}, /*index...) custom-call(bf16[128,896]{1,0:T(8,128)(2,1)} %get-tuple-element.39.r, ...), custom_call_target="tpu_custom_call" | custom-call | tf_op jit(solution)/shard_map/finish/pallas_call | solution.py:1099
